TPU v7x, 32 devices: a whole 2x2x4 slice. The times are simulated.
32 devices in a mesh: seq: 16 (over z, x, core), head: 2 (over y).
Axes of the slice: x: 2, y: 2, z: 4, core: 2. Of those that a mesh axis runs over, the one named last changes fastest.
Arguments:
- queries: bfloat16 [16, 4096, 128], P('head', 'seq'), may hold values from -1.75 to 1.75
- key_rows: bfloat16 [16, 4096, 128], P('head', 'seq'), may hold values from -1.75 to 1.75
- value_rows: bfloat16 [16, 4096, 128], P('head', 'seq'), may hold values from -1.75 to 1.75
- grad_out: bfloat16 [16, 4096, 128], P('head', 'seq'), may hold values from -1.75 to 1.75
Outputs:
- grad_query: bfloat16 [16, 4096, 128], P('head', 'seq')
- grad_key: bfloat16 [16, 4096, 128], P('head', 'seq')
- grad_value: bfloat16 [16, 4096, 128], P('head', 'seq')
All inputs are finite; a program needn't handle non-finite values.
Results may differ from a plain program's by a relative error of at most 0.0049.
Values sent between devices are 32-bit elements; how exact they have to be, the bound alone decides.
No kernel may reach another device: no remote copies, remote signals or barrier semaphores. Data moves between devices by JAX's collectives and lax.ppermute only.
A program may use at most 192 MiB of HBM per device.

v0:
```python
import jax
import jax.numpy as jnp
from jax import lax
from jax.sharding import PartitionSpec as P

TILE = 256


def entering(x, axis, combine, identity, reverse):
    count, place = (lax.axis_size(axis), lax.axis_index(axis))
    everything = lax.all_gather(x, axis)
    start = jnp.broadcast_to(jnp.asarray(identity, x.dtype), x.shape)

    def turn(k, before):
        at = count - 1 - k if reverse else k
        reached = at > place if reverse else at < place
        new = combine(before, everything[at])
        return jnp.where(reached, new, before)

    return lax.fori_loop(0, count, turn, start)


def add_states(earlier, latter):
    return earlier + latter


def body(queries, key_rows, value_rows, grad_out):
    head_count, tokens, head_width = queries.shape
    tile_count = tokens // TILE
    tile_shape = (head_count, tile_count, TILE, head_width)
    query_tiles = queries.reshape(tile_shape)
    key_tiles = key_rows.reshape(tile_shape)
    value_tiles = value_rows.reshape(tile_shape)
    grad_tiles = grad_out.reshape(tile_shape)
    key_state = jnp.einsum(
        "hjsa,hjsb->hjab", key_tiles, value_tiles, preferred_element_type=jnp.float32
    )
    query_state = jnp.einsum(
        "hjta,hjtb->hjab", query_tiles, grad_tiles, preferred_element_type=jnp.float32
    )
    local_keys = jnp.sum(key_state, 1)
    local_queries = jnp.sum(query_state, 1)
    blank_state = jnp.zeros_like(local_keys)
    incoming = entering(local_keys, "seq", add_states, blank_state, False)
    outgoing = entering(local_queries, "seq", add_states, blank_state, True)
    zero_state = jnp.zeros((head_count, 1, head_width, head_width), jnp.float32)
    earlier_states = incoming[:, None] + jnp.concatenate(
        [zero_state, jnp.cumsum(key_state, 1)[:, :-1]], 1
    )
    later_states = outgoing[:, None] + jnp.concatenate(
        [jnp.cumsum(query_state[:, ::-1], 1)[:, ::-1][:, 1:], zero_state], 1
    )
    earlier_states = earlier_states.astype(jnp.bfloat16)
    later_states = later_states.astype(jnp.bfloat16)
    causal = (jnp.arange(TILE)[:, None] >= jnp.arange(TILE)[None, :])[None, None]
    out_scores = jnp.einsum(
        "hjta,hjsa->hjts", grad_tiles, value_tiles, preferred_element_type=jnp.float32
    )
    out_scores = jnp.where(causal, out_scores, 0.0).astype(jnp.bfloat16)
    attn_scores = jnp.einsum(
        "hjta,hjsa->hjts", query_tiles, key_tiles, preferred_element_type=jnp.float32
    )
    attn_scores = jnp.where(causal, attn_scores, 0.0).astype(jnp.bfloat16)
    grad_query = jnp.einsum(
        "hjts,hjsa->hjta", out_scores, key_tiles, preferred_element_type=jnp.float32
    )
    grad_query = grad_query + jnp.einsum(
        "hjtb,hjab->hjta", grad_tiles, earlier_states, preferred_element_type=jnp.float32
    )
    grad_key = jnp.einsum(
        "hjts,hjta->hjsa", out_scores, query_tiles, preferred_element_type=jnp.float32
    )
    grad_key = grad_key + jnp.einsum(
        "hjsb,hjab->hjsa", value_tiles, later_states, preferred_element_type=jnp.float32
    )
    grad_value = jnp.einsum(
        "hjts,hjtb->hjsb", attn_scores, grad_tiles, preferred_element_type=jnp.float32
    )
    grad_value = grad_value + jnp.einsum(
        "hjsa,hjab->hjsb", key_tiles, later_states, preferred_element_type=jnp.float32
    )
    flat_shape = (head_count, tokens, head_width)
    return (
        grad_query.astype(jnp.bfloat16).reshape(flat_shape),
        grad_key.astype(jnp.bfloat16).reshape(flat_shape),
        grad_value.astype(jnp.bfloat16).reshape(flat_shape),
    )


def solution(mesh):
    placed = (
        P("head", "seq", None),
        P("head", "seq", None),
        P("head", "seq", None),
        P("head", "seq", None),
    )
    return jax.shard_map(
        body,
        mesh=mesh,
        in_specs=placed,
        out_specs=(P("head", "seq", None), P("head", "seq", None), P("head", "seq", None)),
        check_vma=False,
    )
```

profile of v0, /device:TPU:1, one launch (start us, length us, event | category | flops | bytes accessed | tf_op | source)
XLA Modules:
  0.0 194.8 jit_solution(15987373123797507754)
XLA Ops:
  7.2 1.0 copy-done
  8.2 2.2 %fusion.16 = f32[8,128,128]{2,1,0:T(8,128)} fusion(bf16[8,256,128]{2,1,0:T(8,128)(2,1)} %param.8, bf16[8,256,128]{2,1,0:T(8,128)(2,1)S(1)} %copy-done), kind=kOutput, calls=%fused_computation.24 | convolution fusion | flops 67108864 | bytes 1572864 | tf_op jit(solution)/shard_map/hjta,hjtb->hjab/dot_general | solution.py:38
  10.4 0.0 all-gather.5.cloned.1.call-start
  10.5 1.1 fusion.14
  11.7 0.4 select_convert_fusion.1
  12.2 1.5 fusion.15
  13.7 0.4 fusion.13
  14.1 74.1 %all-gather.7.cloned.1.call-done = f32[128,128,128]{2,1,0:T(8,128)} async-done(((f32[8,128,128]{2,1,0:T(8,128)}), f32[128,128,128]{2,1,0:T(8,128)}) %all-gather.7.cloned.1.call-update) | async-done | bytes 8388624 | tf_op jit(solution)/shard_map/all_gather | solution.py:11
  88.2 20.1 %while.31 = (s32[]{:T(128)}, f32[8,128,128]{2,1,0:T(8,128)S(1)}, s32[]{:T(128)}, f32[16,8,128,128]{3,2,1,0:T(8,128)}, s32[]{:T(128)}, /*index=5*/s32[]{:T(128)}, s32[]{:T(128)}, s32[]{:T(128)}) while((s32[]{:T(128)}, f32[8,128,128]{2,1,0:T(8,128)S(1)}, s32[]{:T(128)}, f32[16,8,128,128]{3,2,1,0:T(8,128)}, s32[]{:T(128)}, ...), condition=%wide.region_3.4_spmd.clone, body=%wide.region_2.3_spmd.clone.sunk | while | flops 393224 | bytes 1573019 | solution.py:20
  88.2 1.2 add_select_fusion.5
  89.5 1.2 add_select_fusion.5
  90.7 1.2 add_select_fusion.5
  92.0 1.2 add_select_fusion.5
  93.2 1.2 add_select_fusion.5
  94.5 1.2 add_select_fusion.5
  95.7 1.3 add_select_fusion.5
  97.0 1.2 add_select_fusion.5
  98.3 1.2 add_select_fusion.5
  99.6 1.2 add_select_fusion.5
  100.8 1.2 add_select_fusion.5
  102.1 1.2 add_select_fusion.5
  103.3 1.2 add_select_fusion.5
  104.6 1.2 add_select_fusion.5
  105.9 1.2 add_select_fusion.5
  107.1 1.2 add_select_fusion.5
  108.4 1.4 convolution_bitcast_fusion
  109.7 0.3 copy-done.4
  110.1 1.1 fusion.6
  111.2 52.9 %all-gather.5.cloned.1.call-done = f32[128,128,128]{2,1,0:T(8,128)} async-done(((f32[8,128,128]{2,1,0:T(8,128)}), f32[128,128,128]{2,1,0:T(8,128)}) %all-gather.5.cloned.1.call-update) | async-done | bytes 8388624 | tf_op jit(solution)/shard_map/all_gather | solution.py:11
  164.1 20.1 %while.30 = (s32[]{:T(128)}, f32[8,128,128]{2,1,0:T(8,128)S(1)}, s32[]{:T(128)}, f32[16,8,128,128]{3,2,1,0:T(8,128)}, s32[]{:T(128)}, /*index=5*/s32[]{:T(128)}) while((s32[]{:T(128)}, f32[8,128,128]{2,1,0:T(8,128)S(1)}, s32[]{:T(128)}, f32[16,8,128,128]{3,2,1,0:T(8,128)}, s32[]{:T(128)}, /*index=5*/s32[]{:T(128)}) %tuple.81), condition=%wide.region_1.0_spmd.clone, body=%wide.region_0.0_spmd.clone.sunk | while | flops 393220 | bytes 1572957 | solution.py:20
  164.1 1.3 add_select_fusion.4
  165.4 1.2 add_select_fusion.4
  166.7 1.2 add_select_fusion.4
  167.9 1.2 add_select_fusion.4
  169.2 1.2 add_select_fusion.4
  170.4 1.2 add_select_fusion.4
  171.7 1.2 add_select_fusion.4
  172.9 1.2 add_select_fusion.4
  174.2 1.2 add_select_fusion.4
  175.4 1.2 add_select_fusion.4
  176.7 1.2 add_select_fusion.4
  177.9 1.2 add_select_fusion.4
  179.2 1.2 add_select_fusion.4
  180.4 1.2 add_select_fusion.4
  181.7 1.2 add_select_fusion.4
  182.9 1.2 add_select_fusion.4
  184.2 2.7 %fusion.4 = bf16[8,256,128]{2,1,0:T(8,128)(2,1)} fusion(f32[8,256,128]{2,1,0:T(8,128)} %convolution_bitcast_fusion, bf16[8,256,128]{2,1,0:T(8,128)(2,1)S(1)} %copy-done, bf16[8,256,128]{2,1,0:T(8,128)(2,1)S(1)} %copy-done.6, bf16[8,256,128]{2,1,0:T(8,128)(2,1)S(1)} %copy-done.1, pred[256,256]{1,0:T(8,128)(4,1)S(1)} %iota_compare_fusion), kind=kOutput, calls=%fused_computation.11 | convolution fusion | flops 270008320 | bytes 3211264 | tf_op jit(solution)/shard_map/hjts,hjtb->hjsb/dot_general | solution.py:76
  186.9 1.1 fusion.5
  (18 shorter events, 0.1 us)
Async XLA Ops:
  7.2 1.0 copy-start
  7.2 3.3 %copy-start.3 = (bf16[8,256,128]{2,1,0:T(8,128)(2,1)S(1)}, bf16[8,256,128]{2,1,0:T(8,128)(2,1)}, u32[]{:S(2)}) copy-start(bf16[8,256,128]{2,1,0:T(8,128)(2,1)} %param.10) | copy-start | bytes 1572868
  7.2 3.3 %copy-start.1 = (bf16[8,256,128]{2,1,0:T(8,128)(2,1)S(1)}, bf16[8,256,128]{2,1,0:T(8,128)(2,1)}, u32[]{:S(2)}) copy-start(bf16[8,256,128]{2,1,0:T(8,128)(2,1)} %param.9) | copy-start | bytes 1572868
  7.2 81.0 %all-gather.7.cloned.1.call-start = ((), (), s32[]{:S(2)}) async-start(), calls=%async_computation.1 | async-start | bytes 8912896 | tf_op jit(solution)/shard_map/all_gather | solution.py:11
  10.4 1.8 copy-start.5
  10.4 153.7 %all-gather.5.cloned.1.call-start = ((), (), s32[]{:S(2)}) async-start(), calls=%async_computation | async-start | bytes 8912896 | tf_op jit(solution)/shard_map/all_gather | solution.py:11
  108.4 1.4 copy-start.2
  108.4 1.7 copy-start.4
  164.1 20.1 %copy-start.6 = (bf16[8,256,128]{2,1,0:T(8,128)(2,1)S(1)}, bf16[8,256,128]{2,1,0:T(8,128)(2,1)}, u32[]{:S(2)}) copy-start(bf16[8,256,128]{2,1,0:T(8,128)(2,1)} %param.8) | copy-start | bytes 1572868
Sparse Core Ops, SparseCore 0:
  10.8 77.3 all-gather.6
  90.9 73.1 all-gather.4
where the time goes:
time: 197 us; the launch traced here: 195 us
  waiting for transfers between devices  127 us (64%)
  other arithmetic  39.4 us (20%)
  between operations  14.2 us (7%)
  matrix products  11.9 us (6%)
    all_gather x2, waiting for transfers between devices, entering(): everything = lax.all_gather(x, axis)  127 us
    select_n x32, other arithmetic, turn(): return jnp.where(reached, new, before)  39.4 us
  transfers between devices with their start and end apart: 2, of which 2 were waited for; matrix products, arithmetic and copies ran while one was open for 13% of the time, Pallas kernels for 0%

commit v1 on v0

v1 whole, which is shorter than its diff:
```python
import jax
import jax.numpy as jnp
from jax import lax
from jax.experimental import pallas as pl
from jax.experimental.pallas import tpu as pltpu
from jax.sharding import PartitionSpec as P

TILE = 256
SPEC = P("head", "seq", None)
F32 = jnp.float32
BF16 = jnp.bfloat16


def entering(x, axis, combine, identity, reverse):
    count, place = (lax.axis_size(axis), lax.axis_index(axis))
    everything = lax.all_gather(x, axis)
    start = jnp.broadcast_to(jnp.asarray(identity, x.dtype), x.shape)

    def turn(k, before):
        at = count - 1 - k if reverse else k
        reached = at > place if reverse else at < place
        new = combine(before, everything[at])
        return jnp.where(reached, new, before)

    return lax.fori_loop(0, count, turn, start)


def add_states(earlier, latter):
    return earlier + latter


def plain_body(queries, key_rows, value_rows, grad_out):
    head_count, tokens, head_width = queries.shape
    tile_count = tokens // TILE
    tile_shape = (head_count, tile_count, TILE, head_width)
    query_tiles = queries.reshape(tile_shape)
    key_tiles = key_rows.reshape(tile_shape)
    value_tiles = value_rows.reshape(tile_shape)
    grad_tiles = grad_out.reshape(tile_shape)

    def product(rule, a, b):
        return jnp.einsum(rule, a, b, preferred_element_type=F32)

    key_state = product("hjsa,hjsb->hjab", key_tiles, value_tiles)
    query_state = product("hjta,hjtb->hjab", query_tiles, grad_tiles)
    local_keys = jnp.sum(key_state, 1)
    local_queries = jnp.sum(query_state, 1)
    blank_state = jnp.zeros_like(local_keys)
    incoming = entering(local_keys, "seq", add_states, blank_state, False)
    outgoing = entering(local_queries, "seq", add_states, blank_state, True)
    zero_state = jnp.zeros((head_count, 1, head_width, head_width), F32)
    earlier_states = incoming[:, None] + jnp.concatenate(
        [zero_state, jnp.cumsum(key_state, 1)[:, :-1]], 1
    )
    later_states = outgoing[:, None] + jnp.concatenate(
        [jnp.cumsum(query_state[:, ::-1], 1)[:, ::-1][:, 1:], zero_state], 1
    )
    earlier_states = earlier_states.astype(BF16)
    later_states = later_states.astype(BF16)
    causal = (jnp.arange(TILE)[:, None] >= jnp.arange(TILE)[None, :])[None, None]
    out_scores = product("hjta,hjsa->hjts", grad_tiles, value_tiles)
    out_scores = jnp.where(causal, out_scores, 0.0).astype(BF16)
    attn_scores = product("hjta,hjsa->hjts", query_tiles, key_tiles)
    attn_scores = jnp.where(causal, attn_scores, 0.0).astype(BF16)
    grad_query = product("hjts,hjsa->hjta", out_scores, key_tiles)
    grad_query = grad_query + product("hjtb,hjab->hjta", grad_tiles, earlier_states)
    grad_key = product("hjts,hjta->hjsa", out_scores, query_tiles)
    grad_key = grad_key + product("hjsb,hjab->hjsa", value_tiles, later_states)
    grad_value = product("hjts,hjtb->hjsb", attn_scores, grad_tiles)
    grad_value = grad_value + product("hjsa,hjab->hjsb", key_tiles, later_states)
    flat_shape = (head_count, tokens, head_width)
    return tuple(
        x.astype(BF16).reshape(flat_shape) for x in (grad_query, grad_key, grad_value)
    )


def dot(a, b, da, db):
    return lax.dot_general(a, b, (((da,), (db,)), ((), ())), preferred_element_type=F32)


def state_kernel(place, q, k, v, g, out):
    out[0, 0] = dot(k[0], v[0], 0, 0)
    out[0, 1] = dot(q[0], g[0], 0, 0)


def states_of(place, q, k, v, g, slots, other):
    _, tokens, width = q.shape

    def head(i, place):
        core = 1 - place[0] if other else place[0]
        return core * slots + (i ^ place[1])

    rows = pl.BlockSpec((1, tokens, width), lambda i, place: (head(i, place), 0, 0))
    return pl.pallas_call(
        state_kernel,
        out_shape=jax.ShapeDtypeStruct((slots, 2, width, width), F32),
        grid_spec=pltpu.PrefetchScalarGridSpec(
            num_scalar_prefetch=1,
            grid=(slots,),
            in_specs=[rows] * 4,
            out_specs=pl.BlockSpec((1, 2, width, width), lambda i, place: (i, 0, 0, 0)),
        ),
        cost_estimate=pl.CostEstimate(
            flops=slots * 4 * tokens * width * width,
            bytes_accessed=slots * (8 * tokens * width + 8 * width * width),
            transcendentals=0,
        ),
    )(place, q, k, v, g)


def local_kernel(q, k, v, g, gq, gk, gv):
    tokens = q.shape[1]
    row = lax.broadcasted_iota(jnp.int32, (tokens, tokens), 0)
    col = lax.broadcasted_iota(jnp.int32, (tokens, tokens), 1)
    q, k, v, g = q[0], k[0], v[0], g[0]
    score = jnp.where(row >= col, dot(g, v, 1, 1), 0.0).astype(BF16)
    gq[0] = dot(score, k, 1, 0)
    score = jnp.where(row <= col, dot(v, g, 1, 1), 0.0).astype(BF16)
    gk[0] = dot(score, q, 1, 0)
    score = jnp.where(row <= col, dot(k, q, 1, 1), 0.0).astype(BF16)
    gv[0] = dot(score, g, 1, 0)


def local_parts(q, k, v, g):
    heads, tokens, width = q.shape
    rows = pl.BlockSpec((1, tokens, width), lambda i: (i, 0, 0))
    return pl.pallas_call(
        local_kernel,
        out_shape=[jax.ShapeDtypeStruct(q.shape, F32)] * 3,
        grid=(heads,),
        in_specs=[rows] * 4,
        out_specs=[rows] * 3,
        cost_estimate=pl.CostEstimate(
            flops=heads * 12 * tokens * tokens * width,
            bytes_accessed=heads * 20 * tokens * width,
            transcendentals=0,
        ),
    )(q, k, v, g)


def final_kernel(place, k, v, g, lq, lk, lv, own, other, gq, gk, gv):
    mine = pl.program_id(0) < pl.num_programs(0) // 2
    state = jnp.where(mine, own[0], other[0]).astype(BF16)
    earlier, later = state[0], state[1]
    gq[0] = (lq[0] + dot(g[0], earlier, 1, 1)).astype(BF16)
    gk[0] = (lk[0] + dot(v[0], later, 1, 1)).astype(BF16)
    gv[0] = (lv[0] + dot(k[0], later, 1, 0)).astype(BF16)


def final_sums(place, k, v, g, parts, own, other):
    heads, tokens, width = k.shape
    slots = own.shape[0]

    def head(i, place):
        core = place[0] ^ (i // slots)
        return core * slots + ((i % slots) ^ place[1])

    rows = pl.BlockSpec((1, tokens, width), lambda i, place: (head(i, place), 0, 0))
    first = pl.BlockSpec(
        (1, 2, width, width), lambda i, place: (jnp.minimum(i, slots - 1), 0, 0, 0)
    )
    second = pl.BlockSpec(
        (1, 2, width, width), lambda i, place: (jnp.maximum(i - slots, 0), 0, 0, 0)
    )
    return pl.pallas_call(
        final_kernel,
        out_shape=[jax.ShapeDtypeStruct(k.shape, BF16)] * 3,
        grid_spec=pltpu.PrefetchScalarGridSpec(
            num_scalar_prefetch=1,
            grid=(heads,),
            in_specs=[rows] * 6 + [first, second],
            out_specs=[rows] * 3,
        ),
        cost_estimate=pl.CostEstimate(
            flops=heads * 6 * tokens * width * width,
            bytes_accessed=heads * (24 * tokens * width + 8 * width * width),
            transcendentals=0,
        ),
    )(place, k, v, g, *parts, own, other)


def swap(x, mask):
    count = lax.axis_size("seq")
    return lax.ppermute(x, "seq", [(i, i ^ mask) for i in range(count)])


def sliced_body(group):
    def body(queries, key_rows, value_rows, grad_out):
        count, index = lax.axis_size("seq"), lax.axis_index("seq")
        slots = group
        core = index & 1
        rank = (index >> 1) & (group - 1)
        place = jnp.stack([core, rank]).astype(jnp.int32)
        data = (queries, key_rows, value_rows, grad_out)

        away = states_of(place, *data, slots, True)
        came = swap(away, 1)
        keep = states_of(place, *data, slots, False)
        total = came + keep

        held = [total[0]] + [swap(total[j], 2 * j) for j in range(1, group)]
        parts = local_parts(*data)

        block = sum(held[1:], held[0])
        keys, rests = block[0], block[1]
        carry = jnp.zeros_like(block)
        bit = 2 * group
        while bit < count:
            upper = (index & bit) != 0
            if 2 * bit < count:
                got = swap(jnp.stack([keys, rests]), bit)
                keys, rests = keys + got[0], rests + got[1]
                got_keys, got_rests = got[0], got[1]
            else:
                got_keys = got_rests = swap(jnp.where(upper, rests, keys), bit)
            carry = carry + jnp.stack(
                [jnp.where(upper, got_keys, 0.0), jnp.where(upper, 0.0, got_rests)]
            )
            bit *= 2

        def outside(j):
            earlier, later = carry[0], carry[1]
            for i in range(group):
                if i != j:
                    before = (rank ^ i) < (rank ^ j)
                    earlier = earlier + jnp.where(before, held[i][0], 0.0)
                    later = later + jnp.where(before, 0.0, held[i][1])
            return jnp.stack([earlier, later])

        around = jnp.stack(
            [outside(0)] + [swap(outside(j), 2 * j) for j in range(1, group)]
        )
        first = core == 0
        mine = around + jnp.stack(
            [jnp.where(first, 0.0, came[:, 0]), jnp.where(first, came[:, 1], 0.0)], 1
        )
        theirs = around + jnp.stack(
            [jnp.where(first, keep[:, 0], 0.0), jnp.where(first, 0.0, keep[:, 1])], 1
        )
        other = swap(theirs, 1)
        return tuple(final_sums(place, key_rows, value_rows, grad_out, parts, mine, other))

    return body


def solution(mesh):
    count = mesh.shape["seq"]

    def run(queries, key_rows, value_rows, grad_out):
        heads = queries.shape[0] // mesh.shape["head"]
        tokens = queries.shape[1] // count
        group = heads // 2
        powers = all(n > 0 and n & (n - 1) == 0 for n in (count, group))
        fits = powers and heads == 2 * group and tokens == TILE and count >= 4 * group
        body = sliced_body(group) if fits else plain_body
        return jax.shard_map(
            body, mesh=mesh, in_specs=(SPEC,) * 4, out_specs=(SPEC,) * 3, check_vma=False
        )(queries, key_rows, value_rows, grad_out)

    return run
```

time: 197 us -> 55.3 us (0.28)
  waiting for transfers between devices: 127 us -> 13.2 us
  other arithmetic: 39.4 us -> 2.91 us
  Pallas kernels: 0 us -> 24.1 us
  between operations: 14.2 us -> 0.73 us
  starting transfers between devices: 0.08 us -> 12.4 us
  matrix products: 11.9 us -> 0 us
    all_gather x2 -> x0, waiting for transfers between devices: 127 us -> none  [entering(): everything = lax.all_gather(x, axis)]
    select_n x32 -> x3, other arithmetic: 39.4 us -> 0.08 us  [the longest x1 0.04 us: body(): jnp.where(first, keep[:, 0], 0.0)]
    pallas_call x0 -> x4, Pallas kernels: none -> 24.1 us  [the longest x2 8.7 us: states_of(): pl.pallas_call(state_kernel, out_shape=jax.ShapeDtypeStruct((slots, 2, wi...]
    ppermute x0 -> x9, waiting for transfers between devices: none -> 13.2 us  [swap(): return lax.ppermute(x, 'seq', [(i, i ^ mask) for i in range(count)])]
    ppermute x0 -> x9, starting transfers between devices: none -> 12.4 us  [swap(): return lax.ppermute(x, 'seq', [(i, i ^ mask) for i in range(count)])]
    dot_general x9 -> x0, matrix products: 11.9 us -> none  [the longest x1 2.73 us: body(): jnp.einsum('hjts,hjtb->hjsb', attn_scores, grad_tiles, preferred_element_...]
    add x0 -> x3, other arithmetic: none -> 2.04 us  [the longest x1 1.1 us: body(): total = came + keep]
  transfers between devices with their start and end apart: 2 -> 9, of which waited for: 2 -> 6; matrix products, arithmetic and copies ran while one was open for 13% -> 0% of each run, Pallas kernels for 0% -> 22%
where the time goes in v1:
time: 55.3 us; the launch traced here: 54.3 us
  Pallas kernels  24.1 us (44%)
  waiting for transfers between devices  13.2 us (24%)
  starting transfers between devices  12.4 us (22%)
  other arithmetic  2.91 us (5%)
  local copies, waits for them, and re-layouts  0.83 us (2%)
  between operations  0.73 us (1%)
    ppermute x9, waiting for transfers between devices, swap(): return lax.ppermute(x, 'seq', [(i, i ^ mask) for i in range(count)])  13.2 us
    ppermute x9, starting transfers between devices, swap(): return lax.ppermute(x, 'seq', [(i, i ^ mask) for i in range(count)])  12.4 us
    pallas_call x2, Pallas kernels, states_of(): pl.pallas_call(state_kernel, out_shape=jax.ShapeDtypeStruct((slots, 2, wi...  8.7 us
    pallas_call x1, Pallas kernels, final_sums(): pl.pallas_call(final_kernel, out_shape=[jax.ShapeDtypeStruct(k.shape, BF1...  7.8 us
    pallas_call x1, Pallas kernels, local_parts(): pl.pallas_call(local_kernel, out_shape=[jax.ShapeDtypeStruct(q.shape, F32...  7.65 us
  transfers between devices with their start and end apart: 9, of which 6 were waited for; matrix products, arithmetic and copies ran while one was open for 0% of the time, Pallas kernels for 22%

profile of v1, /device:TPU:1, one launch (start us, length us, event | category | flops | bytes accessed | tf_op | source)
XLA Modules:
  0.0 54.3 jit_solution(15119247528633524569)
XLA Ops:
  0.6 0.6 %pad_add_fusion.place = s32[2]{0:T(128)} fusion(s32[1]{0:T(128)} %bitcast.1, s32[1]{0:T(128)} %bitcast), kind=kLoop, calls=%fused_computation.52 | loop fusion | flops 2 | bytes 16 | tf_op jit(solution)/shard_map/stack | solution.py:193
  1.2 4.4 %shard_map.68 = f32[4,2,128,128]{3,2,1,0:T(8,128)} custom-call(s32[2]{0:T(128)} %pad_add_fusion.place, bf16[8,256,128]{2,1,0:T(8,128)(2,1)} %q.5, bf16[8,256,128]{2,1,0:T(8,128)(2,1)} %k.7, bf16[8,256,128]{2,1,0:T(8,128)(2,1)} %v.7, bf16[8,256,128]{2,1,0:T(8,128)(2,1)} %g.7), custom_call_target="tpu_custom_call" | custom-call | flops 67108864 | bytes 1572864 | tf_op jit(solution)/shard_map/pallas_call | solution.py:94
  5.6 0.1 collective-permute-start
  5.7 4.3 %shard_map.69 = f32[4,2,128,128]{3,2,1,0:T(8,128)} custom-call(s32[2]{0:T(128)} %pad_add_fusion.place, bf16[8,256,128]{2,1,0:T(8,128)(2,1)} %q.5, bf16[8,256,128]{2,1,0:T(8,128)(2,1)} %k.7, bf16[8,256,128]{2,1,0:T(8,128)(2,1)} %v.7, bf16[8,256,128]{2,1,0:T(8,128)(2,1)} %g.7), custom_call_target="tpu_custom_call" | custom-call | flops 67108864 | bytes 1572864 | tf_op jit(solution)/shard_map/pallas_call | solution.py:94
  10.0 0.0 collective-permute-done
  10.0 1.1 %add.90 = f32[4,2,128,128]{3,2,1,0:T(8,128)S(1)} add(f32[4,2,128,128]{3,2,1,0:T(8,128)S(1)} %collective-permute-done, f32[4,2,128,128]{3,2,1,0:T(8,128)} %shard_map.69) | non-fusion elementwise | flops 131072 | bytes 1572864 | tf_op jit(solution)/shard_map/add | solution.py:199
  11.1 0.0 copy-start
  11.2 3.7 %collective-permute-start.3 = (f32[2,128,128]{2,1,0:T(8,128)S(1)}, f32[2,128,128]{2,1,0:T(8,128)S(1)}, u32[]{:S(2)}, u32[]{:S(2)}) collective-permute-start(f32[2,128,128]{2,1,0:T(8,128)S(1)} %get-tuple-element.19), channel_id=1, source_target_pairs={{0,12},{2,14},{4,8},{6,10},{8,4},{10,6},{12,0},{14,2},{16,28},{18,... | collective-permute-start | bytes 393224 | tf_op jit(solution)/shard_map/ppermute | solution.py:184
  14.9 0.2 collective-permute-start.2
  15.1 0.2 collective-permute-start.1
  15.3 0.0 copy-done
  15.3 3.5 %collective-permute-done.3 = f32[2,128,128]{2,1,0:T(8,128)S(1)} collective-permute-done((f32[2,128,128]{2,1,0:T(8,128)S(1)}, f32[2,128,128]{2,1,0:T(8,128)S(1)}, u32[]{:S(2)}, u32[]{:S(2)}) %collective-permute-start.3) | collective-permute-done | bytes 131104 | tf_op jit(solution)/shard_map/ppermute | solution.py:184
  18.8 2.8 %collective-permute-done.2 = f32[2,128,128]{2,1,0:T(8,128)S(1)} collective-permute-done((f32[2,128,128]{2,1,0:T(8,128)S(1)}, f32[2,128,128]{2,1,0:T(8,128)S(1)}, u32[]{:S(2)}, u32[]{:S(2)}) %collective-permute-start.2) | collective-permute-done | bytes 131104 | tf_op jit(solution)/shard_map/ppermute | solution.py:184
  21.6 0.1 collective-permute-done.1
  21.7 2.5 %collective-permute-start.4 = (f32[128,128]{1,0:T(8,128)S(1)}, f32[128,128]{1,0:T(8,128)S(1)}, u32[]{:S(2)}, u32[]{:S(2)}) collective-permute-start(f32[128,128]{1,0:T(8,128)S(1)} %fusion.3), channel_id=1, source_target_pairs={{0,16},{2,18},{4,20},{6,22},{8,24},{10,26},{12,28},{14,30},{16,0},... | collective-permute-start | bytes 196616 | tf_op jit(solution)/shard_map/ppermute | solution.py:184
  24.3 1.6 %collective-permute-done.4 = f32[128,128]{1,0:T(8,128)S(1)} collective-permute-done((f32[128,128]{1,0:T(8,128)S(1)}, f32[128,128]{1,0:T(8,128)S(1)}, u32[]{:S(2)}, u32[]{:S(2)}) %collective-permute-start.4) | collective-permute-done | bytes 65568 | tf_op jit(solution)/shard_map/ppermute | solution.py:184
  25.9 3.6 %collective-permute-start.7 = (f32[2,128,128]{2,1,0:T(8,128)S(1)}, f32[2,128,128]{2,1,0:T(8,128)S(1)}, u32[]{:S(2)}, u32[]{:S(2)}) collective-permute-start(f32[2,128,128]{2,1,0:T(8,128)S(1)} %pad_maximum_fusion.3), channel_id=1, source_target_pairs={{0,12},{2,14},{4,8},{6,10},{8,4},{10,6},{12,0},{14,2},{16,28},{18,... | collective-permute-start | bytes 393224 | tf_op jit(solution)/shard_map/ppermute | solution.py:184
  29.6 0.1 collective-permute-start.5
  29.7 0.3 collective-permute-start.6
  30.1 1.8 %collective-permute-done.7 = f32[2,128,128]{2,1,0:T(8,128)S(1)} collective-permute-done((f32[2,128,128]{2,1,0:T(8,128)S(1)}, f32[2,128,128]{2,1,0:T(8,128)S(1)}, u32[]{:S(2)}, u32[]{:S(2)}) %collective-permute-start.7) | collective-permute-done | bytes 131104 | tf_op jit(solution)/shard_map/ppermute | solution.py:184
  31.9 3.5 %collective-permute-done.5 = f32[2,128,128]{2,1,0:T(8,128)S(1)} collective-permute-done((f32[2,128,128]{2,1,0:T(8,128)S(1)}, f32[2,128,128]{2,1,0:T(8,128)S(1)}, u32[]{:S(2)}, u32[]{:S(2)}) %collective-permute-start.5) | collective-permute-done | bytes 131104 | tf_op jit(solution)/shard_map/ppermute | solution.py:184
  35.4 0.0 collective-permute-done.6
  35.4 0.9 %maximum_add_fusion.1 = (f32[4,2,128,128]{3,2,1,0:T(8,128)S(1)}, f32[4,2,128,128]{3,2,1,0:T(8,128)}) fusion(f32[4,1,128,128]{3,2,1,0:T(8,128)S(1)} %get-tuple-element.18, f32[4,1,128,128]{3,2,1,0:T(8,128)S(1)} %get-tuple-element.17, f32[1,2,128,128]{3,2,1,0:T(8,128)S(1)} %bitcast.135, f32[1,2,128,128]{3,2,1,0:T(8,128)S(1)} %bitcast.137, ...), kind=kLoop, calls=%fused_computation.2 | loop fusion | flops 917504 | bytes 2621440 | tf_op jit(solution)/shard_map/add | solution.py:237
  36.3 1.7 %collective-permute-start.8 = (f32[4,2,128,128]{3,2,1,0:T(8,128)S(1)}, f32[4,2,128,128]{3,2,1,0:T(8,128)S(1)}, u32[]{:S(2)}, u32[]{:S(2)}) collective-permute-start(f32[4,2,128,128]{3,2,1,0:T(8,128)S(1)} %get-tuple-element.15), channel_id=1, source_target_pairs={{0,2},{2,0},{4,6},{6,4},{8,10},{10,8},{12,14},{14,12},{16,18},{18,... | collective-permute-start | bytes 1572872 | tf_op jit(solution)/shard_map/ppermute | solution.py:184
  38.0 7.6 %shard_map.67 = (f32[8,256,128]{2,1,0:T(8,128)}, f32[8,256,128]{2,1,0:T(8,128)}, f32[8,256,128]{2,1,0:T(8,128)}) custom-call(bf16[8,256,128]{2,1,0:T(8,128)(2,1)} %q.5, bf16[8,256,128]{2,1,0:T(8,128)(2,1)} %k.7, bf16[8,256,128]{2,1,0:T(8,128)(2,1)} %v.7, bf16[8,256,128]{2,1,0:T(8,128)(2,1)} %g.7), custom_call_target="tpu_custom_call" | custom-call | flops 805306368 | bytes 5242880 | tf_op jit(solution)/shard_map/pallas_call | solution.py:127
  45.7 0.0 collective-permute-done.8.other
  45.7 0.0 copy-start.1
  45.7 0.8 %copy-done.1 = f32[4,2,128,128]{3,2,1,0:T(8,128)} copy-done((f32[4,2,128,128]{3,2,1,0:T(8,128)}, f32[4,2,128,128]{3,2,1,0:T(8,128)S(1)}, u32[]{:S(2)}) %copy-start.1) | copy-done | bytes 524312
  46.5 7.8 %shard_map.70 = (bf16[8,256,128]{2,1,0:T(8,128)(2,1)}, bf16[8,256,128]{2,1,0:T(8,128)(2,1)}, bf16[8,256,128]{2,1,0:T(8,128)(2,1)}) custom-call(s32[2]{0:T(128)} %pad_add_fusion.place, bf16[8,256,128]{2,1,0:T(8,128)(2,1)} %k.7, bf16[8,256,128]{2,1,0:T(8,128)(2,1)} %v.7, bf16[8,256,128]{2,1,0:T(8,128)(2,1)} %g.7, f32[8,256,128]{2,1,0:T(8,128)} %get-tuple-element.6.lq, ...), custom_call_target="tpu_custom_call" | custom-call | flops 201326592 | bytes 7340032 | tf_op jit(solution)/shard_map/pallas_call | solution.py:165
  (13 shorter events, 0.3 us)
Async XLA Ops:
  5.6 4.4 %collective-permute-start = (f32[4,2,128,128]{3,2,1,0:T(8,128)}, f32[4,2,128,128]{3,2,1,0:T(8,128)S(1)}, u32[]{:S(2)}, u32[]{:S(2)}) collective-permute-start(f32[4,2,128,128]{3,2,1,0:T(8,128)} %shard_map.68), channel_id=1, source_target_pairs={{0,2},{2,0},{4,6},{6,4},{8,10},{10,8},{12,14},{14,12},{16,18},{18,... | collective-permute-start | bytes 1572872 | tf_op jit(solution)/shard_map/ppermute | solution.py:184
  11.1 4.2 %copy-start = (f32[4,2,128,128]{3,2,1,0:T(8,128)S(1)}, f32[4,2,128,128]{3,2,1,0:T(8,128)}, u32[]{:S(2)}) copy-start(f32[4,2,128,128]{3,2,1,0:T(8,128)} %shard_map.69) | copy-start | bytes 1572868
  11.2 7.6 %collective-permute-start.3 = (f32[2,128,128]{2,1,0:T(8,128)S(1)}, f32[2,128,128]{2,1,0:T(8,128)S(1)}, u32[]{:S(2)}, u32[]{:S(2)}) collective-permute-start(f32[2,128,128]{2,1,0:T(8,128)S(1)} %get-tuple-element.19), channel_id=1, source_target_pairs={{0,12},{2,14},{4,8},{6,10},{8,4},{10,6},{12,0},{14,2},{16,28},{18,... | collective-permute-start | bytes 393224 | tf_op jit(solution)/shard_map/ppermute | solution.py:184
  14.9 6.7 %collective-permute-start.2 = (f32[2,128,128]{2,1,0:T(8,128)S(1)}, f32[2,128,128]{2,1,0:T(8,128)S(1)}, u32[]{:S(2)}, u32[]{:S(2)}) collective-permute-start(f32[2,128,128]{2,1,0:T(8,128)S(1)} %get-tuple-element.20), channel_id=1, source_target_pairs={{0,8},{2,10},{4,12},{6,14},{8,0},{10,2},{12,4},{14,6},{16,24},{18,... | collective-permute-start | bytes 393224 | tf_op jit(solution)/shard_map/ppermute | solution.py:184
  15.1 6.6 %collective-permute-start.1 = (f32[2,128,128]{2,1,0:T(8,128)S(1)}, f32[2,128,128]{2,1,0:T(8,128)S(1)}, u32[]{:S(2)}, u32[]{:S(2)}) collective-permute-start(f32[2,128,128]{2,1,0:T(8,128)S(1)} %get-tuple-element.21), channel_id=1, source_target_pairs={{0,4},{2,6},{4,0},{6,2},{8,12},{10,14},{12,8},{14,10},{16,20},{18,... | collective-permute-start | bytes 393224 | tf_op jit(solution)/shard_map/ppermute | solution.py:184
  21.7 4.2 %collective-permute-start.4 = (f32[128,128]{1,0:T(8,128)S(1)}, f32[128,128]{1,0:T(8,128)S(1)}, u32[]{:S(2)}, u32[]{:S(2)}) collective-permute-start(f32[128,128]{1,0:T(8,128)S(1)} %fusion.3), channel_id=1, source_target_pairs={{0,16},{2,18},{4,20},{6,22},{8,24},{10,26},{12,28},{14,30},{16,0},... | collective-permute-start | bytes 196616 | tf_op jit(solution)/shard_map/ppermute | solution.py:184
  25.9 5.9 %collective-permute-start.7 = (f32[2,128,128]{2,1,0:T(8,128)S(1)}, f32[2,128,128]{2,1,0:T(8,128)S(1)}, u32[]{:S(2)}, u32[]{:S(2)}) collective-permute-start(f32[2,128,128]{2,1,0:T(8,128)S(1)} %pad_maximum_fusion.3), channel_id=1, source_target_pairs={{0,12},{2,14},{4,8},{6,10},{8,4},{10,6},{12,0},{14,2},{16,28},{18,... | collective-permute-start | bytes 393224 | tf_op jit(solution)/shard_map/ppermute | solution.py:184
  29.6 5.8 %collective-permute-start.5 = (f32[2,128,128]{2,1,0:T(8,128)S(1)}, f32[2,128,128]{2,1,0:T(8,128)S(1)}, u32[]{:S(2)}, u32[]{:S(2)}) collective-permute-start(f32[2,128,128]{2,1,0:T(8,128)S(1)} %pad_maximum_fusion.1), channel_id=1, source_target_pairs={{0,4},{2,6},{4,0},{6,2},{8,12},{10,14},{12,8},{14,10},{16,20},{18,... | collective-permute-start | bytes 393224 | tf_op jit(solution)/shard_map/ppermute | solution.py:184
  29.7 5.7 %collective-permute-start.6 = (f32[2,128,128]{2,1,0:T(8,128)S(1)}, f32[2,128,128]{2,1,0:T(8,128)S(1)}, u32[]{:S(2)}, u32[]{:S(2)}) collective-permute-start(f32[2,128,128]{2,1,0:T(8,128)S(1)} %pad_maximum_fusion.2), channel_id=1, source_target_pairs={{0,8},{2,10},{4,12},{6,14},{8,0},{10,2},{12,4},{14,6},{16,24},{18,... | collective-permute-start | bytes 393224 | tf_op jit(solution)/shard_map/ppermute | solution.py:184
  36.3 9.4 %collective-permute-start.8 = (f32[4,2,128,128]{3,2,1,0:T(8,128)S(1)}, f32[4,2,128,128]{3,2,1,0:T(8,128)S(1)}, u32[]{:S(2)}, u32[]{:S(2)}) collective-permute-start(f32[4,2,128,128]{3,2,1,0:T(8,128)S(1)} %get-tuple-element.15), channel_id=1, source_target_pairs={{0,2},{2,0},{4,6},{6,4},{8,10},{10,8},{12,14},{14,12},{16,18},{18,... | collective-permute-start | bytes 1572872 | tf_op jit(solution)/shard_map/ppermute | solution.py:184
  45.7 0.8 %copy-start.1 = (f32[4,2,128,128]{3,2,1,0:T(8,128)}, f32[4,2,128,128]{3,2,1,0:T(8,128)S(1)}, u32[]{:S(2)}) copy-start(f32[4,2,128,128]{3,2,1,0:T(8,128)S(1)} %collective-permute-done.8.other) | copy-start | bytes 1572868

commit v2 on v1

--- a/solution.py
+++ b/solution.py
@@ -1,3 +1,5 @@
+import functools
+
 import jax
 import jax.numpy as jnp
 from jax import lax
@@ -74,109 +76,163 @@
     )
 
 
+WHOLE = pl.BlockSpec(memory_space=pltpu.VMEM)
+PLACED = pl.BlockSpec(memory_space=pl.ANY)
+ROOM = pltpu.CompilerParams(vmem_limit_bytes=16 * 2**20)
+
+
+def near(x):
+    return pltpu.with_memory_space_constraint(x, pltpu.VMEM)
+
+
 def dot(a, b, da, db):
     return lax.dot_general(a, b, (((da,), (db,)), ((), ())), preferred_element_type=F32)
 
 
-def state_kernel(place, q, k, v, g, out):
-    out[0, 0] = dot(k[0], v[0], 0, 0)
-    out[0, 1] = dot(q[0], g[0], 0, 0)
-
-
-def states_of(place, q, k, v, g, slots, other):
-    _, tokens, width = q.shape
-
-    def head(i, place):
-        core = 1 - place[0] if other else place[0]
-        return core * slots + (i ^ place[1])
-
-    rows = pl.BlockSpec((1, tokens, width), lambda i, place: (head(i, place), 0, 0))
+def head_of(slots, slot, other):
+    index = lax.axis_index("seq")
+    core = 1 - (index & 1) if other else index & 1
+    return core * slots + (((index >> 1) & (slots - 1)) ^ slot)
+
+
+def state_kernel(q, k, v, g, qs, ks, vs, gs, out, sems, *, slots, other):
+    copies = []
+    for i in range(slots):
+        head = head_of(slots, i, other)
+        row = []
+        for n, (far, close) in enumerate(((k, ks), (v, vs), (q, qs), (g, gs))):
+            row.append(pltpu.make_async_copy(far.at[head], close.at[i], sems.at[i, n]))
+            row[-1].start()
+        copies.append(row)
+    for i in range(slots):
+        copies[i][0].wait()
+        copies[i][1].wait()
+        out[i, 0] = dot(ks[i], vs[i], 0, 0)
+        copies[i][2].wait()
+        copies[i][3].wait()
+        out[i, 1] = dot(qs[i], gs[i], 0, 0)
+
+
+def states_of(data, slots, other):
+    _, tokens, width = data[0].shape
+    rows = pltpu.VMEM((slots, tokens, width), BF16)
     return pl.pallas_call(
-        state_kernel,
-        out_shape=jax.ShapeDtypeStruct((slots, 2, width, width), F32),
-        grid_spec=pltpu.PrefetchScalarGridSpec(
-            num_scalar_prefetch=1,
-            grid=(slots,),
-            in_specs=[rows] * 4,
-            out_specs=pl.BlockSpec((1, 2, width, width), lambda i, place: (i, 0, 0, 0)),
-        ),
+        functools.partial(state_kernel, slots=slots, other=other),
+        out_shape=[rows] * 4 + [pltpu.VMEM((slots, 2, width, width), F32)],
+        in_specs=[PLACED] * 4,
+        out_specs=[WHOLE] * 5,
+        scratch_shapes=[pltpu.SemaphoreType.DMA((slots, 4))],
+        compiler_params=ROOM,
         cost_estimate=pl.CostEstimate(
             flops=slots * 4 * tokens * width * width,
-            bytes_accessed=slots * (8 * tokens * width + 8 * width * width),
+            bytes_accessed=slots * 8 * tokens * width,
             transcendentals=0,
         ),
-    )(place, q, k, v, g)
-
-
-def local_kernel(q, k, v, g, gq, gk, gv):
-    tokens = q.shape[1]
+    )(*data)
+
+
+def total_kernel(came, keep, *outs):
+    for i, out in enumerate(outs):
+        out[...] = came[i] + keep[i]
+
+
+def totals_of(came, keep):
+    slots, _, width, _ = keep.shape
+    return pl.pallas_call(
+        total_kernel,
+        out_shape=[pltpu.VMEM((2, width, width), F32)] * slots,
+        in_specs=[WHOLE] * 2,
+        out_specs=[WHOLE] * slots,
+        compiler_params=ROOM,
+    )(near(came), near(keep))
+
+
+def local_kernel(qa, ka, va, ga, qb, kb, vb, gb, after, *outs):
+    slots, tokens, _ = qa.shape
     row = lax.broadcasted_iota(jnp.int32, (tokens, tokens), 0)
     col = lax.broadcasted_iota(jnp.int32, (tokens, tokens), 1)
-    q, k, v, g = q[0], k[0], v[0], g[0]
-    score = jnp.where(row >= col, dot(g, v, 1, 1), 0.0).astype(BF16)
-    gq[0] = dot(score, k, 1, 0)
-    score = jnp.where(row <= col, dot(v, g, 1, 1), 0.0).astype(BF16)
-    gk[0] = dot(score, q, 1, 0)
-    score = jnp.where(row <= col, dot(k, q, 1, 1), 0.0).astype(BF16)
-    gv[0] = dot(score, g, 1, 0)
-
-
-def local_parts(q, k, v, g):
-    heads, tokens, width = q.shape
-    rows = pl.BlockSpec((1, tokens, width), lambda i: (i, 0, 0))
-    return pl.pallas_call(
+    for half, (qs, ks, vs, gs) in enumerate(((qa, ka, va, ga), (qb, kb, vb, gb))):
+        gq, gk, gv = outs[3 * half : 3 * half + 3]
+        for i in range(slots):
+            q, k, v, g = qs[i], ks[i], vs[i], gs[i]
+            score = jnp.where(row >= col, dot(g, v, 1, 1), 0.0).astype(BF16)
+            gq[i] = dot(score, k, 1, 0)
+            score = jnp.where(row <= col, dot(v, g, 1, 1), 0.0).astype(BF16)
+            gk[i] = dot(score, q, 1, 0)
+            score = jnp.where(row <= col, dot(k, q, 1, 1), 0.0).astype(BF16)
+            gv[i] = dot(score, g, 1, 0)
+
+
+def local_parts(own, other, after):
+    slots, tokens, width = own[0].shape
+    out = pl.pallas_call(
         local_kernel,
-        out_shape=[jax.ShapeDtypeStruct(q.shape, F32)] * 3,
-        grid=(heads,),
-        in_specs=[rows] * 4,
-        out_specs=[rows] * 3,
+        out_shape=[pltpu.VMEM(own[0].shape, F32)] * 6,
+        in_specs=[WHOLE] * 8 + [PLACED],
+        out_specs=[WHOLE] * 6,
+        compiler_params=ROOM,
         cost_estimate=pl.CostEstimate(
-            flops=heads * 12 * tokens * tokens * width,
-            bytes_accessed=heads * 20 * tokens * width,
+            flops=slots * 24 * tokens * tokens * width,
+            bytes_accessed=slots * 40 * tokens * width,
             transcendentals=0,
         ),
-    )(q, k, v, g)
-
-
-def final_kernel(place, k, v, g, lq, lk, lv, own, other, gq, gk, gv):
-    mine = pl.program_id(0) < pl.num_programs(0) // 2
-    state = jnp.where(mine, own[0], other[0]).astype(BF16)
-    earlier, later = state[0], state[1]
-    gq[0] = (lq[0] + dot(g[0], earlier, 1, 1)).astype(BF16)
-    gk[0] = (lk[0] + dot(v[0], later, 1, 1)).astype(BF16)
-    gv[0] = (lv[0] + dot(k[0], later, 1, 0)).astype(BF16)
-
-
-def final_sums(place, k, v, g, parts, own, other):
-    heads, tokens, width = k.shape
-    slots = own.shape[0]
-
-    def head(i, place):
-        core = place[0] ^ (i // slots)
-        return core * slots + ((i % slots) ^ place[1])
-
-    rows = pl.BlockSpec((1, tokens, width), lambda i, place: (head(i, place), 0, 0))
-    first = pl.BlockSpec(
-        (1, 2, width, width), lambda i, place: (jnp.minimum(i, slots - 1), 0, 0, 0)
-    )
-    second = pl.BlockSpec(
-        (1, 2, width, width), lambda i, place: (jnp.maximum(i - slots, 0), 0, 0, 0)
-    )
+    )(*[near(x) for x in own], *[near(x) for x in other], near(after))
+    return out[:3], out[3:]
+
+
+def block_kernel(after, *refs):
+    out = refs[-1]
+    total = refs[0][...]
+    for x in refs[1:-1]:
+        total = total + x[...]
+    out[...] = total
+
+
+def block_sum(held, after):
     return pl.pallas_call(
-        final_kernel,
-        out_shape=[jax.ShapeDtypeStruct(k.shape, BF16)] * 3,
-        grid_spec=pltpu.PrefetchScalarGridSpec(
-            num_scalar_prefetch=1,
-            grid=(heads,),
-            in_specs=[rows] * 6 + [first, second],
-            out_specs=[rows] * 3,
-        ),
+        block_kernel,
+        out_shape=pltpu.VMEM(held[0].shape, F32),
+        in_specs=[PLACED] + [WHOLE] * len(held),
+        out_specs=WHOLE,
+        compiler_params=ROOM,
+    )(near(after), *[near(x) for x in held])
+
+
+def final_kernel(k, v, g, lq, lk, lv, state, *refs, other):
+    gq, gk, gv, bq, bk, bv, sems = refs[-7:]
+    slots = k.shape[0]
+    copies = []
+    for i in range(slots):
+        earlier, later = state[i, 0].astype(BF16), state[i, 1].astype(BF16)
+        head = head_of(slots, i, other)
+        bq[i] = (lq[i] + dot(g[i], earlier, 1, 1)).astype(BF16)
+        bk[i] = (lk[i] + dot(v[i], later, 1, 1)).astype(BF16)
+        bv[i] = (lv[i] + dot(k[i], later, 1, 0)).astype(BF16)
+        for n, (close, far) in enumerate(((bq, gq), (bk, gk), (bv, gv))):
+            copies.append(pltpu.make_async_copy(close.at[i], far.at[head], sems.at[i, n]))
+            copies[-1].start()
+    for copy in copies:
+        copy.wait()
+
+
+def final_sums(rows, parts, state, heads, other, filled=()):
+    _, k, v, g = rows
+    slots, tokens, width = k.shape
+    return pl.pallas_call(
+        functools.partial(final_kernel, other=other),
+        out_shape=[jax.ShapeDtypeStruct((heads, tokens, width), BF16)] * 3,
+        in_specs=[WHOLE] * 7 + [PLACED] * len(filled),
+        out_specs=[PLACED] * 3,
+        input_output_aliases={7 + n: n for n in range(len(filled))},
+        scratch_shapes=[pltpu.VMEM(k.shape, BF16)] * 3
+        + [pltpu.SemaphoreType.DMA((slots, 3))],
+        compiler_params=ROOM,
         cost_estimate=pl.CostEstimate(
-            flops=heads * 6 * tokens * width * width,
-            bytes_accessed=heads * (24 * tokens * width + 8 * width * width),
+            flops=slots * 6 * tokens * width * width,
+            bytes_accessed=slots * 6 * tokens * width,
             transcendentals=0,
         ),
-    )(place, k, v, g, *parts, own, other)
+    )(*[near(x) for x in (k, v, g, *parts, state)], *filled)
 
 
 def swap(x, mask):
@@ -190,18 +246,17 @@
         slots = group
         core = index & 1
         rank = (index >> 1) & (group - 1)
-        place = jnp.stack([core, rank]).astype(jnp.int32)
         data = (queries, key_rows, value_rows, grad_out)
 
-        away = states_of(place, *data, slots, True)
+        *away_rows, away = states_of(data, slots, True)
         came = swap(away, 1)
-        keep = states_of(place, *data, slots, False)
-        total = came + keep
+        *keep_rows, keep = states_of(data, slots, False)
+        total = totals_of(came, keep)
 
         held = [total[0]] + [swap(total[j], 2 * j) for j in range(1, group)]
-        parts = local_parts(*data)
-
-        block = sum(held[1:], held[0])
+        own_parts, other_parts = local_parts(keep_rows, away_rows, total[0])
+
+        block = block_sum(held, own_parts[0])
         keys, rests = block[0], block[1]
         carry = jnp.zeros_like(block)
         bit = 2 * group
@@ -238,7 +293,10 @@
             [jnp.where(first, keep[:, 0], 0.0), jnp.where(first, 0.0, keep[:, 1])], 1
         )
         other = swap(theirs, 1)
-        return tuple(final_sums(place, key_rows, value_rows, grad_out, parts, mine, other))
+        done = final_sums(keep_rows, own_parts, mine, queries.shape[0], False)
+        return tuple(
+            final_sums(away_rows, other_parts, other, queries.shape[0], True, done)
+        )
 
     return body
 

time: 55.3 us -> 43.2 us (0.78)
  Pallas kernels: 24.1 us -> 11.5 us
  local copies, waits for them, and re-layouts: 0.83 us -> 7.15 us
  waiting for transfers between devices: 13.2 us -> 9.57 us
  other arithmetic: 2.91 us -> 1.16 us
    pallas_call x4 -> x7, Pallas kernels: 24.1 us -> 11.5 us  [the longest x2 7.1 us: states_of(): pl.pallas_call(functools.partial(state_kernel, slots=slots, other=other),...]
    unnamed x4 -> x40, local copies, waits for them, and re-layouts: 0.8 us -> 7.15 us
    ppermute x9, waiting for transfers between devices: 13.2 us -> 9.57 us  [swap(): return lax.ppermute(x, 'seq', [(i, i ^ mask) for i in range(count)])]
    add x3 -> x1, other arithmetic: 2.04 us -> 0.11 us  [body(): around + jnp.stack([jnp.where(first, 0.0, came[:, 0]), jnp.where(first, c...]
    select_n x1, other arithmetic: 0.04 us -> 0.83 us  [body(): jnp.where(first, keep[:, 0], 0.0)]
    another operation x1 -> x0, other arithmetic: 0.61 us -> none  [body(): place = jnp.stack([core, rank]).astype(jnp.int32)]
  transfers between devices with their start and end apart: 9 -> 9, of which waited for: 6 -> 6; matrix products, arithmetic and copies ran while one was open for 0% -> 2% of each run, Pallas kernels for 22% -> 15%
where the time goes in v2:
time: 43.2 us; the launch traced here: 42.5 us
  starting transfers between devices  12.2 us (28%)
  Pallas kernels  11.5 us (27%)
  waiting for transfers between devices  9.57 us (22%)
  local copies, waits for them, and re-layouts  7.15 us (17%)
  other arithmetic  1.16 us (3%)
  between operations  0.86 us (2%)
    ppermute x9, starting transfers between devices, swap(): return lax.ppermute(x, 'seq', [(i, i ^ mask) for i in range(count)])  12.2 us
    ppermute x9, waiting for transfers between devices, swap(): return lax.ppermute(x, 'seq', [(i, i ^ mask) for i in range(count)])  9.57 us
    unnamed x40, local copies, waits for them, and re-layouts  7.15 us
    pallas_call x2, Pallas kernels, states_of(): pl.pallas_call(functools.partial(state_kernel, slots=slots, other=other),...  7.1 us
    pallas_call x2, Pallas kernels, final_sums(): pl.pallas_call(functools.partial(final_kernel, other=other), out_shape=[j...  2.33 us
    pallas_call x1, Pallas kernels, local_parts(): pl.pallas_call(local_kernel, out_shape=[pltpu.VMEM(own[0].shape, F32)] *...  2.02 us
  transfers between devices with their start and end apart: 9, of which 6 were waited for; matrix products, arithmetic and copies ran while one was open for 2% of the time, Pallas kernels for 15%

profile of v2, /device:TPU:1, one launch (start us, length us, event | category | flops | bytes accessed | tf_op | source)
XLA Modules:
  0.0 42.5 jit_solution(16266833489429627850)
XLA Ops:
  0.6 0.0 copy-start
  0.6 1.0 %copy-done = bf16[8,256,128]{2,1,0:T(8,128)(2,1)S(1)} copy-done((bf16[8,256,128]{2,1,0:T(8,128)(2,1)S(1)}, bf16[8,256,128]{2,1,0:T(8,128)(2,1)}, u32[]{:S(2)}) %copy-start) | copy-done | bytes 524312
  1.7 1.0 %copy-done.2 = bf16[8,256,128]{2,1,0:T(8,128)(2,1)S(1)} copy-done((bf16[8,256,128]{2,1,0:T(8,128)(2,1)S(1)}, bf16[8,256,128]{2,1,0:T(8,128)(2,1)}, u32[]{:S(2)}) %copy-start.2) | copy-done | bytes 524312
  2.7 1.0 %copy-done.4 = bf16[8,256,128]{2,1,0:T(8,128)(2,1)S(1)} copy-done((bf16[8,256,128]{2,1,0:T(8,128)(2,1)S(1)}, bf16[8,256,128]{2,1,0:T(8,128)(2,1)}, u32[]{:S(2)}) %copy-start.4) | copy-done | bytes 524312
  3.8 1.0 %copy-done.6 = bf16[8,256,128]{2,1,0:T(8,128)(2,1)S(1)} copy-done((bf16[8,256,128]{2,1,0:T(8,128)(2,1)S(1)}, bf16[8,256,128]{2,1,0:T(8,128)(2,1)}, u32[]{:S(2)}) %copy-start.6) | copy-done | bytes 524312
  4.8 3.9 %shard_map.67 = (bf16[4,256,128]{2,1,0:T(8,128)(2,1)S(1)}, bf16[4,256,128]{2,1,0:T(8,128)(2,1)S(1)}, bf16[4,256,128]{2,1,0:T(8,128)(2,1)S(1)}, bf16[4,256,128]{2,1,0:T(8,128)(2,1)S(1)}, f32[4,2,128,128]{3,2,1,0:T(8,128)}) custom-call(bf16[8,256,128]{2,1,0:T(8,128)(2,1)S(1)} %copy-done, bf16[8,256,128]{2,1,0:T(8,128)(2,1)S(1)} %copy-done.2, ...), custom_call_target="tpu_custom_call" | custom-call | flops 67108864 | bytes 1048576 | tf_op jit(solution)/shard_map/pallas_call | solution.py:119
  8.8 0.0 copy-start.14
  8.8 0.7 %copy-done.14 = bf16[4,256,128]{2,1,0:T(8,128)(2,1)} copy-done((bf16[4,256,128]{2,1,0:T(8,128)(2,1)}, bf16[4,256,128]{2,1,0:T(8,128)(2,1)S(1)}, u32[]{:S(2)}) %copy-start.14) | copy-done | bytes 262168
  9.5 0.1 collective-permute-start
  9.5 0.0 copy-done.1
  9.5 0.0 copy-done.3
  9.5 3.2 %shard_map.68 = (bf16[4,256,128]{2,1,0:T(8,128)(2,1)S(1)}, bf16[4,256,128]{2,1,0:T(8,128)(2,1)S(1)}, bf16[4,256,128]{2,1,0:T(8,128)(2,1)S(1)}, bf16[4,256,128]{2,1,0:T(8,128)(2,1)S(1)}, f32[4,2,128,128]{3,2,1,0:T(8,128)S(1)}) custom-call(bf16[8,256,128]{2,1,0:T(8,128)(2,1)S(1)} %copy-done.1, bf16[8,256,128]{2,1,0:T(8,128)(2,1)S(1)} %copy-done.3, ...), custom_call_target="tpu_custom_call" | custom-call | flops 67108864 | bytes 1048576 | tf_op jit(solution)/shard_map/pallas_call | solution.py:119
  12.7 0.0 copy-start.8
  12.7 0.0 copy-start.16
  12.8 0.0 collective-permute-done.came
  12.8 0.1 shard_map.69
  12.8 0.6 %copy-done.8 = bf16[4,256,128]{2,1,0:T(8,128)(2,1)} copy-done((bf16[4,256,128]{2,1,0:T(8,128)(2,1)}, bf16[4,256,128]{2,1,0:T(8,128)(2,1)S(1)}, u32[]{:S(2)}) %copy-start.8) | copy-done | bytes 262168
  13.4 0.1 copy-done.10
  13.5 0.1 copy-done.12
  13.6 0.1 copy-done.16
  13.7 2.7 %collective-permute-start.1 = (f32[2,128,128]{2,1,0:T(8,128)S(1)}, f32[2,128,128]{2,1,0:T(8,128)S(1)}, u32[]{:S(2)}, u32[]{:S(2)}) collective-permute-start(f32[2,128,128]{2,1,0:T(8,128)S(1)} %get-tuple-element.41), channel_id=1, source_target_pairs={{0,4},{2,6},{4,0},{6,2},{8,12},{10,14},{12,8},{14,10},{16,20},{18,... | collective-permute-start | bytes 393224 | tf_op jit(solution)/shard_map/ppermute | solution.py:240
  16.3 1.3 %collective-permute-start.2 = (f32[2,128,128]{2,1,0:T(8,128)S(1)}, f32[2,128,128]{2,1,0:T(8,128)S(1)}, u32[]{:S(2)}, u32[]{:S(2)}) collective-permute-start(f32[2,128,128]{2,1,0:T(8,128)S(1)} %get-tuple-element.42), channel_id=1, source_target_pairs={{0,8},{2,10},{4,12},{6,14},{8,0},{10,2},{12,4},{14,6},{16,24},{18,... | collective-permute-start | bytes 393224 | tf_op jit(solution)/shard_map/ppermute | solution.py:240
  17.6 0.1 collective-permute-start.3
  17.7 0.8 %slice_select_fusion.3 = (f32[4,1,128,128]{3,2,1,0:T(8,128)}, f32[4,1,128,128]{3,2,1,0:T(8,128)}) fusion(f32[4,2,128,128]{3,2,1,0:T(8,128)S(1)} %get-tuple-element.35.keep, pred[]{:T(512)S(6)} %eq.3), kind=kLoop, calls=%fused_computation.6 | loop fusion | flops 131072 | bytes 1048577 | tf_op jit(solution)/shard_map/jit(_where)/select_n | solution.py:293
  18.5 0.0 copy-done.9
  18.6 0.1 copy-done.11
  18.7 0.2 copy-done.13
  18.9 0.1 copy-done.15
  19.0 0.9 %copy-done.17 = bf16[4,256,128]{2,1,0:T(8,128)(2,1)S(1)} copy-done((bf16[4,256,128]{2,1,0:T(8,128)(2,1)S(1)}, bf16[4,256,128]{2,1,0:T(8,128)(2,1)}, u32[]{:S(2)}) %copy-start.17) | copy-done | bytes 262168
  20.0 2.0 %shard_map.70 = (f32[4,256,128]{2,1,0:T(8,128)S(1)}, f32[4,256,128]{2,1,0:T(8,128)S(1)}, f32[4,256,128]{2,1,0:T(8,128)S(1)}, f32[4,256,128]{2,1,0:T(8,128)S(1)},...) custom-call(bf16[4,256,128]{2,1,0:T(8,128)(2,1)S(1)} %copy-done.17, bf16[4,256,128]{2,1,0:T(8,128)(2,1)S(1)} %copy-done.9, ...), custom_call_target="tpu_custom_call" | custom-call | flops 805306368 | bytes 5242880 | tf_op jit(solution)/shard_map/pallas_call | solution.py:168
  22.0 0.0 collective-permute-done.1.refs_1_
  22.0 0.0 collective-permute-done.2.refs_2_
  22.0 1.8 %collective-permute-done.3.refs_3_ = f32[2,128,128]{2,1,0:T(8,128)S(1)} collective-permute-done((f32[2,128,128]{2,1,0:T(8,128)S(1)}, f32[2,128,128]{2,1,0:T(8,128)S(1)}, u32[]{:S(2)}, u32[]{:S(2)}) %collective-permute-start.3) | collective-permute-done | bytes 131104 | tf_op jit(solution)/shard_map/ppermute | solution.py:240
  23.8 2.7 %collective-permute-start.4 = (f32[128,128]{1,0:T(8,128)S(1)}, f32[128,128]{1,0:T(8,128)S(1)}, u32[]{:S(2)}, u32[]{:S(2)}) collective-permute-start(f32[128,128]{1,0:T(8,128)S(1)} %fusion), channel_id=1, source_target_pairs={{0,16},{2,18},{4,20},{6,22},{8,24},{10,26},{12,28},{14,30},{16,0},... | collective-permute-start | bytes 196616 | tf_op jit(solution)/shard_map/ppermute | solution.py:240
  26.6 1.6 %collective-permute-done.4 = f32[128,128]{1,0:T(8,128)S(1)} collective-permute-done((f32[128,128]{1,0:T(8,128)S(1)}, f32[128,128]{1,0:T(8,128)S(1)}, u32[]{:S(2)}, u32[]{:S(2)}) %collective-permute-start.4) | collective-permute-done | bytes 65568 | tf_op jit(solution)/shard_map/ppermute | solution.py:240
  28.2 1.4 %collective-permute-start.6 = (f32[2,128,128]{2,1,0:T(8,128)S(1)}, f32[2,128,128]{2,1,0:T(8,128)S(1)}, u32[]{:S(2)}, u32[]{:S(2)}) collective-permute-start(f32[2,128,128]{2,1,0:T(8,128)S(1)} %pad_maximum_fusion.2), channel_id=1, source_target_pairs={{0,8},{2,10},{4,12},{6,14},{8,0},{10,2},{12,4},{14,6},{16,24},{18,... | collective-permute-start | bytes 393224 | tf_op jit(solution)/shard_map/ppermute | solution.py:240
  29.7 1.2 %collective-permute-start.5 = (f32[2,128,128]{2,1,0:T(8,128)S(1)}, f32[2,128,128]{2,1,0:T(8,128)S(1)}, u32[]{:S(2)}, u32[]{:S(2)}) collective-permute-start(f32[2,128,128]{2,1,0:T(8,128)S(1)} %pad_maximum_fusion.1), channel_id=1, source_target_pairs={{0,4},{2,6},{4,0},{6,2},{8,12},{10,14},{12,8},{14,10},{16,20},{18,... | collective-permute-start | bytes 393224 | tf_op jit(solution)/shard_map/ppermute | solution.py:240
  30.9 0.2 collective-permute-start.7
  31.2 0.0 copy-start.18
  31.3 0.9 %collective-permute-done.6 = f32[2,128,128]{2,1,0:T(8,128)S(1)} collective-permute-done((f32[2,128,128]{2,1,0:T(8,128)S(1)}, f32[2,128,128]{2,1,0:T(8,128)S(1)}, u32[]{:S(2)}, u32[]{:S(2)}) %collective-permute-start.6) | collective-permute-done | bytes 131104 | tf_op jit(solution)/shard_map/ppermute | solution.py:240
  32.1 1.8 %collective-permute-done.5 = f32[2,128,128]{2,1,0:T(8,128)S(1)} collective-permute-done((f32[2,128,128]{2,1,0:T(8,128)S(1)}, f32[2,128,128]{2,1,0:T(8,128)S(1)}, u32[]{:S(2)}, u32[]{:S(2)}) %collective-permute-start.5) | collective-permute-done | bytes 131104 | tf_op jit(solution)/shard_map/ppermute | solution.py:240
  33.9 3.2 %collective-permute-done.7 = f32[2,128,128]{2,1,0:T(8,128)S(1)} collective-permute-done((f32[2,128,128]{2,1,0:T(8,128)S(1)}, f32[2,128,128]{2,1,0:T(8,128)S(1)}, u32[]{:S(2)}, u32[]{:S(2)}) %collective-permute-start.7) | collective-permute-done | bytes 131104 | tf_op jit(solution)/shard_map/ppermute | solution.py:240
  37.1 0.0 copy-done.19
  37.1 0.1 maximum_add_fusion.1
  37.2 2.6 %collective-permute-start.8 = (f32[4,2,128,128]{3,2,1,0:T(8,128)S(1)}, f32[4,2,128,128]{3,2,1,0:T(8,128)S(1)}, u32[]{:S(2)}, u32[]{:S(2)}) collective-permute-start(f32[4,2,128,128]{3,2,1,0:T(8,128)S(1)} %get-tuple-element.50), channel_id=1, source_target_pairs={{0,2},{2,0},{4,6},{6,4},{8,10},{10,8},{12,14},{14,12},{16,18},{18,... | collective-permute-start | bytes 1572872 | tf_op jit(solution)/shard_map/ppermute | solution.py:240
  39.8 1.2 %shard_map.72 = (bf16[8,256,128]{2,1,0:T(8,128)(2,1)}, bf16[8,256,128]{2,1,0:T(8,128)(2,1)}, bf16[8,256,128]{2,1,0:T(8,128)(2,1)}) custom-call(bf16[4,256,128]{2,1,0:T(8,128)(2,1)S(1)} %copy-done.9, bf16[4,256,128]{2,1,0:T(8,128)(2,1)S(1)} %copy-done.11, bf16[4,256,128]{2,1,0:T(8,128)(2,1)S(1)} %copy-done.13, f32[4,256,128]{2,1,0:T(8,128)S(1)} %get-tuple-element.40.after.lq, ...), custom_call_target="tpu_custom_call" | custom-call | flops 100663296 | bytes 786432 | tf_op jit(solution)/shard_map/pallas_call | solution.py:221
  41.0 0.4 collective-permute-done.8.state
  41.3 1.2 %shard_map.73 = (bf16[8,256,128]{2,1,0:T(8,128)(2,1)}, bf16[8,256,128]{2,1,0:T(8,128)(2,1)}, bf16[8,256,128]{2,1,0:T(8,128)(2,1)}) custom-call(bf16[4,256,128]{2,1,0:T(8,128)(2,1)S(1)} %get-tuple-element.26.kb.k, bf16[4,256,128]{2,1,0:T(8,128)(2,1)S(1)} %get-tuple-element.27.vb.v, ...), custom_call_target="tpu_custom_call", output_to_operand_aliasing={{0}: (7, {}), {1}: (8, {}), {2}: (9, {})} | custom-call | flops 100663296 | bytes 786432 | tf_op jit(solution)/shard_map/pallas_call | solution.py:221
  (29 shorter events, 0.3 us)
Async XLA Ops:
  0.6 1.0 %copy-start = (bf16[8,256,128]{2,1,0:T(8,128)(2,1)S(1)}, bf16[8,256,128]{2,1,0:T(8,128)(2,1)}, u32[]{:S(2)}) copy-start(bf16[8,256,128]{2,1,0:T(8,128)(2,1)} %q.3) | copy-start | bytes 1572868
  1.7 1.0 %copy-start.2 = (bf16[8,256,128]{2,1,0:T(8,128)(2,1)S(1)}, bf16[8,256,128]{2,1,0:T(8,128)(2,1)}, u32[]{:S(2)}) copy-start(bf16[8,256,128]{2,1,0:T(8,128)(2,1)} %k.3) | copy-start | bytes 1572868
  2.7 1.0 %copy-start.4 = (bf16[8,256,128]{2,1,0:T(8,128)(2,1)S(1)}, bf16[8,256,128]{2,1,0:T(8,128)(2,1)}, u32[]{:S(2)}) copy-start(bf16[8,256,128]{2,1,0:T(8,128)(2,1)} %v.3) | copy-start | bytes 1572868
  3.8 1.0 %copy-start.6 = (bf16[8,256,128]{2,1,0:T(8,128)(2,1)S(1)}, bf16[8,256,128]{2,1,0:T(8,128)(2,1)}, u32[]{:S(2)}) copy-start(bf16[8,256,128]{2,1,0:T(8,128)(2,1)} %g.3) | copy-start | bytes 1572868
  4.8 4.7 %copy-start.1 = (bf16[8,256,128]{2,1,0:T(8,128)(2,1)S(1)}, bf16[8,256,128]{2,1,0:T(8,128)(2,1)}, u32[]{:S(2)}) copy-start(bf16[8,256,128]{2,1,0:T(8,128)(2,1)} %q.3) | copy-start | bytes 1572868
  4.8 4.7 %copy-start.3 = (bf16[8,256,128]{2,1,0:T(8,128)(2,1)S(1)}, bf16[8,256,128]{2,1,0:T(8,128)(2,1)}, u32[]{:S(2)}) copy-start(bf16[8,256,128]{2,1,0:T(8,128)(2,1)} %k.3) | copy-start | bytes 1572868
  4.8 4.7 %copy-start.5 = (bf16[8,256,128]{2,1,0:T(8,128)(2,1)S(1)}, bf16[8,256,128]{2,1,0:T(8,128)(2,1)}, u32[]{:S(2)}) copy-start(bf16[8,256,128]{2,1,0:T(8,128)(2,1)} %v.3) | copy-start | bytes 1572868
  4.8 4.7 %copy-start.7 = (bf16[8,256,128]{2,1,0:T(8,128)(2,1)S(1)}, bf16[8,256,128]{2,1,0:T(8,128)(2,1)}, u32[]{:S(2)}) copy-start(bf16[8,256,128]{2,1,0:T(8,128)(2,1)} %g.3) | copy-start | bytes 1572868
  8.8 0.7 %copy-start.14 = (bf16[4,256,128]{2,1,0:T(8,128)(2,1)}, bf16[4,256,128]{2,1,0:T(8,128)(2,1)S(1)}, u32[]{:S(2)}) copy-start(bf16[4,256,128]{2,1,0:T(8,128)(2,1)S(1)} %get-tuple-element.33.qb) | copy-start | bytes 786436
  9.5 3.3 %collective-permute-start = (f32[4,2,128,128]{3,2,1,0:T(8,128)}, f32[4,2,128,128]{3,2,1,0:T(8,128)S(1)}, u32[]{:S(2)}, u32[]{:S(2)}) collective-permute-start(f32[4,2,128,128]{3,2,1,0:T(8,128)} %get-tuple-element.34), channel_id=1, source_target_pairs={{0,2},{2,0},{4,6},{6,4},{8,10},{10,8},{12,14},{14,12},{16,18},{18,... | collective-permute-start | bytes 1572872 | tf_op jit(solution)/shard_map/ppermute | solution.py:240
  12.7 0.7 %copy-start.8 = (bf16[4,256,128]{2,1,0:T(8,128)(2,1)}, bf16[4,256,128]{2,1,0:T(8,128)(2,1)S(1)}, u32[]{:S(2)}) copy-start(bf16[4,256,128]{2,1,0:T(8,128)(2,1)S(1)} %get-tuple-element.30.ka.k) | copy-start | bytes 786436
  12.7 0.8 %copy-start.10 = (bf16[4,256,128]{2,1,0:T(8,128)(2,1)}, bf16[4,256,128]{2,1,0:T(8,128)(2,1)S(1)}, u32[]{:S(2)}) copy-start(bf16[4,256,128]{2,1,0:T(8,128)(2,1)S(1)} %get-tuple-element.31.va.v) | copy-start | bytes 786436
  12.7 0.9 %copy-start.12 = (bf16[4,256,128]{2,1,0:T(8,128)(2,1)}, bf16[4,256,128]{2,1,0:T(8,128)(2,1)S(1)}, u32[]{:S(2)}) copy-start(bf16[4,256,128]{2,1,0:T(8,128)(2,1)S(1)} %get-tuple-element.32.ga.g) | copy-start | bytes 786436
  12.7 0.9 %copy-start.16 = (bf16[4,256,128]{2,1,0:T(8,128)(2,1)}, bf16[4,256,128]{2,1,0:T(8,128)(2,1)S(1)}, u32[]{:S(2)}) copy-start(bf16[4,256,128]{2,1,0:T(8,128)(2,1)S(1)} %get-tuple-element.29.qa) | copy-start | bytes 786436
  13.7 8.3 %collective-permute-start.1 = (f32[2,128,128]{2,1,0:T(8,128)S(1)}, f32[2,128,128]{2,1,0:T(8,128)S(1)}, u32[]{:S(2)}, u32[]{:S(2)}) collective-permute-start(f32[2,128,128]{2,1,0:T(8,128)S(1)} %get-tuple-element.41), channel_id=1, source_target_pairs={{0,4},{2,6},{4,0},{6,2},{8,12},{10,14},{12,8},{14,10},{16,20},{18,... | collective-permute-start | bytes 393224 | tf_op jit(solution)/shard_map/ppermute | solution.py:240
  16.3 5.7 %collective-permute-start.2 = (f32[2,128,128]{2,1,0:T(8,128)S(1)}, f32[2,128,128]{2,1,0:T(8,128)S(1)}, u32[]{:S(2)}, u32[]{:S(2)}) collective-permute-start(f32[2,128,128]{2,1,0:T(8,128)S(1)} %get-tuple-element.42), channel_id=1, source_target_pairs={{0,8},{2,10},{4,12},{6,14},{8,0},{10,2},{12,4},{14,6},{16,24},{18,... | collective-permute-start | bytes 393224 | tf_op jit(solution)/shard_map/ppermute | solution.py:240
  17.6 0.9 %copy-start.9 = (bf16[4,256,128]{2,1,0:T(8,128)(2,1)S(1)}, bf16[4,256,128]{2,1,0:T(8,128)(2,1)}, u32[]{:S(2)}) copy-start(bf16[4,256,128]{2,1,0:T(8,128)(2,1)} %copy-done.8) | copy-start | bytes 786436
  17.6 1.1 %copy-start.11 = (bf16[4,256,128]{2,1,0:T(8,128)(2,1)S(1)}, bf16[4,256,128]{2,1,0:T(8,128)(2,1)}, u32[]{:S(2)}) copy-start(bf16[4,256,128]{2,1,0:T(8,128)(2,1)} %copy-done.10) | copy-start | bytes 786436
  17.6 1.3 %copy-start.13 = (bf16[4,256,128]{2,1,0:T(8,128)(2,1)S(1)}, bf16[4,256,128]{2,1,0:T(8,128)(2,1)}, u32[]{:S(2)}) copy-start(bf16[4,256,128]{2,1,0:T(8,128)(2,1)} %copy-done.12) | copy-start | bytes 786436
  17.6 1.4 %copy-start.15 = (bf16[4,256,128]{2,1,0:T(8,128)(2,1)S(1)}, bf16[4,256,128]{2,1,0:T(8,128)(2,1)}, u32[]{:S(2)}) copy-start(bf16[4,256,128]{2,1,0:T(8,128)(2,1)} %copy-done.14) | copy-start | bytes 786436
  17.6 6.1 %collective-permute-start.3 = (f32[2,128,128]{2,1,0:T(8,128)S(1)}, f32[2,128,128]{2,1,0:T(8,128)S(1)}, u32[]{:S(2)}, u32[]{:S(2)}) collective-permute-start(f32[2,128,128]{2,1,0:T(8,128)S(1)} %get-tuple-element.43), channel_id=1, source_target_pairs={{0,12},{2,14},{4,8},{6,10},{8,4},{10,6},{12,0},{14,2},{16,28},{18,... | collective-permute-start | bytes 393224 | tf_op jit(solution)/shard_map/ppermute | solution.py:240
  19.0 0.9 %copy-start.17 = (bf16[4,256,128]{2,1,0:T(8,128)(2,1)S(1)}, bf16[4,256,128]{2,1,0:T(8,128)(2,1)}, u32[]{:S(2)}) copy-start(bf16[4,256,128]{2,1,0:T(8,128)(2,1)} %copy-done.16) | copy-start | bytes 786436
  23.8 4.4 %collective-permute-start.4 = (f32[128,128]{1,0:T(8,128)S(1)}, f32[128,128]{1,0:T(8,128)S(1)}, u32[]{:S(2)}, u32[]{:S(2)}) collective-permute-start(f32[128,128]{1,0:T(8,128)S(1)} %fusion), channel_id=1, source_target_pairs={{0,16},{2,18},{4,20},{6,22},{8,24},{10,26},{12,28},{14,30},{16,0},... | collective-permute-start | bytes 196616 | tf_op jit(solution)/shard_map/ppermute | solution.py:240
  28.2 3.9 %collective-permute-start.6 = (f32[2,128,128]{2,1,0:T(8,128)S(1)}, f32[2,128,128]{2,1,0:T(8,128)S(1)}, u32[]{:S(2)}, u32[]{:S(2)}) collective-permute-start(f32[2,128,128]{2,1,0:T(8,128)S(1)} %pad_maximum_fusion.2), channel_id=1, source_target_pairs={{0,8},{2,10},{4,12},{6,14},{8,0},{10,2},{12,4},{14,6},{16,24},{18,... | collective-permute-start | bytes 393224 | tf_op jit(solution)/shard_map/ppermute | solution.py:240
  29.7 4.2 %collective-permute-start.5 = (f32[2,128,128]{2,1,0:T(8,128)S(1)}, f32[2,128,128]{2,1,0:T(8,128)S(1)}, u32[]{:S(2)}, u32[]{:S(2)}) collective-permute-start(f32[2,128,128]{2,1,0:T(8,128)S(1)} %pad_maximum_fusion.1), channel_id=1, source_target_pairs={{0,4},{2,6},{4,0},{6,2},{8,12},{10,14},{12,8},{14,10},{16,20},{18,... | collective-permute-start | bytes 393224 | tf_op jit(solution)/shard_map/ppermute | solution.py:240
  30.9 6.1 %collective-permute-start.7 = (f32[2,128,128]{2,1,0:T(8,128)S(1)}, f32[2,128,128]{2,1,0:T(8,128)S(1)}, u32[]{:S(2)}, u32[]{:S(2)}) collective-permute-start(f32[2,128,128]{2,1,0:T(8,128)S(1)} %pad_maximum_fusion.3), channel_id=1, source_target_pairs={{0,12},{2,14},{4,8},{6,10},{8,4},{10,6},{12,0},{14,2},{16,28},{18,... | collective-permute-start | bytes 393224 | tf_op jit(solution)/shard_map/ppermute | solution.py:240
  31.2 5.9 %copy-start.19 = (f32[4,1,128,128]{3,2,1,0:T(8,128)S(1)}, f32[4,1,128,128]{3,2,1,0:T(8,128)}, u32[]{:S(2)}) copy-start(f32[4,1,128,128]{3,2,1,0:T(8,128)} %get-tuple-element.54) | copy-start | bytes 786436
  31.2 5.9 %copy-start.18 = (f32[4,1,128,128]{3,2,1,0:T(8,128)S(1)}, f32[4,1,128,128]{3,2,1,0:T(8,128)}, u32[]{:S(2)}) copy-start(f32[4,1,128,128]{3,2,1,0:T(8,128)} %get-tuple-element.53) | copy-start | bytes 786436
  37.2 4.1 %collective-permute-start.8 = (f32[4,2,128,128]{3,2,1,0:T(8,128)S(1)}, f32[4,2,128,128]{3,2,1,0:T(8,128)S(1)}, u32[]{:S(2)}, u32[]{:S(2)}) collective-permute-start(f32[4,2,128,128]{3,2,1,0:T(8,128)S(1)} %get-tuple-element.50), channel_id=1, source_target_pairs={{0,2},{2,0},{4,6},{6,4},{8,10},{10,8},{12,14},{14,12},{16,18},{18,... | collective-permute-start | bytes 1572872 | tf_op jit(solution)/shard_map/ppermute | solution.py:240

commit v3 on v2

--- a/solution.py
+++ b/solution.py
@@ -78,11 +78,16 @@
 
 WHOLE = pl.BlockSpec(memory_space=pltpu.VMEM)
 PLACED = pl.BlockSpec(memory_space=pl.ANY)
+FAR = pl.BlockSpec(memory_space=pltpu.HBM)
 ROOM = pltpu.CompilerParams(vmem_limit_bytes=16 * 2**20)
 
 
 def near(x):
     return pltpu.with_memory_space_constraint(x, pltpu.VMEM)
+
+
+def far(x):
+    return pltpu.with_memory_space_constraint(x, pltpu.HBM)
 
 
 def dot(a, b, da, db):
@@ -100,8 +105,8 @@
     for i in range(slots):
         head = head_of(slots, i, other)
         row = []
-        for n, (far, close) in enumerate(((k, ks), (v, vs), (q, qs), (g, gs))):
-            row.append(pltpu.make_async_copy(far.at[head], close.at[i], sems.at[i, n]))
+        for n, (there, here) in enumerate(((k, ks), (v, vs), (q, qs), (g, gs))):
+            row.append(pltpu.make_async_copy(there.at[head], here.at[i], sems.at[i, n]))
             row[-1].start()
         copies.append(row)
     for i in range(slots):
@@ -119,7 +124,7 @@
     return pl.pallas_call(
         functools.partial(state_kernel, slots=slots, other=other),
         out_shape=[rows] * 4 + [pltpu.VMEM((slots, 2, width, width), F32)],
-        in_specs=[PLACED] * 4,
+        in_specs=[FAR] * 4,
         out_specs=[WHOLE] * 5,
         scratch_shapes=[pltpu.SemaphoreType.DMA((slots, 4))],
         compiler_params=ROOM,
@@ -128,7 +133,7 @@
             bytes_accessed=slots * 8 * tokens * width,
             transcendentals=0,
         ),
-    )(*data)
+    )(*[far(x) for x in data])
 
 
 def total_kernel(came, keep, *outs):
@@ -208,8 +213,8 @@
         bq[i] = (lq[i] + dot(g[i], earlier, 1, 1)).astype(BF16)
         bk[i] = (lk[i] + dot(v[i], later, 1, 1)).astype(BF16)
         bv[i] = (lv[i] + dot(k[i], later, 1, 0)).astype(BF16)
-        for n, (close, far) in enumerate(((bq, gq), (bk, gk), (bv, gv))):
-            copies.append(pltpu.make_async_copy(close.at[i], far.at[head], sems.at[i, n]))
+        for n, (here, there) in enumerate(((bq, gq), (bk, gk), (bv, gv))):
+            copies.append(pltpu.make_async_copy(here.at[i], there.at[head], sems.at[i, n]))
             copies[-1].start()
     for copy in copies:
         copy.wait()

time: 43.2 us -> 35.6 us (0.82)
  local copies, waits for them, and re-layouts: 7.15 us -> 0.01 us
  Pallas kernels: 11.5 us -> 9.75 us
  waiting for transfers between devices: 9.57 us -> 11.1 us
    unnamed x40 -> x4, local copies, waits for them, and re-layouts: 7.15 us -> 0.01 us
    pallas_call x2, Pallas kernels: 7.1 us -> 5.32 us  [states_of(): pl.pallas_call(functools.partial(state_kernel, slots=slots, other=other),...]
    ppermute x9, waiting for transfers between devices: 9.57 us -> 11.1 us  [swap(): return lax.ppermute(x, 'seq', [(i, i ^ mask) for i in range(count)])]
  transfers between devices with their start and end apart: 9 -> 9, of which waited for: 6 -> 7; matrix products, arithmetic and copies ran while one was open for 2% -> 3% of each run, Pallas kernels for 15% -> 17%
where the time goes in v3:
time: 35.6 us; the launch traced here: 35.1 us
  starting transfers between devices  12.3 us (35%)
  waiting for transfers between devices  11.1 us (31%)
  Pallas kernels  9.75 us (27%)
  other arithmetic  1.17 us (3%)
  between operations  0.77 us (2%)
    ppermute x9, starting transfers between devices, swap(): return lax.ppermute(x, 'seq', [(i, i ^ mask) for i in range(count)])  12.3 us
    ppermute x9, waiting for transfers between devices, swap(): return lax.ppermute(x, 'seq', [(i, i ^ mask) for i in range(count)])  11.1 us
    pallas_call x2, Pallas kernels, states_of(): pl.pallas_call(functools.partial(state_kernel, slots=slots, other=other),...  5.32 us
    pallas_call x2, Pallas kernels, final_sums(): pl.pallas_call(functools.partial(final_kernel, other=other), out_shape=[j...  2.33 us
    pallas_call x1, Pallas kernels, local_parts(): pl.pallas_call(local_kernel, out_shape=[pltpu.VMEM(own[0].shape, F32)] *...  2.02 us
    select_n x1, other arithmetic, body(): jnp.where(first, keep[:, 0], 0.0)  0.83 us
  transfers between devices with their start and end apart: 9, of which 7 were waited for; matrix products, arithmetic and copies ran while one was open for 3% of the time, Pallas kernels for 17%

profile of v3, /device:TPU:1, one launch (start us, length us, event | category | flops | bytes accessed | tf_op | source)
XLA Modules:
  0.0 35.1 jit_solution(13091261214629570172)
XLA Ops:
  0.6 2.7 %shard_map.67 = (bf16[4,256,128]{2,1,0:T(8,128)(2,1)S(1)}, bf16[4,256,128]{2,1,0:T(8,128)(2,1)S(1)}, bf16[4,256,128]{2,1,0:T(8,128)(2,1)S(1)}, bf16[4,256,128]{2,1,0:T(8,128)(2,1)S(1)}, f32[4,2,128,128]{3,2,1,0:T(8,128)S(1)}) custom-call(bf16[8,256,128]{2,1,0:T(8,128)(2,1)} %q.3, bf16[8,256,128]{2,1,0:T(8,128)(2,1)} %k.3, bf16[8,256,128]{2,1,0:T(8,128)(2,1)} %v.3, ...), custom_call_target="tpu_custom_call" | custom-call | flops 67108864 | bytes 1048576 | tf_op jit(solution)/shard_map/pallas_call | solution.py:124
  3.3 0.1 collective-permute-start
  3.4 2.6 %shard_map.68 = (bf16[4,256,128]{2,1,0:T(8,128)(2,1)S(1)}, bf16[4,256,128]{2,1,0:T(8,128)(2,1)S(1)}, bf16[4,256,128]{2,1,0:T(8,128)(2,1)S(1)}, bf16[4,256,128]{2,1,0:T(8,128)(2,1)S(1)}, f32[4,2,128,128]{3,2,1,0:T(8,128)S(1)}) custom-call(bf16[8,256,128]{2,1,0:T(8,128)(2,1)} %q.3, bf16[8,256,128]{2,1,0:T(8,128)(2,1)} %k.3, bf16[8,256,128]{2,1,0:T(8,128)(2,1)} %v.3, ...), custom_call_target="tpu_custom_call" | custom-call | flops 67108864 | bytes 1048576 | tf_op jit(solution)/shard_map/pallas_call | solution.py:124
  6.1 0.0 collective-permute-done.came
  6.1 0.1 shard_map.69
  6.2 2.7 %collective-permute-start.1 = (f32[2,128,128]{2,1,0:T(8,128)S(1)}, f32[2,128,128]{2,1,0:T(8,128)S(1)}, u32[]{:S(2)}, u32[]{:S(2)}) collective-permute-start(f32[2,128,128]{2,1,0:T(8,128)S(1)} %get-tuple-element.41), channel_id=1, source_target_pairs={{0,4},{2,6},{4,0},{6,2},{8,12},{10,14},{12,8},{14,10},{16,20},{18,... | collective-permute-start | bytes 393224 | tf_op jit(solution)/shard_map/ppermute | solution.py:245
  8.9 1.3 %collective-permute-start.2 = (f32[2,128,128]{2,1,0:T(8,128)S(1)}, f32[2,128,128]{2,1,0:T(8,128)S(1)}, u32[]{:S(2)}, u32[]{:S(2)}) collective-permute-start(f32[2,128,128]{2,1,0:T(8,128)S(1)} %get-tuple-element.42), channel_id=1, source_target_pairs={{0,8},{2,10},{4,12},{6,14},{8,0},{10,2},{12,4},{14,6},{16,24},{18,... | collective-permute-start | bytes 393224 | tf_op jit(solution)/shard_map/ppermute | solution.py:245
  10.2 0.0 collective-permute-start.3
  10.2 0.8 %slice_select_fusion.3 = (f32[4,1,128,128]{3,2,1,0:T(8,128)}, f32[4,1,128,128]{3,2,1,0:T(8,128)}) fusion(f32[4,2,128,128]{3,2,1,0:T(8,128)S(1)} %get-tuple-element.35.keep, pred[]{:T(512)S(6)} %eq.3), kind=kLoop, calls=%fused_computation.6 | loop fusion | flops 131072 | bytes 1048577 | tf_op jit(solution)/shard_map/jit(_where)/select_n | solution.py:298
  11.0 2.0 %shard_map.70 = (f32[4,256,128]{2,1,0:T(8,128)S(1)}, f32[4,256,128]{2,1,0:T(8,128)S(1)}, f32[4,256,128]{2,1,0:T(8,128)S(1)}, f32[4,256,128]{2,1,0:T(8,128)S(1)},...) custom-call(bf16[4,256,128]{2,1,0:T(8,128)(2,1)S(1)} %get-tuple-element.29.qa, ...), custom_call_target="tpu_custom_call" | custom-call | flops 805306368 | bytes 5242880 | tf_op jit(solution)/shard_map/pallas_call | solution.py:173
  13.0 0.0 collective-permute-done.1.refs_1_
  13.0 0.6 %collective-permute-done.2.refs_2_ = f32[2,128,128]{2,1,0:T(8,128)S(1)} collective-permute-done((f32[2,128,128]{2,1,0:T(8,128)S(1)}, f32[2,128,128]{2,1,0:T(8,128)S(1)}, u32[]{:S(2)}, u32[]{:S(2)}) %collective-permute-start.2) | collective-permute-done | bytes 131104 | tf_op jit(solution)/shard_map/ppermute | solution.py:245
  13.7 2.7 %collective-permute-done.3.refs_3_ = f32[2,128,128]{2,1,0:T(8,128)S(1)} collective-permute-done((f32[2,128,128]{2,1,0:T(8,128)S(1)}, f32[2,128,128]{2,1,0:T(8,128)S(1)}, u32[]{:S(2)}, u32[]{:S(2)}) %collective-permute-start.3) | collective-permute-done | bytes 131104 | tf_op jit(solution)/shard_map/ppermute | solution.py:245
  16.4 2.7 %collective-permute-start.4 = (f32[128,128]{1,0:T(8,128)S(1)}, f32[128,128]{1,0:T(8,128)S(1)}, u32[]{:S(2)}, u32[]{:S(2)}) collective-permute-start(f32[128,128]{1,0:T(8,128)S(1)} %fusion), channel_id=1, source_target_pairs={{0,16},{2,18},{4,20},{6,22},{8,24},{10,26},{12,28},{14,30},{16,0},... | collective-permute-start | bytes 196616 | tf_op jit(solution)/shard_map/ppermute | solution.py:245
  19.1 1.6 %collective-permute-done.4 = f32[128,128]{1,0:T(8,128)S(1)} collective-permute-done((f32[128,128]{1,0:T(8,128)S(1)}, f32[128,128]{1,0:T(8,128)S(1)}, u32[]{:S(2)}, u32[]{:S(2)}) %collective-permute-start.4) | collective-permute-done | bytes 65568 | tf_op jit(solution)/shard_map/ppermute | solution.py:245
  20.8 1.4 %collective-permute-start.6 = (f32[2,128,128]{2,1,0:T(8,128)S(1)}, f32[2,128,128]{2,1,0:T(8,128)S(1)}, u32[]{:S(2)}, u32[]{:S(2)}) collective-permute-start(f32[2,128,128]{2,1,0:T(8,128)S(1)} %pad_maximum_fusion.2), channel_id=1, source_target_pairs={{0,8},{2,10},{4,12},{6,14},{8,0},{10,2},{12,4},{14,6},{16,24},{18,... | collective-permute-start | bytes 393224 | tf_op jit(solution)/shard_map/ppermute | solution.py:245
  22.2 1.2 %collective-permute-start.5 = (f32[2,128,128]{2,1,0:T(8,128)S(1)}, f32[2,128,128]{2,1,0:T(8,128)S(1)}, u32[]{:S(2)}, u32[]{:S(2)}) collective-permute-start(f32[2,128,128]{2,1,0:T(8,128)S(1)} %pad_maximum_fusion.1), channel_id=1, source_target_pairs={{0,4},{2,6},{4,0},{6,2},{8,12},{10,14},{12,8},{14,10},{16,20},{18,... | collective-permute-start | bytes 393224 | tf_op jit(solution)/shard_map/ppermute | solution.py:245
  23.5 0.3 collective-permute-start.7
  23.8 0.0 copy-start.1
  23.8 0.0 copy-start
  23.8 0.9 %collective-permute-done.6 = f32[2,128,128]{2,1,0:T(8,128)S(1)} collective-permute-done((f32[2,128,128]{2,1,0:T(8,128)S(1)}, f32[2,128,128]{2,1,0:T(8,128)S(1)}, u32[]{:S(2)}, u32[]{:S(2)}) %collective-permute-start.6) | collective-permute-done | bytes 131104 | tf_op jit(solution)/shard_map/ppermute | solution.py:245
  24.7 1.7 %collective-permute-done.5 = f32[2,128,128]{2,1,0:T(8,128)S(1)} collective-permute-done((f32[2,128,128]{2,1,0:T(8,128)S(1)}, f32[2,128,128]{2,1,0:T(8,128)S(1)}, u32[]{:S(2)}, u32[]{:S(2)}) %collective-permute-start.5) | collective-permute-done | bytes 131104 | tf_op jit(solution)/shard_map/ppermute | solution.py:245
  26.4 3.2 %collective-permute-done.7 = f32[2,128,128]{2,1,0:T(8,128)S(1)} collective-permute-done((f32[2,128,128]{2,1,0:T(8,128)S(1)}, f32[2,128,128]{2,1,0:T(8,128)S(1)}, u32[]{:S(2)}, u32[]{:S(2)}) %collective-permute-start.7) | collective-permute-done | bytes 131104 | tf_op jit(solution)/shard_map/ppermute | solution.py:245
  29.6 0.0 copy-done.1
  29.6 0.0 copy-done
  29.6 0.1 maximum_add_fusion.1
  29.7 2.6 %collective-permute-start.8 = (f32[4,2,128,128]{3,2,1,0:T(8,128)S(1)}, f32[4,2,128,128]{3,2,1,0:T(8,128)S(1)}, u32[]{:S(2)}, u32[]{:S(2)}) collective-permute-start(f32[4,2,128,128]{3,2,1,0:T(8,128)S(1)} %get-tuple-element.50), channel_id=1, source_target_pairs={{0,2},{2,0},{4,6},{6,4},{8,10},{10,8},{12,14},{14,12},{16,18},{18,... | collective-permute-start | bytes 1572872 | tf_op jit(solution)/shard_map/ppermute | solution.py:245
  32.3 1.2 %shard_map.72 = (bf16[8,256,128]{2,1,0:T(8,128)(2,1)}, bf16[8,256,128]{2,1,0:T(8,128)(2,1)}, bf16[8,256,128]{2,1,0:T(8,128)(2,1)}) custom-call(bf16[4,256,128]{2,1,0:T(8,128)(2,1)S(1)} %get-tuple-element.30.ka.k, bf16[4,256,128]{2,1,0:T(8,128)(2,1)S(1)} %get-tuple-element.31.va.v, bf16[4,256,128]{2,1,0:T(8,128)(2,1)S(1)} %get-tuple-element.32.ga.g, ...), custom_call_target="tpu_custom_call" | custom-call | flops 100663296 | bytes 786432 | tf_op jit(solution)/shard_map/pallas_call | solution.py:226
  33.5 0.4 %collective-permute-done.8.state = f32[4,2,128,128]{3,2,1,0:T(8,128)S(1)} collective-permute-done((f32[4,2,128,128]{3,2,1,0:T(8,128)S(1)}, f32[4,2,128,128]{3,2,1,0:T(8,128)S(1)}, u32[]{:S(2)}, u32[]{:S(2)}) %collective-permute-start.8) | collective-permute-done | bytes 524320 | tf_op jit(solution)/shard_map/ppermute | solution.py:245
  33.9 1.2 %shard_map.73 = (bf16[8,256,128]{2,1,0:T(8,128)(2,1)}, bf16[8,256,128]{2,1,0:T(8,128)(2,1)}, bf16[8,256,128]{2,1,0:T(8,128)(2,1)}) custom-call(bf16[4,256,128]{2,1,0:T(8,128)(2,1)S(1)} %get-tuple-element.26.kb.k, bf16[4,256,128]{2,1,0:T(8,128)(2,1)S(1)} %get-tuple-element.27.vb.v, ...), custom_call_target="tpu_custom_call", output_to_operand_aliasing={{0}: (7, {}), {1}: (8, {}), {2}: (9, {})} | custom-call | flops 100663296 | bytes 786432 | tf_op jit(solution)/shard_map/pallas_call | solution.py:226
  (11 shorter events, 0.3 us)
Async XLA Ops:
  3.3 2.8 %collective-permute-start = (f32[4,2,128,128]{3,2,1,0:T(8,128)S(1)}, f32[4,2,128,128]{3,2,1,0:T(8,128)S(1)}, u32[]{:S(2)}, u32[]{:S(2)}) collective-permute-start(f32[4,2,128,128]{3,2,1,0:T(8,128)S(1)} %get-tuple-element.34), channel_id=1, source_target_pairs={{0,2},{2,0},{4,6},{6,4},{8,10},{10,8},{12,14},{14,12},{16,18},{18,... | collective-permute-start | bytes 1572872 | tf_op jit(solution)/shard_map/ppermute | solution.py:245
  6.2 6.9 %collective-permute-start.1 = (f32[2,128,128]{2,1,0:T(8,128)S(1)}, f32[2,128,128]{2,1,0:T(8,128)S(1)}, u32[]{:S(2)}, u32[]{:S(2)}) collective-permute-start(f32[2,128,128]{2,1,0:T(8,128)S(1)} %get-tuple-element.41), channel_id=1, source_target_pairs={{0,4},{2,6},{4,0},{6,2},{8,12},{10,14},{12,8},{14,10},{16,20},{18,... | collective-permute-start | bytes 393224 | tf_op jit(solution)/shard_map/ppermute | solution.py:245
  8.9 4.8 %collective-permute-start.2 = (f32[2,128,128]{2,1,0:T(8,128)S(1)}, f32[2,128,128]{2,1,0:T(8,128)S(1)}, u32[]{:S(2)}, u32[]{:S(2)}) collective-permute-start(f32[2,128,128]{2,1,0:T(8,128)S(1)} %get-tuple-element.42), channel_id=1, source_target_pairs={{0,8},{2,10},{4,12},{6,14},{8,0},{10,2},{12,4},{14,6},{16,24},{18,... | collective-permute-start | bytes 393224 | tf_op jit(solution)/shard_map/ppermute | solution.py:245
  10.2 6.2 %collective-permute-start.3 = (f32[2,128,128]{2,1,0:T(8,128)S(1)}, f32[2,128,128]{2,1,0:T(8,128)S(1)}, u32[]{:S(2)}, u32[]{:S(2)}) collective-permute-start(f32[2,128,128]{2,1,0:T(8,128)S(1)} %get-tuple-element.43), channel_id=1, source_target_pairs={{0,12},{2,14},{4,8},{6,10},{8,4},{10,6},{12,0},{14,2},{16,28},{18,... | collective-permute-start | bytes 393224 | tf_op jit(solution)/shard_map/ppermute | solution.py:245
  16.4 4.3 %collective-permute-start.4 = (f32[128,128]{1,0:T(8,128)S(1)}, f32[128,128]{1,0:T(8,128)S(1)}, u32[]{:S(2)}, u32[]{:S(2)}) collective-permute-start(f32[128,128]{1,0:T(8,128)S(1)} %fusion), channel_id=1, source_target_pairs={{0,16},{2,18},{4,20},{6,22},{8,24},{10,26},{12,28},{14,30},{16,0},... | collective-permute-start | bytes 196616 | tf_op jit(solution)/shard_map/ppermute | solution.py:245
  20.8 3.9 %collective-permute-start.6 = (f32[2,128,128]{2,1,0:T(8,128)S(1)}, f32[2,128,128]{2,1,0:T(8,128)S(1)}, u32[]{:S(2)}, u32[]{:S(2)}) collective-permute-start(f32[2,128,128]{2,1,0:T(8,128)S(1)} %pad_maximum_fusion.2), channel_id=1, source_target_pairs={{0,8},{2,10},{4,12},{6,14},{8,0},{10,2},{12,4},{14,6},{16,24},{18,... | collective-permute-start | bytes 393224 | tf_op jit(solution)/shard_map/ppermute | solution.py:245
  22.2 4.2 %collective-permute-start.5 = (f32[2,128,128]{2,1,0:T(8,128)S(1)}, f32[2,128,128]{2,1,0:T(8,128)S(1)}, u32[]{:S(2)}, u32[]{:S(2)}) collective-permute-start(f32[2,128,128]{2,1,0:T(8,128)S(1)} %pad_maximum_fusion.1), channel_id=1, source_target_pairs={{0,4},{2,6},{4,0},{6,2},{8,12},{10,14},{12,8},{14,10},{16,20},{18,... | collective-permute-start | bytes 393224 | tf_op jit(solution)/shard_map/ppermute | solution.py:245
  23.5 6.1 %collective-permute-start.7 = (f32[2,128,128]{2,1,0:T(8,128)S(1)}, f32[2,128,128]{2,1,0:T(8,128)S(1)}, u32[]{:S(2)}, u32[]{:S(2)}) collective-permute-start(f32[2,128,128]{2,1,0:T(8,128)S(1)} %pad_maximum_fusion.3), channel_id=1, source_target_pairs={{0,12},{2,14},{4,8},{6,10},{8,4},{10,6},{12,0},{14,2},{16,28},{18,... | collective-permute-start | bytes 393224 | tf_op jit(solution)/shard_map/ppermute | solution.py:245
  23.8 5.9 %copy-start.1 = (f32[4,1,128,128]{3,2,1,0:T(8,128)S(1)}, f32[4,1,128,128]{3,2,1,0:T(8,128)}, u32[]{:S(2)}) copy-start(f32[4,1,128,128]{3,2,1,0:T(8,128)} %get-tuple-element.54) | copy-start | bytes 786436
  23.8 5.8 %copy-start = (f32[4,1,128,128]{3,2,1,0:T(8,128)S(1)}, f32[4,1,128,128]{3,2,1,0:T(8,128)}, u32[]{:S(2)}) copy-start(f32[4,1,128,128]{3,2,1,0:T(8,128)} %get-tuple-element.53) | copy-start | bytes 786436
  29.7 4.2 %collective-permute-start.8 = (f32[4,2,128,128]{3,2,1,0:T(8,128)S(1)}, f32[4,2,128,128]{3,2,1,0:T(8,128)S(1)}, u32[]{:S(2)}, u32[]{:S(2)}) collective-permute-start(f32[4,2,128,128]{3,2,1,0:T(8,128)S(1)} %get-tuple-element.50), channel_id=1, source_target_pairs={{0,2},{2,0},{4,6},{6,4},{8,10},{10,8},{12,14},{14,12},{16,18},{18,... | collective-permute-start | bytes 1572872 | tf_op jit(solution)/shard_map/ppermute | solution.py:245

commit v4 on v3

--- a/solution.py
+++ b/solution.py
@@ -94,46 +94,63 @@
     return lax.dot_general(a, b, (((da,), (db,)), ((), ())), preferred_element_type=F32)
 
 
-def head_of(slots, slot, other):
+def place_of(slots):
     index = lax.axis_index("seq")
-    core = 1 - (index & 1) if other else index & 1
-    return core * slots + (((index >> 1) & (slots - 1)) ^ slot)
-
-
-def state_kernel(q, k, v, g, qs, ks, vs, gs, out, sems, *, slots, other):
+    return index & 1, (index >> 1) & (slots - 1)
+
+
+def away_kernel(q, k, v, g, out, qs, ks, vs, gs, sems):
+    slots = out.shape[0]
+    core, rank = place_of(slots)
+    first = (1 - core) * slots
     copies = []
+    for n, (there, here) in enumerate(((k, ks), (v, vs), (q, qs), (g, gs))):
+        copies.append(pltpu.make_async_copy(there.at[pl.ds(first, slots)], here, sems.at[n]))
+        copies[-1].start()
+    copies[0].wait()
+    copies[1].wait()
     for i in range(slots):
-        head = head_of(slots, i, other)
-        row = []
-        for n, (there, here) in enumerate(((k, ks), (v, vs), (q, qs), (g, gs))):
-            row.append(pltpu.make_async_copy(there.at[head], here.at[i], sems.at[i, n]))
-            row[-1].start()
-        copies.append(row)
+        out[i, 0] = dot(ks[rank ^ i], vs[rank ^ i], 0, 0)
+    copies[2].wait()
+    copies[3].wait()
     for i in range(slots):
-        copies[i][0].wait()
-        copies[i][1].wait()
-        out[i, 0] = dot(ks[i], vs[i], 0, 0)
-        copies[i][2].wait()
-        copies[i][3].wait()
-        out[i, 1] = dot(qs[i], gs[i], 0, 0)
-
-
-def states_of(data, slots, other):
+        out[i, 1] = dot(qs[rank ^ i], gs[rank ^ i], 0, 0)
+
+
+def keep_kernel(q, k, v, g, out):
+    slots = out.shape[0]
+    core, rank = place_of(slots)
+    for i in range(slots):
+        head = core * slots + (rank ^ i)
+        out[i, 0] = dot(k[head], v[head], 0, 0)
+        out[i, 1] = dot(q[head], g[head], 0, 0)
+
+
+def state_call(kernel, data, slots, place, spec, scratch):
     _, tokens, width = data[0].shape
-    rows = pltpu.VMEM((slots, tokens, width), BF16)
-    return pl.pallas_call(
-        functools.partial(state_kernel, slots=slots, other=other),
-        out_shape=[rows] * 4 + [pltpu.VMEM((slots, 2, width, width), F32)],
-        in_specs=[FAR] * 4,
-        out_specs=[WHOLE] * 5,
-        scratch_shapes=[pltpu.SemaphoreType.DMA((slots, 4))],
+    return pl.pallas_call(
+        kernel,
+        out_shape=pltpu.VMEM((slots, 2, width, width), F32),
+        in_specs=[spec] * 4,
+        out_specs=WHOLE,
+        scratch_shapes=scratch,
         compiler_params=ROOM,
         cost_estimate=pl.CostEstimate(
             flops=slots * 4 * tokens * width * width,
             bytes_accessed=slots * 8 * tokens * width,
             transcendentals=0,
         ),
-    )(*[far(x) for x in data])
+    )(*[place(x) for x in data])
+
+
+def away_states(data, slots):
+    _, tokens, width = data[0].shape
+    scratch = [pltpu.VMEM((slots, tokens, width), BF16)] * 4 + [pltpu.SemaphoreType.DMA((4,))]
+    return state_call(away_kernel, data, slots, far, FAR, scratch)
+
+
+def keep_states(data, slots):
+    return state_call(keep_kernel, data, slots, near, WHOLE, [])
 
 
 def total_kernel(came, keep, *outs):
@@ -152,37 +169,34 @@
     )(near(came), near(keep))
 
 
-def local_kernel(qa, ka, va, ga, qb, kb, vb, gb, after, *outs):
-    slots, tokens, _ = qa.shape
+def local_kernel(qs, ks, vs, gs, after, gq, gk, gv):
+    heads, tokens, _ = qs.shape
     row = lax.broadcasted_iota(jnp.int32, (tokens, tokens), 0)
     col = lax.broadcasted_iota(jnp.int32, (tokens, tokens), 1)
-    for half, (qs, ks, vs, gs) in enumerate(((qa, ka, va, ga), (qb, kb, vb, gb))):
-        gq, gk, gv = outs[3 * half : 3 * half + 3]
-        for i in range(slots):
-            q, k, v, g = qs[i], ks[i], vs[i], gs[i]
-            score = jnp.where(row >= col, dot(g, v, 1, 1), 0.0).astype(BF16)
-            gq[i] = dot(score, k, 1, 0)
-            score = jnp.where(row <= col, dot(v, g, 1, 1), 0.0).astype(BF16)
-            gk[i] = dot(score, q, 1, 0)
-            score = jnp.where(row <= col, dot(k, q, 1, 1), 0.0).astype(BF16)
-            gv[i] = dot(score, g, 1, 0)
-
-
-def local_parts(own, other, after):
-    slots, tokens, width = own[0].shape
-    out = pl.pallas_call(
+    for i in range(heads):
+        q, k, v, g = qs[i], ks[i], vs[i], gs[i]
+        score = jnp.where(row >= col, dot(g, v, 1, 1), 0.0).astype(BF16)
+        gq[i] = dot(score, k, 1, 0)
+        score = jnp.where(row <= col, dot(v, g, 1, 1), 0.0).astype(BF16)
+        gk[i] = dot(score, q, 1, 0)
+        score = jnp.where(row <= col, dot(k, q, 1, 1), 0.0).astype(BF16)
+        gv[i] = dot(score, g, 1, 0)
+
+
+def local_parts(data, after):
+    heads, tokens, width = data[0].shape
+    return pl.pallas_call(
         local_kernel,
-        out_shape=[pltpu.VMEM(own[0].shape, F32)] * 6,
-        in_specs=[WHOLE] * 8 + [PLACED],
-        out_specs=[WHOLE] * 6,
+        out_shape=[pltpu.VMEM(data[0].shape, F32)] * 3,
+        in_specs=[WHOLE] * 4 + [PLACED],
+        out_specs=[WHOLE] * 3,
         compiler_params=ROOM,
         cost_estimate=pl.CostEstimate(
-            flops=slots * 24 * tokens * tokens * width,
-            bytes_accessed=slots * 40 * tokens * width,
+            flops=heads * 12 * tokens * tokens * width,
+            bytes_accessed=heads * 20 * tokens * width,
             transcendentals=0,
         ),
-    )(*[near(x) for x in own], *[near(x) for x in other], near(after))
-    return out[:3], out[3:]
+    )(*[near(x) for x in data], near(after))
 
 
 def block_kernel(after, *refs):
@@ -205,14 +219,16 @@
 
 def final_kernel(k, v, g, lq, lk, lv, state, *refs, other):
     gq, gk, gv, bq, bk, bv, sems = refs[-7:]
-    slots = k.shape[0]
+    slots = state.shape[0]
+    core, rank = place_of(slots)
+    first = (1 - core if other else core) * slots
     copies = []
     for i in range(slots):
         earlier, later = state[i, 0].astype(BF16), state[i, 1].astype(BF16)
-        head = head_of(slots, i, other)
-        bq[i] = (lq[i] + dot(g[i], earlier, 1, 1)).astype(BF16)
-        bk[i] = (lk[i] + dot(v[i], later, 1, 1)).astype(BF16)
-        bv[i] = (lv[i] + dot(k[i], later, 1, 0)).astype(BF16)
+        head = first + (rank ^ i)
+        bq[i] = (lq[head] + dot(g[head], earlier, 1, 1)).astype(BF16)
+        bk[i] = (lk[head] + dot(v[head], later, 1, 1)).astype(BF16)
+        bv[i] = (lv[head] + dot(k[head], later, 1, 0)).astype(BF16)
         for n, (here, there) in enumerate(((bq, gq), (bk, gk), (bv, gv))):
             copies.append(pltpu.make_async_copy(here.at[i], there.at[head], sems.at[i, n]))
             copies[-1].start()
@@ -220,16 +236,16 @@
         copy.wait()
 
 
-def final_sums(rows, parts, state, heads, other, filled=()):
-    _, k, v, g = rows
-    slots, tokens, width = k.shape
+def final_sums(data, parts, state, other, filled=()):
+    _, tokens, width = data[0].shape
+    slots = state.shape[0]
     return pl.pallas_call(
         functools.partial(final_kernel, other=other),
-        out_shape=[jax.ShapeDtypeStruct((heads, tokens, width), BF16)] * 3,
+        out_shape=[jax.ShapeDtypeStruct(data[0].shape, BF16)] * 3,
         in_specs=[WHOLE] * 7 + [PLACED] * len(filled),
         out_specs=[PLACED] * 3,
         input_output_aliases={7 + n: n for n in range(len(filled))},
-        scratch_shapes=[pltpu.VMEM(k.shape, BF16)] * 3
+        scratch_shapes=[pltpu.VMEM((slots, tokens, width), BF16)] * 3
         + [pltpu.SemaphoreType.DMA((slots, 3))],
         compiler_params=ROOM,
         cost_estimate=pl.CostEstimate(
@@ -237,7 +253,7 @@
             bytes_accessed=slots * 6 * tokens * width,
             transcendentals=0,
         ),
-    )(*[near(x) for x in (k, v, g, *parts, state)], *filled)
+    )(*[near(x) for x in (*data[1:], *parts, state)], *filled)
 
 
 def swap(x, mask):
@@ -253,15 +269,14 @@
         rank = (index >> 1) & (group - 1)
         data = (queries, key_rows, value_rows, grad_out)
 
-        *away_rows, away = states_of(data, slots, True)
-        came = swap(away, 1)
-        *keep_rows, keep = states_of(data, slots, False)
+        came = swap(away_states(data, slots), 1)
+        keep = keep_states(data, slots)
         total = totals_of(came, keep)
 
         held = [total[0]] + [swap(total[j], 2 * j) for j in range(1, group)]
-        own_parts, other_parts = local_parts(keep_rows, away_rows, total[0])
-
-        block = block_sum(held, own_parts[0])
+        parts = local_parts(data, total[0])
+
+        block = block_sum(held, parts[0])
         keys, rests = block[0], block[1]
         carry = jnp.zeros_like(block)
         bit = 2 * group
@@ -298,10 +313,8 @@
             [jnp.where(first, keep[:, 0], 0.0), jnp.where(first, 0.0, keep[:, 1])], 1
         )
         other = swap(theirs, 1)
-        done = final_sums(keep_rows, own_parts, mine, queries.shape[0], False)
-        return tuple(
-            final_sums(away_rows, other_parts, other, queries.shape[0], True, done)
-        )
+        done = final_sums(data, parts, mine, False)
+        return tuple(final_sums(data, parts, other, True, done))
 
     return body
 

time: 35.6 us -> 33.5 us (0.941)
  Pallas kernels: 9.75 us -> 6.56 us
  waiting for transfers between devices: 11.1 us -> 11.9 us
    pallas_call x3, Pallas kernels: 7.34 us -> 4.14 us  [the longest x2 2.12 us: state_call(): pl.pallas_call(kernel, out_shape=pltpu.VMEM((slots, 2, width, width), F32...]
    ppermute x9, waiting for transfers between devices: 11.1 us -> 11.9 us  [swap(): return lax.ppermute(x, 'seq', [(i, i ^ mask) for i in range(count)])]
    ppermute x9, starting transfers between devices: 12.3 us -> 12.6 us  [swap(): return lax.ppermute(x, 'seq', [(i, i ^ mask) for i in range(count)])]
  transfers between devices with their start and end apart: 9 -> 9, of which waited for: 7 -> 8; matrix products, arithmetic and copies ran while one was open for 3% -> 3% of each run, Pallas kernels for 17% -> 11%
where the time goes in v4:
time: 33.5 us; the launch traced here: 33.1 us
  starting transfers between devices  12.6 us (38%)
  waiting for transfers between devices  11.9 us (36%)
  Pallas kernels  6.56 us (20%)
  other arithmetic  1.16 us (3%)
  between operations  0.8 us (2%)
    ppermute x9, starting transfers between devices, swap(): return lax.ppermute(x, 'seq', [(i, i ^ mask) for i in range(count)])  12.6 us
    ppermute x9, waiting for transfers between devices, swap(): return lax.ppermute(x, 'seq', [(i, i ^ mask) for i in range(count)])  11.9 us
    pallas_call x2, Pallas kernels, final_sums(): pl.pallas_call(functools.partial(final_kernel, other=other), out_shape=[j...  2.34 us
    pallas_call x2, Pallas kernels, state_call(): pl.pallas_call(kernel, out_shape=pltpu.VMEM((slots, 2, width, width), F32...  2.12 us
    pallas_call x1, Pallas kernels, local_parts(): pl.pallas_call(local_kernel, out_shape=[pltpu.VMEM(data[0].shape, F32)] *...  2.02 us
    select_n x1, other arithmetic, body(): jnp.where(first, keep[:, 0], 0.0)  0.83 us
  transfers between devices with their start and end apart: 9, of which 8 were waited for; matrix products, arithmetic and copies ran while one was open for 3% of the time, Pallas kernels for 11%

profile of v4, /device:TPU:1, one launch (start us, length us, event | category | flops | bytes accessed | tf_op | source)
XLA Modules:
  0.0 33.1 jit_solution(16949942372580351271)
XLA Ops:
  0.6 0.0 copy-start.2
  0.6 0.0 copy-start.1
  0.7 0.0 copy-start
  0.7 0.0 copy-start.3
  0.7 1.8 %shard_map.67 = f32[4,2,128,128]{3,2,1,0:T(8,128)S(1)} custom-call(bf16[8,256,128]{2,1,0:T(8,128)(2,1)} %qs.1, bf16[8,256,128]{2,1,0:T(8,128)(2,1)} %k.7, bf16[8,256,128]{2,1,0:T(8,128)(2,1)} %v.7, bf16[8,256,128]{2,1,0:T(8,128)(2,1)} %g.7), custom_call_target="tpu_custom_call" | custom-call | flops 67108864 | bytes 1048576 | tf_op jit(solution)/shard_map/pallas_call | solution.py:131
  2.4 0.1 collective-permute-start
  2.6 0.0 copy-done.2
  2.6 0.0 copy-done.1
  2.6 0.0 copy-done
  2.6 0.0 copy-done.3
  2.6 0.4 %shard_map.68.keep = f32[4,2,128,128]{3,2,1,0:T(8,128)S(1)} custom-call(bf16[8,256,128]{2,1,0:T(8,128)(2,1)S(1)} %copy-done.3, bf16[8,256,128]{2,1,0:T(8,128)(2,1)S(1)} %copy-done, bf16[8,256,128]{2,1,0:T(8,128)(2,1)S(1)} %copy-done.1, bf16[8,256,128]{2,1,0:T(8,128)(2,1)S(1)} %copy-done.2), custom_call_target="tpu_custom_call" | custom-call | flops 67108864 | bytes 1048576 | tf_op jit(solution)/shard_map/pallas_call | solution.py:131
  2.9 1.5 %collective-permute-done.came = f32[4,2,128,128]{3,2,1,0:T(8,128)S(1)} collective-permute-done((f32[4,2,128,128]{3,2,1,0:T(8,128)S(1)}, f32[4,2,128,128]{3,2,1,0:T(8,128)S(1)}, u32[]{:S(2)}, u32[]{:S(2)}) %collective-permute-start) | collective-permute-done | bytes 524320 | tf_op jit(solution)/shard_map/ppermute | solution.py:261
  4.4 0.1 shard_map.69
  4.5 2.4 %collective-permute-start.1 = (f32[2,128,128]{2,1,0:T(8,128)S(1)}, f32[2,128,128]{2,1,0:T(8,128)S(1)}, u32[]{:S(2)}, u32[]{:S(2)}) collective-permute-start(f32[2,128,128]{2,1,0:T(8,128)S(1)} %get-tuple-element.17), channel_id=1, source_target_pairs={{0,4},{2,6},{4,0},{6,2},{8,12},{10,14},{12,8},{14,10},{16,20},{18,... | collective-permute-start | bytes 393224 | tf_op jit(solution)/shard_map/ppermute | solution.py:261
  6.9 1.3 %collective-permute-start.2 = (f32[2,128,128]{2,1,0:T(8,128)S(1)}, f32[2,128,128]{2,1,0:T(8,128)S(1)}, u32[]{:S(2)}, u32[]{:S(2)}) collective-permute-start(f32[2,128,128]{2,1,0:T(8,128)S(1)} %get-tuple-element.18), channel_id=1, source_target_pairs={{0,8},{2,10},{4,12},{6,14},{8,0},{10,2},{12,4},{14,6},{16,24},{18,... | collective-permute-start | bytes 393224 | tf_op jit(solution)/shard_map/ppermute | solution.py:261
  8.2 0.0 collective-permute-start.3
  8.2 0.8 %slice_select_fusion.3 = (f32[4,1,128,128]{3,2,1,0:T(8,128)}, f32[4,1,128,128]{3,2,1,0:T(8,128)}) fusion(f32[4,2,128,128]{3,2,1,0:T(8,128)S(1)} %shard_map.68.keep, pred[]{:T(512)S(6)} %eq.3), kind=kLoop, calls=%fused_computation.6 | loop fusion | flops 131072 | bytes 1048577 | tf_op jit(solution)/shard_map/jit(_where)/select_n | solution.py:313
  9.0 2.0 %shard_map.70 = (f32[8,256,128]{2,1,0:T(8,128)S(1)}, f32[8,256,128]{2,1,0:T(8,128)S(1)}, f32[8,256,128]{2,1,0:T(8,128)S(1)}) custom-call(bf16[8,256,128]{2,1,0:T(8,128)(2,1)S(1)} %copy-done.3, bf16[8,256,128]{2,1,0:T(8,128)(2,1)S(1)} %copy-done, bf16[8,256,128]{2,1,0:T(8,128)(2,1)S(1)} %copy-done.1, bf16[8,256,128]{2,1,0:T(8,128)(2,1)S(1)} %copy-done.2, ...), custom_call_target="tpu_custom_call" | custom-call | flops 805306368 | bytes 5242880 | tf_op jit(solution)/shard_map/pallas_call | solution.py:188
  11.0 0.0 collective-permute-done.1.refs_1_
  11.0 0.2 collective-permute-done.2.refs_2_
  11.3 2.7 %collective-permute-done.3.refs_3_ = f32[2,128,128]{2,1,0:T(8,128)S(1)} collective-permute-done((f32[2,128,128]{2,1,0:T(8,128)S(1)}, f32[2,128,128]{2,1,0:T(8,128)S(1)}, u32[]{:S(2)}, u32[]{:S(2)}) %collective-permute-start.3) | collective-permute-done | bytes 131104 | tf_op jit(solution)/shard_map/ppermute | solution.py:261
  14.0 2.7 %collective-permute-start.4 = (f32[128,128]{1,0:T(8,128)S(1)}, f32[128,128]{1,0:T(8,128)S(1)}, u32[]{:S(2)}, u32[]{:S(2)}) collective-permute-start(f32[128,128]{1,0:T(8,128)S(1)} %fusion), channel_id=1, source_target_pairs={{0,16},{2,18},{4,20},{6,22},{8,24},{10,26},{12,28},{14,30},{16,0},... | collective-permute-start | bytes 196616 | tf_op jit(solution)/shard_map/ppermute | solution.py:261
  16.8 1.6 %collective-permute-done.4 = f32[128,128]{1,0:T(8,128)S(1)} collective-permute-done((f32[128,128]{1,0:T(8,128)S(1)}, f32[128,128]{1,0:T(8,128)S(1)}, u32[]{:S(2)}, u32[]{:S(2)}) %collective-permute-start.4) | collective-permute-done | bytes 65568 | tf_op jit(solution)/shard_map/ppermute | solution.py:261
  18.5 1.4 %collective-permute-start.6 = (f32[2,128,128]{2,1,0:T(8,128)S(1)}, f32[2,128,128]{2,1,0:T(8,128)S(1)}, u32[]{:S(2)}, u32[]{:S(2)}) collective-permute-start(f32[2,128,128]{2,1,0:T(8,128)S(1)} %pad_maximum_fusion.2), channel_id=1, source_target_pairs={{0,8},{2,10},{4,12},{6,14},{8,0},{10,2},{12,4},{14,6},{16,24},{18,... | collective-permute-start | bytes 393224 | tf_op jit(solution)/shard_map/ppermute | solution.py:261
  19.9 1.2 %collective-permute-start.5 = (f32[2,128,128]{2,1,0:T(8,128)S(1)}, f32[2,128,128]{2,1,0:T(8,128)S(1)}, u32[]{:S(2)}, u32[]{:S(2)}) collective-permute-start(f32[2,128,128]{2,1,0:T(8,128)S(1)} %pad_maximum_fusion.1), channel_id=1, source_target_pairs={{0,4},{2,6},{4,0},{6,2},{8,12},{10,14},{12,8},{14,10},{16,20},{18,... | collective-permute-start | bytes 393224 | tf_op jit(solution)/shard_map/ppermute | solution.py:261
  21.1 0.3 collective-permute-start.7
  21.4 0.0 copy-start.5
  21.5 0.0 copy-start.4
  21.5 0.9 %collective-permute-done.6 = f32[2,128,128]{2,1,0:T(8,128)S(1)} collective-permute-done((f32[2,128,128]{2,1,0:T(8,128)S(1)}, f32[2,128,128]{2,1,0:T(8,128)S(1)}, u32[]{:S(2)}, u32[]{:S(2)}) %collective-permute-start.6) | collective-permute-done | bytes 131104 | tf_op jit(solution)/shard_map/ppermute | solution.py:261
  22.3 1.7 %collective-permute-done.5 = f32[2,128,128]{2,1,0:T(8,128)S(1)} collective-permute-done((f32[2,128,128]{2,1,0:T(8,128)S(1)}, f32[2,128,128]{2,1,0:T(8,128)S(1)}, u32[]{:S(2)}, u32[]{:S(2)}) %collective-permute-start.5) | collective-permute-done | bytes 131104 | tf_op jit(solution)/shard_map/ppermute | solution.py:261
  24.0 2.9 %collective-permute-done.7 = f32[2,128,128]{2,1,0:T(8,128)S(1)} collective-permute-done((f32[2,128,128]{2,1,0:T(8,128)S(1)}, f32[2,128,128]{2,1,0:T(8,128)S(1)}, u32[]{:S(2)}, u32[]{:S(2)}) %collective-permute-start.7) | collective-permute-done | bytes 131104 | tf_op jit(solution)/shard_map/ppermute | solution.py:261
  27.0 0.0 copy-done.5
  27.0 0.0 copy-done.4
  27.0 0.1 maximum_add_fusion.1
  27.1 3.3 %collective-permute-start.8 = (f32[4,2,128,128]{3,2,1,0:T(8,128)S(1)}, f32[4,2,128,128]{3,2,1,0:T(8,128)S(1)}, u32[]{:S(2)}, u32[]{:S(2)}) collective-permute-start(f32[4,2,128,128]{3,2,1,0:T(8,128)S(1)} %get-tuple-element.24), channel_id=1, source_target_pairs={{0,2},{2,0},{4,6},{6,4},{8,10},{10,8},{12,14},{14,12},{16,18},{18,... | collective-permute-start | bytes 1572872 | tf_op jit(solution)/shard_map/ppermute | solution.py:261
  30.3 1.2 %shard_map.72 = (bf16[8,256,128]{2,1,0:T(8,128)(2,1)}, bf16[8,256,128]{2,1,0:T(8,128)(2,1)}, bf16[8,256,128]{2,1,0:T(8,128)(2,1)}) custom-call(bf16[8,256,128]{2,1,0:T(8,128)(2,1)S(1)} %copy-done, bf16[8,256,128]{2,1,0:T(8,128)(2,1)S(1)} %copy-done.1, bf16[8,256,128]{2,1,0:T(8,128)(2,1)S(1)} %copy-done.2, f32[8,256,128]{2,1,0:T(8,128)S(1)} %get-tuple-element.14.after.lq, ...), custom_call_target="tpu_custom_call" | custom-call | flops 100663296 | bytes 786432 | tf_op jit(solution)/shard_map/pallas_call | solution.py:242
  31.5 0.4 %collective-permute-done.8.state = f32[4,2,128,128]{3,2,1,0:T(8,128)S(1)} collective-permute-done((f32[4,2,128,128]{3,2,1,0:T(8,128)S(1)}, f32[4,2,128,128]{3,2,1,0:T(8,128)S(1)}, u32[]{:S(2)}, u32[]{:S(2)}) %collective-permute-start.8) | collective-permute-done | bytes 524320 | tf_op jit(solution)/shard_map/ppermute | solution.py:261
  31.9 1.2 %shard_map.73 = (bf16[8,256,128]{2,1,0:T(8,128)(2,1)}, bf16[8,256,128]{2,1,0:T(8,128)(2,1)}, bf16[8,256,128]{2,1,0:T(8,128)(2,1)}) custom-call(bf16[8,256,128]{2,1,0:T(8,128)(2,1)S(1)} %copy-done, bf16[8,256,128]{2,1,0:T(8,128)(2,1)S(1)} %copy-done.1, bf16[8,256,128]{2,1,0:T(8,128)(2,1)S(1)} %copy-done.2, ...), custom_call_target="tpu_custom_call", output_to_operand_aliasing={{0}: (7, {}), {1}: (8, {}), {2}: (9, {})} | custom-call | flops 100663296 | bytes 786432 | tf_op jit(solution)/shard_map/pallas_call | solution.py:242
  (11 shorter events, 0.3 us)
Async XLA Ops:
  0.6 1.9 %copy-start.2 = (bf16[8,256,128]{2,1,0:T(8,128)(2,1)S(1)}, bf16[8,256,128]{2,1,0:T(8,128)(2,1)}, u32[]{:S(2)}) copy-start(bf16[8,256,128]{2,1,0:T(8,128)(2,1)} %g.7) | copy-start | bytes 1572868
  0.6 1.9 %copy-start.1 = (bf16[8,256,128]{2,1,0:T(8,128)(2,1)S(1)}, bf16[8,256,128]{2,1,0:T(8,128)(2,1)}, u32[]{:S(2)}) copy-start(bf16[8,256,128]{2,1,0:T(8,128)(2,1)} %v.7) | copy-start | bytes 1572868
  0.7 1.9 %copy-start = (bf16[8,256,128]{2,1,0:T(8,128)(2,1)S(1)}, bf16[8,256,128]{2,1,0:T(8,128)(2,1)}, u32[]{:S(2)}) copy-start(bf16[8,256,128]{2,1,0:T(8,128)(2,1)} %k.7) | copy-start | bytes 1572868
  0.7 1.9 %copy-start.3 = (bf16[8,256,128]{2,1,0:T(8,128)(2,1)S(1)}, bf16[8,256,128]{2,1,0:T(8,128)(2,1)}, u32[]{:S(2)}) copy-start(bf16[8,256,128]{2,1,0:T(8,128)(2,1)} %qs.1) | copy-start | bytes 1572868
  2.4 2.0 %collective-permute-start = (f32[4,2,128,128]{3,2,1,0:T(8,128)S(1)}, f32[4,2,128,128]{3,2,1,0:T(8,128)S(1)}, u32[]{:S(2)}, u32[]{:S(2)}) collective-permute-start(f32[4,2,128,128]{3,2,1,0:T(8,128)S(1)} %shard_map.67), channel_id=1, source_target_pairs={{0,2},{2,0},{4,6},{6,4},{8,10},{10,8},{12,14},{14,12},{16,18},{18,... | collective-permute-start | bytes 1572872 | tf_op jit(solution)/shard_map/ppermute | solution.py:261
  4.5 6.6 %collective-permute-start.1 = (f32[2,128,128]{2,1,0:T(8,128)S(1)}, f32[2,128,128]{2,1,0:T(8,128)S(1)}, u32[]{:S(2)}, u32[]{:S(2)}) collective-permute-start(f32[2,128,128]{2,1,0:T(8,128)S(1)} %get-tuple-element.17), channel_id=1, source_target_pairs={{0,4},{2,6},{4,0},{6,2},{8,12},{10,14},{12,8},{14,10},{16,20},{18,... | collective-permute-start | bytes 393224 | tf_op jit(solution)/shard_map/ppermute | solution.py:261
  6.9 4.4 %collective-permute-start.2 = (f32[2,128,128]{2,1,0:T(8,128)S(1)}, f32[2,128,128]{2,1,0:T(8,128)S(1)}, u32[]{:S(2)}, u32[]{:S(2)}) collective-permute-start(f32[2,128,128]{2,1,0:T(8,128)S(1)} %get-tuple-element.18), channel_id=1, source_target_pairs={{0,8},{2,10},{4,12},{6,14},{8,0},{10,2},{12,4},{14,6},{16,24},{18,... | collective-permute-start | bytes 393224 | tf_op jit(solution)/shard_map/ppermute | solution.py:261
  8.2 5.8 %collective-permute-start.3 = (f32[2,128,128]{2,1,0:T(8,128)S(1)}, f32[2,128,128]{2,1,0:T(8,128)S(1)}, u32[]{:S(2)}, u32[]{:S(2)}) collective-permute-start(f32[2,128,128]{2,1,0:T(8,128)S(1)} %get-tuple-element.19), channel_id=1, source_target_pairs={{0,12},{2,14},{4,8},{6,10},{8,4},{10,6},{12,0},{14,2},{16,28},{18,... | collective-permute-start | bytes 393224 | tf_op jit(solution)/shard_map/ppermute | solution.py:261
  14.0 4.4 %collective-permute-start.4 = (f32[128,128]{1,0:T(8,128)S(1)}, f32[128,128]{1,0:T(8,128)S(1)}, u32[]{:S(2)}, u32[]{:S(2)}) collective-permute-start(f32[128,128]{1,0:T(8,128)S(1)} %fusion), channel_id=1, source_target_pairs={{0,16},{2,18},{4,20},{6,22},{8,24},{10,26},{12,28},{14,30},{16,0},... | collective-permute-start | bytes 196616 | tf_op jit(solution)/shard_map/ppermute | solution.py:261
  18.5 3.9 %collective-permute-start.6 = (f32[2,128,128]{2,1,0:T(8,128)S(1)}, f32[2,128,128]{2,1,0:T(8,128)S(1)}, u32[]{:S(2)}, u32[]{:S(2)}) collective-permute-start(f32[2,128,128]{2,1,0:T(8,128)S(1)} %pad_maximum_fusion.2), channel_id=1, source_target_pairs={{0,8},{2,10},{4,12},{6,14},{8,0},{10,2},{12,4},{14,6},{16,24},{18,... | collective-permute-start | bytes 393224 | tf_op jit(solution)/shard_map/ppermute | solution.py:261
  19.9 4.2 %collective-permute-start.5 = (f32[2,128,128]{2,1,0:T(8,128)S(1)}, f32[2,128,128]{2,1,0:T(8,128)S(1)}, u32[]{:S(2)}, u32[]{:S(2)}) collective-permute-start(f32[2,128,128]{2,1,0:T(8,128)S(1)} %pad_maximum_fusion.1), channel_id=1, source_target_pairs={{0,4},{2,6},{4,0},{6,2},{8,12},{10,14},{12,8},{14,10},{16,20},{18,... | collective-permute-start | bytes 393224 | tf_op jit(solution)/shard_map/ppermute | solution.py:261
  21.1 5.9 %collective-permute-start.7 = (f32[2,128,128]{2,1,0:T(8,128)S(1)}, f32[2,128,128]{2,1,0:T(8,128)S(1)}, u32[]{:S(2)}, u32[]{:S(2)}) collective-permute-start(f32[2,128,128]{2,1,0:T(8,128)S(1)} %pad_maximum_fusion.3), channel_id=1, source_target_pairs={{0,12},{2,14},{4,8},{6,10},{8,4},{10,6},{12,0},{14,2},{16,28},{18,... | collective-permute-start | bytes 393224 | tf_op jit(solution)/shard_map/ppermute | solution.py:261
  21.4 5.5 %copy-start.5 = (f32[4,1,128,128]{3,2,1,0:T(8,128)S(1)}, f32[4,1,128,128]{3,2,1,0:T(8,128)}, u32[]{:S(2)}) copy-start(f32[4,1,128,128]{3,2,1,0:T(8,128)} %get-tuple-element.28) | copy-start | bytes 786436
  21.5 5.5 %copy-start.4 = (f32[4,1,128,128]{3,2,1,0:T(8,128)S(1)}, f32[4,1,128,128]{3,2,1,0:T(8,128)}, u32[]{:S(2)}) copy-start(f32[4,1,128,128]{3,2,1,0:T(8,128)} %get-tuple-element.27) | copy-start | bytes 786436
  27.1 4.8 %collective-permute-start.8 = (f32[4,2,128,128]{3,2,1,0:T(8,128)S(1)}, f32[4,2,128,128]{3,2,1,0:T(8,128)S(1)}, u32[]{:S(2)}, u32[]{:S(2)}) collective-permute-start(f32[4,2,128,128]{3,2,1,0:T(8,128)S(1)} %get-tuple-element.24), channel_id=1, source_target_pairs={{0,2},{2,0},{4,6},{6,4},{8,10},{10,8},{12,14},{14,12},{16,18},{18,... | collective-permute-start | bytes 1572872 | tf_op jit(solution)/shard_map/ppermute | solution.py:261

commit v5 on v4

--- a/solution.py
+++ b/solution.py
@@ -153,20 +153,71 @@
     return state_call(keep_kernel, data, slots, near, WHOLE, [])
 
 
-def total_kernel(came, keep, *outs):
-    for i, out in enumerate(outs):
+def total_kernel(came, keep, *refs):
+    *totals, inner, outer = refs
+    core, _ = place_of(len(totals))
+    for i, out in enumerate(totals):
         out[...] = came[i] + keep[i]
+        inner[i] = jnp.where(core == 0, came[i, 1], came[i, 0])
+        outer[i] = jnp.where(core == 0, keep[i, 0], keep[i, 1])
 
 
 def totals_of(came, keep):
     slots, _, width, _ = keep.shape
     return pl.pallas_call(
         total_kernel,
-        out_shape=[pltpu.VMEM((2, width, width), F32)] * slots,
+        out_shape=[pltpu.VMEM((2, width, width), F32)] * slots
+        + [pltpu.VMEM((slots, width, width), F32)] * 2,
         in_specs=[WHOLE] * 2,
-        out_specs=[WHOLE] * slots,
+        out_specs=[WHOLE] * (slots + 2),
         compiler_params=ROOM,
     )(near(came), near(keep))
+
+
+def outside_kernel(carry, *refs, slot, group):
+    out = refs[-1]
+    _, rank = place_of(group)
+    earlier, later = carry[0], carry[1]
+    for i in range(group):
+        if i != slot:
+            before = (rank ^ i) < (rank ^ slot)
+            earlier = earlier + jnp.where(before, refs[i][0], 0.0)
+            later = later + jnp.where(before, 0.0, refs[i][1])
+    out[0] = earlier
+    out[1] = later
+
+
+def outside_of(carry, held, slot):
+    return pl.pallas_call(
+        functools.partial(outside_kernel, slot=slot, group=len(held)),
+        out_shape=pltpu.VMEM(carry.shape, F32),
+        in_specs=[WHOLE] * (1 + len(held)),
+        out_specs=WHOLE,
+        compiler_params=ROOM,
+    )(near(carry), *[near(x) for x in held])
+
+
+def share_kernel(inner, outer, *refs, slots):
+    around, (mine, theirs) = refs[: len(slots)], refs[-2:]
+    core, _ = place_of(inner.shape[0])
+    first = core == 0
+    for n, i in enumerate(slots):
+        earlier, later = around[n][0], around[n][1]
+        mine[n, 0] = earlier + jnp.where(first, 0.0, inner[i])
+        mine[n, 1] = later + jnp.where(first, inner[i], 0.0)
+        theirs[n, 0] = earlier + jnp.where(first, outer[i], 0.0)
+        theirs[n, 1] = later + jnp.where(first, 0.0, outer[i])
+
+
+def shares_of(inner, outer, around, slots, after=()):
+    _, width, _ = inner.shape
+    return pl.pallas_call(
+        functools.partial(share_kernel, slots=slots),
+        out_shape=[pltpu.VMEM((len(slots), 2, width, width), F32)] * 2,
+        in_specs=[WHOLE] * (2 + len(slots)) + [PLACED] * len(after),
+        out_specs=[WHOLE] * 2,
+        compiler_params=ROOM,
+    )(near(inner), near(outer), *[near(around[i]) for i in slots], *[near(x) for x in after])
 
 
 def local_kernel(qs, ks, vs, gs, after, gq, gk, gv):
@@ -217,43 +268,49 @@
     )(near(after), *[near(x) for x in held])
 
 
-def final_kernel(k, v, g, lq, lk, lv, state, *refs, other):
-    gq, gk, gv, bq, bk, bv, sems = refs[-7:]
-    slots = state.shape[0]
-    core, rank = place_of(slots)
-    first = (1 - core if other else core) * slots
+def final_kernel(k, v, g, lq, lk, lv, *refs, pieces, given):
+    bq, bk, bv, sems = refs[-4:]
+    gq, gk, gv, *marks = refs[len(pieces) + given : -4]
+    for mark in marks:
+        mark[...] = jnp.zeros_like(mark)
+    half = k.shape[0] // 2
+    core, rank = place_of(half)
     copies = []
-    for i in range(slots):
-        earlier, later = state[i, 0].astype(BF16), state[i, 1].astype(BF16)
-        head = first + (rank ^ i)
-        bq[i] = (lq[head] + dot(g[head], earlier, 1, 1)).astype(BF16)
-        bk[i] = (lk[head] + dot(v[head], later, 1, 1)).astype(BF16)
-        bv[i] = (lv[head] + dot(k[head], later, 1, 0)).astype(BF16)
-        for n, (here, there) in enumerate(((bq, gq), (bk, gk), (bv, gv))):
-            copies.append(pltpu.make_async_copy(here.at[i], there.at[head], sems.at[i, n]))
-            copies[-1].start()
+    for state, (other, slots) in zip(refs, pieces):
+        first = (1 - core if other else core) * half
+        for i, slot in enumerate(slots):
+            earlier, later = state[i, 0].astype(BF16), state[i, 1].astype(BF16)
+            head, n = first + (rank ^ slot), len(copies) // 3
+            bq[n] = (lq[head] + dot(g[head], earlier, 1, 1)).astype(BF16)
+            bk[n] = (lk[head] + dot(v[head], later, 1, 1)).astype(BF16)
+            bv[n] = (lv[head] + dot(k[head], later, 1, 0)).astype(BF16)
+            for m, (here, there) in enumerate(((bq, gq), (bk, gk), (bv, gv))):
+                copies.append(pltpu.make_async_copy(here.at[n], there.at[head], sems.at[n, m]))
+                copies[-1].start()
     for copy in copies:
         copy.wait()
 
 
-def final_sums(data, parts, state, other, filled=()):
+def final_sums(data, parts, states, pieces, filled=()):
     _, tokens, width = data[0].shape
-    slots = state.shape[0]
-    return pl.pallas_call(
-        functools.partial(final_kernel, other=other),
-        out_shape=[jax.ShapeDtypeStruct(data[0].shape, BF16)] * 3,
-        in_specs=[WHOLE] * 7 + [PLACED] * len(filled),
-        out_specs=[PLACED] * 3,
-        input_output_aliases={7 + n: n for n in range(len(filled))},
-        scratch_shapes=[pltpu.VMEM((slots, tokens, width), BF16)] * 3
-        + [pltpu.SemaphoreType.DMA((slots, 3))],
+    count = sum(len(slots) for _, slots in pieces)
+    held = 6 + len(states)
+    return pl.pallas_call(
+        functools.partial(final_kernel, pieces=pieces, given=len(filled)),
+        out_shape=[jax.ShapeDtypeStruct(data[0].shape, BF16)] * 3
+        + [pltpu.VMEM((8, width), F32)] * (not filled),
+        in_specs=[WHOLE] * held + [PLACED] * len(filled),
+        out_specs=[PLACED] * 3 + [WHOLE] * (not filled),
+        input_output_aliases={held + n: n for n in range(len(filled))},
+        scratch_shapes=[pltpu.VMEM((count, tokens, width), BF16)] * 3
+        + [pltpu.SemaphoreType.DMA((count, 3))],
         compiler_params=ROOM,
         cost_estimate=pl.CostEstimate(
-            flops=slots * 6 * tokens * width * width,
-            bytes_accessed=slots * 6 * tokens * width,
+            flops=count * 6 * tokens * width * width,
+            bytes_accessed=count * 6 * tokens * width,
             transcendentals=0,
         ),
-    )(*[near(x) for x in (*data[1:], *parts, state)], *filled)
+    )(*[near(x) for x in (*data[1:], *parts, *states)], *filled)
 
 
 def swap(x, mask):
@@ -265,13 +322,11 @@
     def body(queries, key_rows, value_rows, grad_out):
         count, index = lax.axis_size("seq"), lax.axis_index("seq")
         slots = group
-        core = index & 1
-        rank = (index >> 1) & (group - 1)
         data = (queries, key_rows, value_rows, grad_out)
 
         came = swap(away_states(data, slots), 1)
         keep = keep_states(data, slots)
-        total = totals_of(came, keep)
+        *total, inner, outer = totals_of(came, keep)
 
         held = [total[0]] + [swap(total[j], 2 * j) for j in range(1, group)]
         parts = local_parts(data, total[0])
@@ -293,28 +348,17 @@
             )
             bit *= 2
 
-        def outside(j):
-            earlier, later = carry[0], carry[1]
-            for i in range(group):
-                if i != j:
-                    before = (rank ^ i) < (rank ^ j)
-                    earlier = earlier + jnp.where(before, held[i][0], 0.0)
-                    later = later + jnp.where(before, 0.0, held[i][1])
-            return jnp.stack([earlier, later])
-
-        around = jnp.stack(
-            [outside(0)] + [swap(outside(j), 2 * j) for j in range(1, group)]
-        )
-        first = core == 0
-        mine = around + jnp.stack(
-            [jnp.where(first, 0.0, came[:, 0]), jnp.where(first, came[:, 1], 0.0)], 1
-        )
-        theirs = around + jnp.stack(
-            [jnp.where(first, keep[:, 0], 0.0), jnp.where(first, 0.0, keep[:, 1])], 1
-        )
+        around = [outside_of(carry, held, j) for j in range(group)]
+        around = [swap(x, 2 * j) if j else x for j, x in enumerate(around)]
+        soon, late = (0, group - 1), tuple(range(group - 2, 0, -1))
+        mine, theirs = shares_of(inner, outer, around, soon)
         other = swap(theirs, 1)
-        done = final_sums(data, parts, mine, False)
-        return tuple(final_sums(data, parts, other, True, done))
+        *done, mark = final_sums(data, parts, [mine], [(False, soon)])
+        late_mine, late_theirs = shares_of(inner, outer, around, late, [mark])
+        late_other = swap(late_theirs, 1)
+        pieces = [(True, soon), (False, late)]
+        done = final_sums(data, parts, [other, late_mine], pieces, done)
+        return tuple(final_sums(data, parts, [late_other], [(True, late)], done))
 
     return body
 

time: 33.5 us -> 31.9 us (0.952)
  waiting for transfers between devices: 11.9 us -> 8.73 us
  starting transfers between devices: 12.6 us -> 14.3 us
  other arithmetic: 1.16 us -> 0.03 us
  Pallas kernels: 6.56 us -> 7.66 us
    ppermute x9 -> x10, waiting for transfers between devices: 11.9 us -> 8.73 us  [swap(): return lax.ppermute(x, 'seq', [(i, i ^ mask) for i in range(count)])]
    ppermute x9 -> x10, starting transfers between devices: 12.6 us -> 14.3 us  [swap(): return lax.ppermute(x, 'seq', [(i, i ^ mask) for i in range(count)])]
    pallas_call x2 -> x9, Pallas kernels: 2.34 us -> 3.41 us  [the longest x3 3.15 us: final_sums(): pl.pallas_call(functools.partial(final_kernel, pieces=pieces, given=len(f...]
    select_n x2 -> x0, other arithmetic: 0.86 us -> none  [the longest x1 0.83 us: body(): jnp.where(first, keep[:, 0], 0.0)]
  transfers between devices with their start and end apart: 9 -> 10, of which waited for: 8 -> 6; matrix products, arithmetic and copies ran while one was open for 3% -> 0% of each run, Pallas kernels for 11% -> 15%
where the time goes in v5:
time: 31.9 us; the launch traced here: 31.5 us
  starting transfers between devices  14.3 us (45%)
  waiting for transfers between devices  8.73 us (27%)
  Pallas kernels  7.66 us (24%)
  between operations  0.79 us (2%)
    ppermute x10, starting transfers between devices, swap(): return lax.ppermute(x, 'seq', [(i, i ^ mask) for i in range(count)])  14.3 us
    ppermute x10, waiting for transfers between devices, swap(): return lax.ppermute(x, 'seq', [(i, i ^ mask) for i in range(count)])  8.73 us
    pallas_call x3, Pallas kernels, final_sums(): pl.pallas_call(functools.partial(final_kernel, pieces=pieces, given=len(f...  3.15 us
    pallas_call x2, Pallas kernels, state_call(): pl.pallas_call(kernel, out_shape=pltpu.VMEM((slots, 2, width, width), F32...  2.12 us
    pallas_call x1, Pallas kernels, local_parts(): pl.pallas_call(local_kernel, out_shape=[pltpu.VMEM(data[0].shape, F32)] *...  2.02 us
  transfers between devices with their start and end apart: 10, of which 6 were waited for; matrix products, arithmetic and copies ran while one was open for 0% of the time, Pallas kernels for 15%

profile of v5, /device:TPU:1, one launch (start us, length us, event | category | flops | bytes accessed | tf_op | source)
XLA Modules:
  0.0 31.5 jit_solution(18385146263756762125)
XLA Ops:
  0.6 0.0 copy-start
  0.6 0.0 copy-start.1
  0.7 0.0 copy-start.2
  0.7 0.0 copy-start.3
  0.7 1.8 %shard_map.67 = f32[4,2,128,128]{3,2,1,0:T(8,128)S(1)} custom-call(bf16[8,256,128]{2,1,0:T(8,128)(2,1)} %qs.1, bf16[8,256,128]{2,1,0:T(8,128)(2,1)} %k.9, bf16[8,256,128]{2,1,0:T(8,128)(2,1)} %v.9, bf16[8,256,128]{2,1,0:T(8,128)(2,1)} %g.9), custom_call_target="tpu_custom_call" | custom-call | flops 67108864 | bytes 1048576 | tf_op jit(solution)/shard_map/pallas_call | solution.py:131
  2.4 0.1 collective-permute-start
  2.6 0.0 copy-done
  2.6 0.0 copy-done.1
  2.6 0.0 copy-done.2
  2.6 0.0 copy-done.3
  2.6 0.4 %shard_map.68.keep = f32[4,2,128,128]{3,2,1,0:T(8,128)S(1)} custom-call(bf16[8,256,128]{2,1,0:T(8,128)(2,1)S(1)} %copy-done.3, bf16[8,256,128]{2,1,0:T(8,128)(2,1)S(1)} %copy-done, bf16[8,256,128]{2,1,0:T(8,128)(2,1)S(1)} %copy-done.1, bf16[8,256,128]{2,1,0:T(8,128)(2,1)S(1)} %copy-done.2), custom_call_target="tpu_custom_call" | custom-call | flops 67108864 | bytes 1048576 | tf_op jit(solution)/shard_map/pallas_call | solution.py:131
  2.9 1.5 %collective-permute-done.came = f32[4,2,128,128]{3,2,1,0:T(8,128)S(1)} collective-permute-done((f32[4,2,128,128]{3,2,1,0:T(8,128)S(1)}, f32[4,2,128,128]{3,2,1,0:T(8,128)S(1)}, u32[]{:S(2)}, u32[]{:S(2)}) %collective-permute-start) | collective-permute-done | bytes 524320 | tf_op jit(solution)/shard_map/ppermute | solution.py:318
  4.4 0.1 shard_map.69
  4.5 2.4 %collective-permute-start.1 = (f32[2,128,128]{2,1,0:T(8,128)S(1)}, f32[2,128,128]{2,1,0:T(8,128)S(1)}, u32[]{:S(2)}, u32[]{:S(2)}) collective-permute-start(f32[2,128,128]{2,1,0:T(8,128)S(1)} %get-tuple-element.29), channel_id=1, source_target_pairs={{0,4},{2,6},{4,0},{6,2},{8,12},{10,14},{12,8},{14,10},{16,20},{18,... | collective-permute-start | bytes 393224 | tf_op jit(solution)/shard_map/ppermute | solution.py:318
  6.9 1.3 %collective-permute-start.2 = (f32[2,128,128]{2,1,0:T(8,128)S(1)}, f32[2,128,128]{2,1,0:T(8,128)S(1)}, u32[]{:S(2)}, u32[]{:S(2)}) collective-permute-start(f32[2,128,128]{2,1,0:T(8,128)S(1)} %get-tuple-element.30), channel_id=1, source_target_pairs={{0,8},{2,10},{4,12},{6,14},{8,0},{10,2},{12,4},{14,6},{16,24},{18,... | collective-permute-start | bytes 393224 | tf_op jit(solution)/shard_map/ppermute | solution.py:318
  8.2 0.0 collective-permute-start.3
  8.2 2.0 %shard_map.70 = (f32[8,256,128]{2,1,0:T(8,128)S(1)}, f32[8,256,128]{2,1,0:T(8,128)S(1)}, f32[8,256,128]{2,1,0:T(8,128)S(1)}) custom-call(bf16[8,256,128]{2,1,0:T(8,128)(2,1)S(1)} %copy-done.3, bf16[8,256,128]{2,1,0:T(8,128)(2,1)S(1)} %copy-done, bf16[8,256,128]{2,1,0:T(8,128)(2,1)S(1)} %copy-done.1, bf16[8,256,128]{2,1,0:T(8,128)(2,1)S(1)} %copy-done.2, ...), custom_call_target="tpu_custom_call" | custom-call | flops 805306368 | bytes 5242880 | tf_op jit(solution)/shard_map/pallas_call | solution.py:239
  10.2 0.2 collective-permute-done.1.refs_1_
  10.5 0.8 %collective-permute-done.2.refs_2_ = f32[2,128,128]{2,1,0:T(8,128)S(1)} collective-permute-done((f32[2,128,128]{2,1,0:T(8,128)S(1)}, f32[2,128,128]{2,1,0:T(8,128)S(1)}, u32[]{:S(2)}, u32[]{:S(2)}) %collective-permute-start.2) | collective-permute-done | bytes 131104 | tf_op jit(solution)/shard_map/ppermute | solution.py:318
  11.3 2.7 %collective-permute-done.3.refs_3_ = f32[2,128,128]{2,1,0:T(8,128)S(1)} collective-permute-done((f32[2,128,128]{2,1,0:T(8,128)S(1)}, f32[2,128,128]{2,1,0:T(8,128)S(1)}, u32[]{:S(2)}, u32[]{:S(2)}) %collective-permute-start.3) | collective-permute-done | bytes 131104 | tf_op jit(solution)/shard_map/ppermute | solution.py:318
  14.1 2.7 %collective-permute-start.4 = (f32[128,128]{1,0:T(8,128)S(1)}, f32[128,128]{1,0:T(8,128)S(1)}, u32[]{:S(2)}, u32[]{:S(2)}) collective-permute-start(f32[128,128]{1,0:T(8,128)S(1)} %fusion), channel_id=1, source_target_pairs={{0,16},{2,18},{4,20},{6,22},{8,24},{10,26},{12,28},{14,30},{16,0},... | collective-permute-start | bytes 196616 | tf_op jit(solution)/shard_map/ppermute | solution.py:318
  16.8 1.7 %collective-permute-done.4 = f32[128,128]{1,0:T(8,128)S(1)} collective-permute-done((f32[128,128]{1,0:T(8,128)S(1)}, f32[128,128]{1,0:T(8,128)S(1)}, u32[]{:S(2)}, u32[]{:S(2)}) %collective-permute-start.4) | collective-permute-done | bytes 65568 | tf_op jit(solution)/shard_map/ppermute | solution.py:318
  18.5 0.1 shard_map.75
  18.5 2.2 %collective-permute-start.7 = (f32[2,128,128]{2,1,0:T(8,128)S(1)}, f32[2,128,128]{2,1,0:T(8,128)S(1)}, u32[]{:S(2)}, u32[]{:S(2)}) collective-permute-start(f32[2,128,128]{2,1,0:T(8,128)S(1)} %shard_map.75), channel_id=1, source_target_pairs={{0,12},{2,14},{4,8},{6,10},{8,4},{10,6},{12,0},{14,2},{16,28},{18,... | collective-permute-start | bytes 393224 | tf_op jit(solution)/shard_map/ppermute | solution.py:318
  20.7 0.1 collective-permute-start.5
  20.9 0.5 %collective-permute-start.6 = (f32[2,128,128]{2,1,0:T(8,128)S(1)}, f32[2,128,128]{2,1,0:T(8,128)S(1)}, u32[]{:S(2)}, u32[]{:S(2)}) collective-permute-start(f32[2,128,128]{2,1,0:T(8,128)S(1)} %shard_map.73), channel_id=1, source_target_pairs={{0,4},{2,6},{4,0},{6,2},{8,12},{10,14},{12,8},{14,10},{16,20},{18,... | collective-permute-start | bytes 393224 | tf_op jit(solution)/shard_map/ppermute | solution.py:318
  21.5 1.8 %collective-permute-done.7.refs_1_ = f32[2,128,128]{2,1,0:T(8,128)S(1)} collective-permute-done((f32[2,128,128]{2,1,0:T(8,128)S(1)}, f32[2,128,128]{2,1,0:T(8,128)S(1)}, u32[]{:S(2)}, u32[]{:S(2)}) %collective-permute-start.7) | collective-permute-done | bytes 131104 | tf_op jit(solution)/shard_map/ppermute | solution.py:318
  23.3 3.7 %collective-permute-start.9 = (f32[2,2,128,128]{3,2,1,0:T(8,128)S(1)}, f32[2,2,128,128]{3,2,1,0:T(8,128)S(1)}, u32[]{:S(2)}, u32[]{:S(2)}) collective-permute-start(f32[2,2,128,128]{3,2,1,0:T(8,128)S(1)} %get-tuple-element.35), channel_id=1, source_target_pairs={{0,2},{2,0},{4,6},{6,4},{8,10},{10,8},{12,14},{14,12},{16,18},{18,... | collective-permute-start | bytes 786440 | tf_op jit(solution)/shard_map/ppermute | solution.py:318
  27.0 1.0 %shard_map.77 = (bf16[8,256,128]{2,1,0:T(8,128)(2,1)}, bf16[8,256,128]{2,1,0:T(8,128)(2,1)}, bf16[8,256,128]{2,1,0:T(8,128)(2,1)}, f32[8,128]{1,0:T(8,128)S(1)}) custom-call(bf16[8,256,128]{2,1,0:T(8,128)(2,1)S(1)} %copy-done, bf16[8,256,128]{2,1,0:T(8,128)(2,1)S(1)} %copy-done.1, bf16[8,256,128]{2,1,0:T(8,128)(2,1)S(1)} %copy-done.2, ...), custom_call_target="tpu_custom_call" | custom-call | flops 50331648 | bytes 393216 | tf_op jit(solution)/shard_map/pallas_call | solution.py:298
  28.0 0.0 collective-permute-done.5.refs_0_
  28.0 0.0 collective-permute-done.6.refs_1_
  28.0 0.1 shard_map.78
  28.1 1.2 %collective-permute-start.8 = (f32[2,2,128,128]{3,2,1,0:T(8,128)S(1)}, f32[2,2,128,128]{3,2,1,0:T(8,128)S(1)}, u32[]{:S(2)}, u32[]{:S(2)}) collective-permute-start(f32[2,2,128,128]{3,2,1,0:T(8,128)S(1)} %get-tuple-element.34), channel_id=1, source_target_pairs={{0,2},{2,0},{4,6},{6,4},{8,10},{10,8},{12,14},{14,12},{16,18},{18,... | collective-permute-start | bytes 786440 | tf_op jit(solution)/shard_map/ppermute | solution.py:318
  29.3 0.0 collective-permute-done.9.refs_0_
  29.3 1.2 %shard_map.79 = (bf16[8,256,128]{2,1,0:T(8,128)(2,1)}, bf16[8,256,128]{2,1,0:T(8,128)(2,1)}, bf16[8,256,128]{2,1,0:T(8,128)(2,1)}) custom-call(bf16[8,256,128]{2,1,0:T(8,128)(2,1)S(1)} %copy-done, bf16[8,256,128]{2,1,0:T(8,128)(2,1)S(1)} %copy-done.1, ...), custom_call_target="tpu_custom_call", output_to_operand_aliasing={{0}: (8, {}), {1}: (9, {}), {2}: (10, {})} | custom-call | flops 100663296 | bytes 786432 | tf_op jit(solution)/shard_map/pallas_call | solution.py:298
  30.5 0.0 collective-permute-done.8.refs_0_
  30.5 1.0 %shard_map.80 = (bf16[8,256,128]{2,1,0:T(8,128)(2,1)}, bf16[8,256,128]{2,1,0:T(8,128)(2,1)}, bf16[8,256,128]{2,1,0:T(8,128)(2,1)}) custom-call(bf16[8,256,128]{2,1,0:T(8,128)(2,1)S(1)} %copy-done, bf16[8,256,128]{2,1,0:T(8,128)(2,1)S(1)} %copy-done.1, bf16[8,256,128]{2,1,0:T(8,128)(2,1)S(1)} %copy-done.2, ...), custom_call_target="tpu_custom_call", output_to_operand_aliasing={{0}: (7, {}), {1}: (8, {}), {2}: (9, {})} | custom-call | flops 50331648 | bytes 393216 | tf_op jit(solution)/shard_map/pallas_call | solution.py:298
  (8 shorter events, 0.2 us)
Async XLA Ops:
  0.6 1.9 %copy-start = (bf16[8,256,128]{2,1,0:T(8,128)(2,1)S(1)}, bf16[8,256,128]{2,1,0:T(8,128)(2,1)}, u32[]{:S(2)}) copy-start(bf16[8,256,128]{2,1,0:T(8,128)(2,1)} %k.9) | copy-start | bytes 1572868
  0.6 1.9 %copy-start.1 = (bf16[8,256,128]{2,1,0:T(8,128)(2,1)S(1)}, bf16[8,256,128]{2,1,0:T(8,128)(2,1)}, u32[]{:S(2)}) copy-start(bf16[8,256,128]{2,1,0:T(8,128)(2,1)} %v.9) | copy-start | bytes 1572868
  0.7 1.9 %copy-start.2 = (bf16[8,256,128]{2,1,0:T(8,128)(2,1)S(1)}, bf16[8,256,128]{2,1,0:T(8,128)(2,1)}, u32[]{:S(2)}) copy-start(bf16[8,256,128]{2,1,0:T(8,128)(2,1)} %g.9) | copy-start | bytes 1572868
  0.7 1.9 %copy-start.3 = (bf16[8,256,128]{2,1,0:T(8,128)(2,1)S(1)}, bf16[8,256,128]{2,1,0:T(8,128)(2,1)}, u32[]{:S(2)}) copy-start(bf16[8,256,128]{2,1,0:T(8,128)(2,1)} %qs.1) | copy-start | bytes 1572868
  2.4 2.0 %collective-permute-start = (f32[4,2,128,128]{3,2,1,0:T(8,128)S(1)}, f32[4,2,128,128]{3,2,1,0:T(8,128)S(1)}, u32[]{:S(2)}, u32[]{:S(2)}) collective-permute-start(f32[4,2,128,128]{3,2,1,0:T(8,128)S(1)} %shard_map.67), channel_id=1, source_target_pairs={{0,2},{2,0},{4,6},{6,4},{8,10},{10,8},{12,14},{14,12},{16,18},{18,... | collective-permute-start | bytes 1572872 | tf_op jit(solution)/shard_map/ppermute | solution.py:318
  4.5 6.0 %collective-permute-start.1 = (f32[2,128,128]{2,1,0:T(8,128)S(1)}, f32[2,128,128]{2,1,0:T(8,128)S(1)}, u32[]{:S(2)}, u32[]{:S(2)}) collective-permute-start(f32[2,128,128]{2,1,0:T(8,128)S(1)} %get-tuple-element.29), channel_id=1, source_target_pairs={{0,4},{2,6},{4,0},{6,2},{8,12},{10,14},{12,8},{14,10},{16,20},{18,... | collective-permute-start | bytes 393224 | tf_op jit(solution)/shard_map/ppermute | solution.py:318
  6.9 4.4 %collective-permute-start.2 = (f32[2,128,128]{2,1,0:T(8,128)S(1)}, f32[2,128,128]{2,1,0:T(8,128)S(1)}, u32[]{:S(2)}, u32[]{:S(2)}) collective-permute-start(f32[2,128,128]{2,1,0:T(8,128)S(1)} %get-tuple-element.30), channel_id=1, source_target_pairs={{0,8},{2,10},{4,12},{6,14},{8,0},{10,2},{12,4},{14,6},{16,24},{18,... | collective-permute-start | bytes 393224 | tf_op jit(solution)/shard_map/ppermute | solution.py:318
  8.2 5.8 %collective-permute-start.3 = (f32[2,128,128]{2,1,0:T(8,128)S(1)}, f32[2,128,128]{2,1,0:T(8,128)S(1)}, u32[]{:S(2)}, u32[]{:S(2)}) collective-permute-start(f32[2,128,128]{2,1,0:T(8,128)S(1)} %get-tuple-element.31), channel_id=1, source_target_pairs={{0,12},{2,14},{4,8},{6,10},{8,4},{10,6},{12,0},{14,2},{16,28},{18,... | collective-permute-start | bytes 393224 | tf_op jit(solution)/shard_map/ppermute | solution.py:318
  14.1 4.4 %collective-permute-start.4 = (f32[128,128]{1,0:T(8,128)S(1)}, f32[128,128]{1,0:T(8,128)S(1)}, u32[]{:S(2)}, u32[]{:S(2)}) collective-permute-start(f32[128,128]{1,0:T(8,128)S(1)} %fusion), channel_id=1, source_target_pairs={{0,16},{2,18},{4,20},{6,22},{8,24},{10,26},{12,28},{14,30},{16,0},... | collective-permute-start | bytes 196616 | tf_op jit(solution)/shard_map/ppermute | solution.py:318
  18.5 4.8 %collective-permute-start.7 = (f32[2,128,128]{2,1,0:T(8,128)S(1)}, f32[2,128,128]{2,1,0:T(8,128)S(1)}, u32[]{:S(2)}, u32[]{:S(2)}) collective-permute-start(f32[2,128,128]{2,1,0:T(8,128)S(1)} %shard_map.75), channel_id=1, source_target_pairs={{0,12},{2,14},{4,8},{6,10},{8,4},{10,6},{12,0},{14,2},{16,28},{18,... | collective-permute-start | bytes 393224 | tf_op jit(solution)/shard_map/ppermute | solution.py:318
  20.7 7.3 %collective-permute-start.5 = (f32[2,128,128]{2,1,0:T(8,128)S(1)}, f32[2,128,128]{2,1,0:T(8,128)S(1)}, u32[]{:S(2)}, u32[]{:S(2)}) collective-permute-start(f32[2,128,128]{2,1,0:T(8,128)S(1)} %shard_map.72), channel_id=1, source_target_pairs={{0,8},{2,10},{4,12},{6,14},{8,0},{10,2},{12,4},{14,6},{16,24},{18,... | collective-permute-start | bytes 393224 | tf_op jit(solution)/shard_map/ppermute | solution.py:318
  20.9 7.1 %collective-permute-start.6 = (f32[2,128,128]{2,1,0:T(8,128)S(1)}, f32[2,128,128]{2,1,0:T(8,128)S(1)}, u32[]{:S(2)}, u32[]{:S(2)}) collective-permute-start(f32[2,128,128]{2,1,0:T(8,128)S(1)} %shard_map.73), channel_id=1, source_target_pairs={{0,4},{2,6},{4,0},{6,2},{8,12},{10,14},{12,8},{14,10},{16,20},{18,... | collective-permute-start | bytes 393224 | tf_op jit(solution)/shard_map/ppermute | solution.py:318
  23.3 6.0 %collective-permute-start.9 = (f32[2,2,128,128]{3,2,1,0:T(8,128)S(1)}, f32[2,2,128,128]{3,2,1,0:T(8,128)S(1)}, u32[]{:S(2)}, u32[]{:S(2)}) collective-permute-start(f32[2,2,128,128]{3,2,1,0:T(8,128)S(1)} %get-tuple-element.35), channel_id=1, source_target_pairs={{0,2},{2,0},{4,6},{6,4},{8,10},{10,8},{12,14},{14,12},{16,18},{18,... | collective-permute-start | bytes 786440 | tf_op jit(solution)/shard_map/ppermute | solution.py:318
  28.1 2.4 %collective-permute-start.8 = (f32[2,2,128,128]{3,2,1,0:T(8,128)S(1)}, f32[2,2,128,128]{3,2,1,0:T(8,128)S(1)}, u32[]{:S(2)}, u32[]{:S(2)}) collective-permute-start(f32[2,2,128,128]{3,2,1,0:T(8,128)S(1)} %get-tuple-element.34), channel_id=1, source_target_pairs={{0,2},{2,0},{4,6},{6,4},{8,10},{10,8},{12,14},{14,12},{16,18},{18,... | collective-permute-start | bytes 786440 | tf_op jit(solution)/shard_map/ppermute | solution.py:318

commit v6 on v5

--- a/solution.py
+++ b/solution.py
@@ -99,8 +99,16 @@
     return index & 1, (index >> 1) & (slots - 1)
 
 
-def away_kernel(q, k, v, g, out, qs, ks, vs, gs, sems):
-    slots = out.shape[0]
+def states_into(outs, split, m, a, b, first, rank):
+    for out, part in zip(outs, split):
+        for n, slot in enumerate(part):
+            head = first + (rank ^ slot)
+            out[n, m] = dot(a[head], b[head], 0, 0)
+
+
+def away_kernel(q, k, v, g, *refs, split):
+    *outs, qs, ks, vs, gs, sems = refs
+    slots = qs.shape[0]
     core, rank = place_of(slots)
     first = (1 - core) * slots
     copies = []
@@ -109,53 +117,49 @@
         copies[-1].start()
     copies[0].wait()
     copies[1].wait()
-    for i in range(slots):
-        out[i, 0] = dot(ks[rank ^ i], vs[rank ^ i], 0, 0)
+    states_into(outs, split, 0, ks, vs, 0, rank)
     copies[2].wait()
     copies[3].wait()
-    for i in range(slots):
-        out[i, 1] = dot(qs[rank ^ i], gs[rank ^ i], 0, 0)
-
-
-def keep_kernel(q, k, v, g, out):
-    slots = out.shape[0]
+    states_into(outs, split, 1, qs, gs, 0, rank)
+
+
+def keep_kernel(q, k, v, g, *outs, split):
+    slots = q.shape[0] // 2
     core, rank = place_of(slots)
-    for i in range(slots):
-        head = core * slots + (rank ^ i)
-        out[i, 0] = dot(k[head], v[head], 0, 0)
-        out[i, 1] = dot(q[head], g[head], 0, 0)
-
-
-def state_call(kernel, data, slots, place, spec, scratch):
-    _, tokens, width = data[0].shape
-    return pl.pallas_call(
-        kernel,
-        out_shape=pltpu.VMEM((slots, 2, width, width), F32),
+    states_into(outs, split, 0, k, v, core * slots, rank)
+    states_into(outs, split, 1, q, g, core * slots, rank)
+
+
+def state_call(kernel, data, split, place, spec, scratch):
+    heads, tokens, width = data[0].shape
+    return pl.pallas_call(
+        functools.partial(kernel, split=split),
+        out_shape=[pltpu.VMEM((len(part), 2, width, width), F32) for part in split],
         in_specs=[spec] * 4,
-        out_specs=WHOLE,
+        out_specs=[WHOLE] * len(split),
         scratch_shapes=scratch,
         compiler_params=ROOM,
         cost_estimate=pl.CostEstimate(
-            flops=slots * 4 * tokens * width * width,
-            bytes_accessed=slots * 8 * tokens * width,
+            flops=heads * 2 * tokens * width * width,
+            bytes_accessed=heads * 4 * tokens * width,
             transcendentals=0,
         ),
     )(*[place(x) for x in data])
 
 
-def away_states(data, slots):
+def away_states(data, slots, split):
     _, tokens, width = data[0].shape
     scratch = [pltpu.VMEM((slots, tokens, width), BF16)] * 4 + [pltpu.SemaphoreType.DMA((4,))]
-    return state_call(away_kernel, data, slots, far, FAR, scratch)
-
-
-def keep_states(data, slots):
-    return state_call(keep_kernel, data, slots, near, WHOLE, [])
+    return state_call(away_kernel, data, split, far, FAR, scratch)
+
+
+def keep_states(data, slots, split):
+    return state_call(keep_kernel, data, split, near, WHOLE, [])
 
 
 def total_kernel(came, keep, *refs):
     *totals, inner, outer = refs
-    core, _ = place_of(len(totals))
+    core = lax.axis_index("seq") & 1
     for i, out in enumerate(totals):
         out[...] = came[i] + keep[i]
         inner[i] = jnp.where(core == 0, came[i, 1], came[i, 0])
@@ -197,12 +201,12 @@
     )(near(carry), *[near(x) for x in held])
 
 
-def share_kernel(inner, outer, *refs, slots):
-    around, (mine, theirs) = refs[: len(slots)], refs[-2:]
-    core, _ = place_of(inner.shape[0])
-    first = core == 0
-    for n, i in enumerate(slots):
-        earlier, later = around[n][0], around[n][1]
+def share_kernel(*refs, rows):
+    mine, theirs = refs[-2:]
+    first = lax.axis_index("seq") & 1 == 0
+    for n, i in enumerate(rows):
+        inner, outer, around = refs[3 * n : 3 * n + 3]
+        earlier, later = around[0], around[1]
         mine[n, 0] = earlier + jnp.where(first, 0.0, inner[i])
         mine[n, 1] = later + jnp.where(first, inner[i], 0.0)
         theirs[n, 0] = earlier + jnp.where(first, outer[i], 0.0)
@@ -210,14 +214,15 @@
 
 
 def shares_of(inner, outer, around, slots, after=()):
-    _, width, _ = inner.shape
-    return pl.pallas_call(
-        functools.partial(share_kernel, slots=slots),
-        out_shape=[pltpu.VMEM((len(slots), 2, width, width), F32)] * 2,
-        in_specs=[WHOLE] * (2 + len(slots)) + [PLACED] * len(after),
+    shape = (len(slots), *around[0].shape)
+    given = [x for i in slots for x in (inner[i][0], outer[i][0], around[i])]
+    return pl.pallas_call(
+        functools.partial(share_kernel, rows=[inner[i][1] for i in slots]),
+        out_shape=[pltpu.VMEM(shape, F32)] * 2,
+        in_specs=[WHOLE] * len(given) + [PLACED] * len(after),
         out_specs=[WHOLE] * 2,
         compiler_params=ROOM,
-    )(near(inner), near(outer), *[near(around[i]) for i in slots], *[near(x) for x in after])
+    )(*[near(x) for x in (*given, *after)])
 
 
 def local_kernel(qs, ks, vs, gs, after, gq, gk, gv):
@@ -324,9 +329,15 @@
         slots = group
         data = (queries, key_rows, value_rows, grad_out)
 
-        came = swap(away_states(data, slots), 1)
-        keep = keep_states(data, slots)
-        *total, inner, outer = totals_of(came, keep)
+        split = ((1, 2), (0, *range(3, slots)))
+        away = away_states(data, slots, split)
+        keep = keep_states(data, slots, split)
+        came = [swap(x, 1) for x in away]
+        total, inner, outer = {}, {}, {}
+        for part, a, b in zip(split, came, keep):
+            *sums, into, from_here = totals_of(a, b)
+            for n, j in enumerate(part):
+                total[j], inner[j], outer[j] = sums[n], (into, n), (from_here, n)
 
         held = [total[0]] + [swap(total[j], 2 * j) for j in range(1, group)]
         parts = local_parts(data, total[0])
@@ -371,7 +382,7 @@
         tokens = queries.shape[1] // count
         group = heads // 2
         powers = all(n > 0 and n & (n - 1) == 0 for n in (count, group))
-        fits = powers and heads == 2 * group and tokens == TILE and count >= 4 * group
+        fits = powers and heads == 2 * group and group >= 4 and tokens == TILE and count >= 4 * group
         body = sliced_body(group) if fits else plain_body
         return jax.shard_map(
             body, mesh=mesh, in_specs=(SPEC,) * 4, out_specs=(SPEC,) * 3, check_vma=False

time: 31.9 us -> 31.5 us (0.987)
  waiting for transfers between devices: 8.73 us -> 7.64 us
  starting transfers between devices: 14.3 us -> 14.9 us
    ppermute x10 -> x11, waiting for transfers between devices: 8.73 us -> 7.64 us  [swap(): return lax.ppermute(x, 'seq', [(i, i ^ mask) for i in range(count)])]
    ppermute x10 -> x11, starting transfers between devices: 14.3 us -> 14.9 us  [swap(): return lax.ppermute(x, 'seq', [(i, i ^ mask) for i in range(count)])]
  transfers between devices with their start and end apart: 10 -> 11, of which waited for: 6 -> 6; matrix products, arithmetic and copies ran while one was open for 0% -> 0% of each run, Pallas kernels for 15% -> 16%
where the time goes in v6:
time: 31.5 us; the launch traced here: 31.1 us
  starting transfers between devices  14.9 us (47%)
  Pallas kernels  7.67 us (24%)
  waiting for transfers between devices  7.64 us (24%)
  between operations  0.81 us (3%)
    ppermute x11, starting transfers between devices, swap(): return lax.ppermute(x, 'seq', [(i, i ^ mask) for i in range(count)])  14.9 us
    ppermute x11, waiting for transfers between devices, swap(): return lax.ppermute(x, 'seq', [(i, i ^ mask) for i in range(count)])  7.64 us
    pallas_call x3, Pallas kernels, final_sums(): pl.pallas_call(functools.partial(final_kernel, pieces=pieces, given=len(f...  3.15 us
    pallas_call x2, Pallas kernels, state_call(): pl.pallas_call(functools.partial(kernel, split=split), out_shape=[pltpu.V...  2.12 us
    pallas_call x1, Pallas kernels, local_parts(): pl.pallas_call(local_kernel, out_shape=[pltpu.VMEM(data[0].shape, F32)] *...  2.02 us
  transfers between devices with their start and end apart: 11, of which 6 were waited for; matrix products, arithmetic and copies ran while one was open for 0% of the time, Pallas kernels for 16%

profile of v6, /device:TPU:1, one launch (start us, length us, event | category | flops | bytes accessed | tf_op | source)
XLA Modules:
  0.0 31.1 jit_solution(3896918808091433505)
XLA Ops:
  0.6 0.0 copy-start
  0.6 0.0 copy-start.1
  0.7 0.0 copy-start.2
  0.7 0.0 copy-start.3
  0.7 1.8 %shard_map.67 = (f32[2,2,128,128]{3,2,1,0:T(8,128)S(1)}, f32[2,2,128,128]{3,2,1,0:T(8,128)S(1)}) custom-call(bf16[8,256,128]{2,1,0:T(8,128)(2,1)} %qs.1, bf16[8,256,128]{2,1,0:T(8,128)(2,1)} %k.9, bf16[8,256,128]{2,1,0:T(8,128)(2,1)} %v.9, bf16[8,256,128]{2,1,0:T(8,128)(2,1)} %g.9), custom_call_target="tpu_custom_call" | custom-call | flops 67108864 | bytes 1048576 | tf_op jit(solution)/shard_map/pallas_call | solution.py:135
  2.4 0.1 collective-permute-start.1
  2.6 0.5 %collective-permute-start = (f32[2,2,128,128]{3,2,1,0:T(8,128)S(1)}, f32[2,2,128,128]{3,2,1,0:T(8,128)S(1)}, u32[]{:S(2)}, u32[]{:S(2)}) collective-permute-start(f32[2,2,128,128]{3,2,1,0:T(8,128)S(1)} %get-tuple-element.29), channel_id=1, source_target_pairs={{0,2},{2,0},{4,6},{6,4},{8,10},{10,8},{12,14},{14,12},{16,18},{18,... | collective-permute-start | bytes 786440 | tf_op jit(solution)/shard_map/ppermute | solution.py:323
  3.0 0.0 copy-done
  3.0 0.0 copy-done.1
  3.0 0.0 copy-done.2
  3.0 0.0 copy-done.3
  3.0 0.4 %shard_map.68 = (f32[2,2,128,128]{3,2,1,0:T(8,128)S(1)}, f32[2,2,128,128]{3,2,1,0:T(8,128)S(1)}) custom-call(bf16[8,256,128]{2,1,0:T(8,128)(2,1)S(1)} %copy-done.3, bf16[8,256,128]{2,1,0:T(8,128)(2,1)S(1)} %copy-done, bf16[8,256,128]{2,1,0:T(8,128)(2,1)S(1)} %copy-done.1, bf16[8,256,128]{2,1,0:T(8,128)(2,1)S(1)} %copy-done.2), custom_call_target="tpu_custom_call" | custom-call | flops 67108864 | bytes 1048576 | tf_op jit(solution)/shard_map/pallas_call | solution.py:135
  3.4 0.6 %collective-permute-done.1.came = f32[2,2,128,128]{3,2,1,0:T(8,128)S(1)} collective-permute-done((f32[2,2,128,128]{3,2,1,0:T(8,128)S(1)}, f32[2,2,128,128]{3,2,1,0:T(8,128)S(1)}, u32[]{:S(2)}, u32[]{:S(2)}) %collective-permute-start.1) | collective-permute-done | bytes 262176 | tf_op jit(solution)/shard_map/ppermute | solution.py:323
  4.1 2.4 %collective-permute-start.2 = (f32[2,128,128]{2,1,0:T(8,128)S(1)}, f32[2,128,128]{2,1,0:T(8,128)S(1)}, u32[]{:S(2)}, u32[]{:S(2)}) collective-permute-start(f32[2,128,128]{2,1,0:T(8,128)S(1)} %get-tuple-element.39), channel_id=1, source_target_pairs={{0,4},{2,6},{4,0},{6,2},{8,12},{10,14},{12,8},{14,10},{16,20},{18,... | collective-permute-start | bytes 393224 | tf_op jit(solution)/shard_map/ppermute | solution.py:323
  6.5 1.3 %collective-permute-start.3 = (f32[2,128,128]{2,1,0:T(8,128)S(1)}, f32[2,128,128]{2,1,0:T(8,128)S(1)}, u32[]{:S(2)}, u32[]{:S(2)}) collective-permute-start(f32[2,128,128]{2,1,0:T(8,128)S(1)} %get-tuple-element.40), channel_id=1, source_target_pairs={{0,8},{2,10},{4,12},{6,14},{8,0},{10,2},{12,4},{14,6},{16,24},{18,... | collective-permute-start | bytes 393224 | tf_op jit(solution)/shard_map/ppermute | solution.py:323
  7.8 0.0 collective-permute-done.came
  7.9 0.1 collective-permute-start.4
  7.9 2.0 %shard_map.70 = (f32[8,256,128]{2,1,0:T(8,128)S(1)}, f32[8,256,128]{2,1,0:T(8,128)S(1)}, f32[8,256,128]{2,1,0:T(8,128)S(1)}) custom-call(bf16[8,256,128]{2,1,0:T(8,128)(2,1)S(1)} %copy-done.3, bf16[8,256,128]{2,1,0:T(8,128)(2,1)S(1)} %copy-done, bf16[8,256,128]{2,1,0:T(8,128)(2,1)S(1)} %copy-done.1, bf16[8,256,128]{2,1,0:T(8,128)(2,1)S(1)} %copy-done.2, ...), custom_call_target="tpu_custom_call" | custom-call | flops 805306368 | bytes 5242880 | tf_op jit(solution)/shard_map/pallas_call | solution.py:244
  10.0 0.1 collective-permute-done.2.refs_1_
  10.1 0.8 %collective-permute-done.3.refs_2_ = f32[2,128,128]{2,1,0:T(8,128)S(1)} collective-permute-done((f32[2,128,128]{2,1,0:T(8,128)S(1)}, f32[2,128,128]{2,1,0:T(8,128)S(1)}, u32[]{:S(2)}, u32[]{:S(2)}) %collective-permute-start.3) | collective-permute-done | bytes 131104 | tf_op jit(solution)/shard_map/ppermute | solution.py:323
  10.9 2.6 %collective-permute-done.4.refs_3_ = f32[2,128,128]{2,1,0:T(8,128)S(1)} collective-permute-done((f32[2,128,128]{2,1,0:T(8,128)S(1)}, f32[2,128,128]{2,1,0:T(8,128)S(1)}, u32[]{:S(2)}, u32[]{:S(2)}) %collective-permute-start.4) | collective-permute-done | bytes 131104 | tf_op jit(solution)/shard_map/ppermute | solution.py:323
  13.5 2.7 %collective-permute-start.5 = (f32[128,128]{1,0:T(8,128)S(1)}, f32[128,128]{1,0:T(8,128)S(1)}, u32[]{:S(2)}, u32[]{:S(2)}) collective-permute-start(f32[128,128]{1,0:T(8,128)S(1)} %fusion), channel_id=1, source_target_pairs={{0,16},{2,18},{4,20},{6,22},{8,24},{10,26},{12,28},{14,30},{16,0},... | collective-permute-start | bytes 196616 | tf_op jit(solution)/shard_map/ppermute | solution.py:323
  16.2 1.7 %collective-permute-done.5 = f32[128,128]{1,0:T(8,128)S(1)} collective-permute-done((f32[128,128]{1,0:T(8,128)S(1)}, f32[128,128]{1,0:T(8,128)S(1)}, u32[]{:S(2)}, u32[]{:S(2)}) %collective-permute-start.5) | collective-permute-done | bytes 65568 | tf_op jit(solution)/shard_map/ppermute | solution.py:323
  17.9 0.1 shard_map.76
  18.0 2.3 %collective-permute-start.8 = (f32[2,128,128]{2,1,0:T(8,128)S(1)}, f32[2,128,128]{2,1,0:T(8,128)S(1)}, u32[]{:S(2)}, u32[]{:S(2)}) collective-permute-start(f32[2,128,128]{2,1,0:T(8,128)S(1)} %shard_map.76), channel_id=1, source_target_pairs={{0,12},{2,14},{4,8},{6,10},{8,4},{10,6},{12,0},{14,2},{16,28},{18,... | collective-permute-start | bytes 393224 | tf_op jit(solution)/shard_map/ppermute | solution.py:323
  20.3 0.1 collective-permute-start.6
  20.5 0.4 %collective-permute-start.7 = (f32[2,128,128]{2,1,0:T(8,128)S(1)}, f32[2,128,128]{2,1,0:T(8,128)S(1)}, u32[]{:S(2)}, u32[]{:S(2)}) collective-permute-start(f32[2,128,128]{2,1,0:T(8,128)S(1)} %shard_map.74), channel_id=1, source_target_pairs={{0,4},{2,6},{4,0},{6,2},{8,12},{10,14},{12,8},{14,10},{16,20},{18,... | collective-permute-start | bytes 393224 | tf_op jit(solution)/shard_map/ppermute | solution.py:323
  21.0 1.8 %collective-permute-done.8.refs_5_ = f32[2,128,128]{2,1,0:T(8,128)S(1)} collective-permute-done((f32[2,128,128]{2,1,0:T(8,128)S(1)}, f32[2,128,128]{2,1,0:T(8,128)S(1)}, u32[]{:S(2)}, u32[]{:S(2)}) %collective-permute-start.8) | collective-permute-done | bytes 131104 | tf_op jit(solution)/shard_map/ppermute | solution.py:323
  22.8 3.8 %collective-permute-start.10 = (f32[2,2,128,128]{3,2,1,0:T(8,128)S(1)}, f32[2,2,128,128]{3,2,1,0:T(8,128)S(1)}, u32[]{:S(2)}, u32[]{:S(2)}) collective-permute-start(f32[2,2,128,128]{3,2,1,0:T(8,128)S(1)} %get-tuple-element.47), channel_id=1, source_target_pairs={{0,2},{2,0},{4,6},{6,4},{8,10},{10,8},{12,14},{14,12},{16,18},{18,... | collective-permute-start | bytes 786440 | tf_op jit(solution)/shard_map/ppermute | solution.py:323
  26.6 1.0 %shard_map.78 = (bf16[8,256,128]{2,1,0:T(8,128)(2,1)}, bf16[8,256,128]{2,1,0:T(8,128)(2,1)}, bf16[8,256,128]{2,1,0:T(8,128)(2,1)}, f32[8,128]{1,0:T(8,128)S(1)}) custom-call(bf16[8,256,128]{2,1,0:T(8,128)(2,1)S(1)} %copy-done, bf16[8,256,128]{2,1,0:T(8,128)(2,1)S(1)} %copy-done.1, bf16[8,256,128]{2,1,0:T(8,128)(2,1)S(1)} %copy-done.2, ...), custom_call_target="tpu_custom_call" | custom-call | flops 50331648 | bytes 393216 | tf_op jit(solution)/shard_map/pallas_call | solution.py:303
  27.6 0.0 collective-permute-done.6.refs_2_
  27.6 0.0 collective-permute-done.7.refs_5_
  27.6 0.1 shard_map.79
  27.7 1.2 %collective-permute-start.9 = (f32[2,2,128,128]{3,2,1,0:T(8,128)S(1)}, f32[2,2,128,128]{3,2,1,0:T(8,128)S(1)}, u32[]{:S(2)}, u32[]{:S(2)}) collective-permute-start(f32[2,2,128,128]{3,2,1,0:T(8,128)S(1)} %get-tuple-element.46), channel_id=1, source_target_pairs={{0,2},{2,0},{4,6},{6,4},{8,10},{10,8},{12,14},{14,12},{16,18},{18,... | collective-permute-start | bytes 786440 | tf_op jit(solution)/shard_map/ppermute | solution.py:323
  28.9 0.0 collective-permute-done.10.refs_0_
  28.9 1.2 %shard_map.80 = (bf16[8,256,128]{2,1,0:T(8,128)(2,1)}, bf16[8,256,128]{2,1,0:T(8,128)(2,1)}, bf16[8,256,128]{2,1,0:T(8,128)(2,1)}) custom-call(bf16[8,256,128]{2,1,0:T(8,128)(2,1)S(1)} %copy-done, bf16[8,256,128]{2,1,0:T(8,128)(2,1)S(1)} %copy-done.1, ...), custom_call_target="tpu_custom_call", output_to_operand_aliasing={{0}: (8, {}), {1}: (9, {}), {2}: (10, {})} | custom-call | flops 100663296 | bytes 786432 | tf_op jit(solution)/shard_map/pallas_call | solution.py:303
  30.1 0.0 collective-permute-done.9.refs_0_
  30.1 1.0 %shard_map.81 = (bf16[8,256,128]{2,1,0:T(8,128)(2,1)}, bf16[8,256,128]{2,1,0:T(8,128)(2,1)}, bf16[8,256,128]{2,1,0:T(8,128)(2,1)}) custom-call(bf16[8,256,128]{2,1,0:T(8,128)(2,1)S(1)} %copy-done, bf16[8,256,128]{2,1,0:T(8,128)(2,1)S(1)} %copy-done.1, bf16[8,256,128]{2,1,0:T(8,128)(2,1)S(1)} %copy-done.2, ...), custom_call_target="tpu_custom_call", output_to_operand_aliasing={{0}: (7, {}), {1}: (8, {}), {2}: (9, {})} | custom-call | flops 50331648 | bytes 393216 | tf_op jit(solution)/shard_map/pallas_call | solution.py:303
  (10 shorter events, 0.3 us)
Async XLA Ops:
  0.6 2.4 %copy-start = (bf16[8,256,128]{2,1,0:T(8,128)(2,1)S(1)}, bf16[8,256,128]{2,1,0:T(8,128)(2,1)}, u32[]{:S(2)}) copy-start(bf16[8,256,128]{2,1,0:T(8,128)(2,1)} %k.9) | copy-start | bytes 1572868
  0.6 2.4 %copy-start.1 = (bf16[8,256,128]{2,1,0:T(8,128)(2,1)S(1)}, bf16[8,256,128]{2,1,0:T(8,128)(2,1)}, u32[]{:S(2)}) copy-start(bf16[8,256,128]{2,1,0:T(8,128)(2,1)} %v.9) | copy-start | bytes 1572868
  0.7 2.4 %copy-start.2 = (bf16[8,256,128]{2,1,0:T(8,128)(2,1)S(1)}, bf16[8,256,128]{2,1,0:T(8,128)(2,1)}, u32[]{:S(2)}) copy-start(bf16[8,256,128]{2,1,0:T(8,128)(2,1)} %g.9) | copy-start | bytes 1572868
  0.7 2.4 %copy-start.3 = (bf16[8,256,128]{2,1,0:T(8,128)(2,1)S(1)}, bf16[8,256,128]{2,1,0:T(8,128)(2,1)}, u32[]{:S(2)}) copy-start(bf16[8,256,128]{2,1,0:T(8,128)(2,1)} %qs.1) | copy-start | bytes 1572868
  2.4 1.6 %collective-permute-start.1 = (f32[2,2,128,128]{3,2,1,0:T(8,128)S(1)}, f32[2,2,128,128]{3,2,1,0:T(8,128)S(1)}, u32[]{:S(2)}, u32[]{:S(2)}) collective-permute-start(f32[2,2,128,128]{3,2,1,0:T(8,128)S(1)} %get-tuple-element.35), channel_id=1, source_target_pairs={{0,2},{2,0},{4,6},{6,4},{8,10},{10,8},{12,14},{14,12},{16,18},{18,... | collective-permute-start | bytes 786440 | tf_op jit(solution)/shard_map/ppermute | solution.py:323
  2.6 5.2 %collective-permute-start = (f32[2,2,128,128]{3,2,1,0:T(8,128)S(1)}, f32[2,2,128,128]{3,2,1,0:T(8,128)S(1)}, u32[]{:S(2)}, u32[]{:S(2)}) collective-permute-start(f32[2,2,128,128]{3,2,1,0:T(8,128)S(1)} %get-tuple-element.29), channel_id=1, source_target_pairs={{0,2},{2,0},{4,6},{6,4},{8,10},{10,8},{12,14},{14,12},{16,18},{18,... | collective-permute-start | bytes 786440 | tf_op jit(solution)/shard_map/ppermute | solution.py:323
  4.1 6.0 %collective-permute-start.2 = (f32[2,128,128]{2,1,0:T(8,128)S(1)}, f32[2,128,128]{2,1,0:T(8,128)S(1)}, u32[]{:S(2)}, u32[]{:S(2)}) collective-permute-start(f32[2,128,128]{2,1,0:T(8,128)S(1)} %get-tuple-element.39), channel_id=1, source_target_pairs={{0,4},{2,6},{4,0},{6,2},{8,12},{10,14},{12,8},{14,10},{16,20},{18,... | collective-permute-start | bytes 393224 | tf_op jit(solution)/shard_map/ppermute | solution.py:323
  6.5 4.4 %collective-permute-start.3 = (f32[2,128,128]{2,1,0:T(8,128)S(1)}, f32[2,128,128]{2,1,0:T(8,128)S(1)}, u32[]{:S(2)}, u32[]{:S(2)}) collective-permute-start(f32[2,128,128]{2,1,0:T(8,128)S(1)} %get-tuple-element.40), channel_id=1, source_target_pairs={{0,8},{2,10},{4,12},{6,14},{8,0},{10,2},{12,4},{14,6},{16,24},{18,... | collective-permute-start | bytes 393224 | tf_op jit(solution)/shard_map/ppermute | solution.py:323
  7.9 5.6 %collective-permute-start.4 = (f32[2,128,128]{2,1,0:T(8,128)S(1)}, f32[2,128,128]{2,1,0:T(8,128)S(1)}, u32[]{:S(2)}, u32[]{:S(2)}) collective-permute-start(f32[2,128,128]{2,1,0:T(8,128)S(1)} %get-tuple-element.41), channel_id=1, source_target_pairs={{0,12},{2,14},{4,8},{6,10},{8,4},{10,6},{12,0},{14,2},{16,28},{18,... | collective-permute-start | bytes 393224 | tf_op jit(solution)/shard_map/ppermute | solution.py:323
  13.5 4.4 %collective-permute-start.5 = (f32[128,128]{1,0:T(8,128)S(1)}, f32[128,128]{1,0:T(8,128)S(1)}, u32[]{:S(2)}, u32[]{:S(2)}) collective-permute-start(f32[128,128]{1,0:T(8,128)S(1)} %fusion), channel_id=1, source_target_pairs={{0,16},{2,18},{4,20},{6,22},{8,24},{10,26},{12,28},{14,30},{16,0},... | collective-permute-start | bytes 196616 | tf_op jit(solution)/shard_map/ppermute | solution.py:323
  18.0 4.8 %collective-permute-start.8 = (f32[2,128,128]{2,1,0:T(8,128)S(1)}, f32[2,128,128]{2,1,0:T(8,128)S(1)}, u32[]{:S(2)}, u32[]{:S(2)}) collective-permute-start(f32[2,128,128]{2,1,0:T(8,128)S(1)} %shard_map.76), channel_id=1, source_target_pairs={{0,12},{2,14},{4,8},{6,10},{8,4},{10,6},{12,0},{14,2},{16,28},{18,... | collective-permute-start | bytes 393224 | tf_op jit(solution)/shard_map/ppermute | solution.py:323
  20.3 7.3 %collective-permute-start.6 = (f32[2,128,128]{2,1,0:T(8,128)S(1)}, f32[2,128,128]{2,1,0:T(8,128)S(1)}, u32[]{:S(2)}, u32[]{:S(2)}) collective-permute-start(f32[2,128,128]{2,1,0:T(8,128)S(1)} %shard_map.73), channel_id=1, source_target_pairs={{0,8},{2,10},{4,12},{6,14},{8,0},{10,2},{12,4},{14,6},{16,24},{18,... | collective-permute-start | bytes 393224 | tf_op jit(solution)/shard_map/ppermute | solution.py:323
  20.5 7.1 %collective-permute-start.7 = (f32[2,128,128]{2,1,0:T(8,128)S(1)}, f32[2,128,128]{2,1,0:T(8,128)S(1)}, u32[]{:S(2)}, u32[]{:S(2)}) collective-permute-start(f32[2,128,128]{2,1,0:T(8,128)S(1)} %shard_map.74), channel_id=1, source_target_pairs={{0,4},{2,6},{4,0},{6,2},{8,12},{10,14},{12,8},{14,10},{16,20},{18,... | collective-permute-start | bytes 393224 | tf_op jit(solution)/shard_map/ppermute | solution.py:323
  22.8 6.1 %collective-permute-start.10 = (f32[2,2,128,128]{3,2,1,0:T(8,128)S(1)}, f32[2,2,128,128]{3,2,1,0:T(8,128)S(1)}, u32[]{:S(2)}, u32[]{:S(2)}) collective-permute-start(f32[2,2,128,128]{3,2,1,0:T(8,128)S(1)} %get-tuple-element.47), channel_id=1, source_target_pairs={{0,2},{2,0},{4,6},{6,4},{8,10},{10,8},{12,14},{14,12},{16,18},{18,... | collective-permute-start | bytes 786440 | tf_op jit(solution)/shard_map/ppermute | solution.py:323
  27.7 2.4 %collective-permute-start.9 = (f32[2,2,128,128]{3,2,1,0:T(8,128)S(1)}, f32[2,2,128,128]{3,2,1,0:T(8,128)S(1)}, u32[]{:S(2)}, u32[]{:S(2)}) collective-permute-start(f32[2,2,128,128]{3,2,1,0:T(8,128)S(1)} %get-tuple-element.46), channel_id=1, source_target_pairs={{0,2},{2,0},{4,6},{6,4},{8,10},{10,8},{12,14},{14,12},{16,18},{18,... | collective-permute-start | bytes 786440 | tf_op jit(solution)/shard_map/ppermute | solution.py:323

commit v7 on v6

--- a/solution.py
+++ b/solution.py
@@ -99,62 +99,63 @@
     return index & 1, (index >> 1) & (slots - 1)
 
 
-def states_into(outs, split, m, a, b, first, rank):
-    for out, part in zip(outs, split):
-        for n, slot in enumerate(part):
-            head = first + (rank ^ slot)
-            out[n, m] = dot(a[head], b[head], 0, 0)
-
-
-def away_kernel(q, k, v, g, *refs, split):
-    *outs, qs, ks, vs, gs, sems = refs
-    slots = qs.shape[0]
+def away_kernel(q, k, v, g, out, qs, ks, vs, gs, sems, *, part):
+    slots = q.shape[0] // 2
     core, rank = place_of(slots)
     first = (1 - core) * slots
     copies = []
     for n, (there, here) in enumerate(((k, ks), (v, vs), (q, qs), (g, gs))):
-        copies.append(pltpu.make_async_copy(there.at[pl.ds(first, slots)], here, sems.at[n]))
-        copies[-1].start()
-    copies[0].wait()
-    copies[1].wait()
-    states_into(outs, split, 0, ks, vs, 0, rank)
-    copies[2].wait()
-    copies[3].wait()
-    states_into(outs, split, 1, qs, gs, 0, rank)
-
-
-def keep_kernel(q, k, v, g, *outs, split):
+        for m, slot in enumerate(part):
+            head = first + (rank ^ slot)
+            copies.append(pltpu.make_async_copy(there.at[head], here.at[m], sems.at[n, m]))
+            copies[-1].start()
+    for copy in copies:
+        copy.wait()
+    for m in range(len(part)):
+        out[m, 0] = dot(ks[m], vs[m], 0, 0)
+        out[m, 1] = dot(qs[m], gs[m], 0, 0)
+
+
+def near_kernel(q, k, v, g, *outs, parts, other):
     slots = q.shape[0] // 2
     core, rank = place_of(slots)
-    states_into(outs, split, 0, k, v, core * slots, rank)
-    states_into(outs, split, 1, q, g, core * slots, rank)
-
-
-def state_call(kernel, data, split, place, spec, scratch):
-    heads, tokens, width = data[0].shape
-    return pl.pallas_call(
-        functools.partial(kernel, split=split),
-        out_shape=[pltpu.VMEM((len(part), 2, width, width), F32) for part in split],
+    first = (1 - core if other else core) * slots
+    for out, part in zip(outs, parts):
+        for m, slot in enumerate(part):
+            head = first + (rank ^ slot)
+            out[m, 0] = dot(k[head], v[head], 0, 0)
+            out[m, 1] = dot(q[head], g[head], 0, 0)
+
+
+def state_call(kernel, data, parts, place, spec, scratch):
+    _, tokens, width = data[0].shape
+    count = sum(len(part) for part in parts)
+    return pl.pallas_call(
+        kernel,
+        out_shape=[pltpu.VMEM((len(part), 2, width, width), F32) for part in parts],
         in_specs=[spec] * 4,
-        out_specs=[WHOLE] * len(split),
+        out_specs=[WHOLE] * len(parts),
         scratch_shapes=scratch,
         compiler_params=ROOM,
         cost_estimate=pl.CostEstimate(
-            flops=heads * 2 * tokens * width * width,
-            bytes_accessed=heads * 4 * tokens * width,
+            flops=count * 4 * tokens * width * width,
+            bytes_accessed=count * 8 * tokens * width,
             transcendentals=0,
         ),
     )(*[place(x) for x in data])
 
 
-def away_states(data, slots, split):
+def away_states(data, part):
     _, tokens, width = data[0].shape
-    scratch = [pltpu.VMEM((slots, tokens, width), BF16)] * 4 + [pltpu.SemaphoreType.DMA((4,))]
-    return state_call(away_kernel, data, split, far, FAR, scratch)
-
-
-def keep_states(data, slots, split):
-    return state_call(keep_kernel, data, split, near, WHOLE, [])
+    scratch = [pltpu.VMEM((len(part), tokens, width), BF16)] * 4
+    scratch.append(pltpu.SemaphoreType.DMA((4, len(part))))
+    kernel = functools.partial(away_kernel, part=part)
+    return state_call(kernel, data, [part], far, FAR, scratch)
+
+
+def near_states(data, parts, other):
+    kernel = functools.partial(near_kernel, parts=parts, other=other)
+    return state_call(kernel, data, parts, near, WHOLE, [])
 
 
 def total_kernel(came, keep, *refs):
@@ -178,7 +179,7 @@
     )(near(came), near(keep))
 
 
-def outside_kernel(carry, *refs, slot, group):
+def outside_kernel(after, carry, *refs, slot, group):
     out = refs[-1]
     _, rank = place_of(group)
     earlier, later = carry[0], carry[1]
@@ -191,14 +192,14 @@
     out[1] = later
 
 
-def outside_of(carry, held, slot):
+def outside_of(carry, held, slot, after):
     return pl.pallas_call(
         functools.partial(outside_kernel, slot=slot, group=len(held)),
         out_shape=pltpu.VMEM(carry.shape, F32),
-        in_specs=[WHOLE] * (1 + len(held)),
+        in_specs=[PLACED] + [WHOLE] * (1 + len(held)),
         out_specs=WHOLE,
         compiler_params=ROOM,
-    )(near(carry), *[near(x) for x in held])
+    )(near(after), near(carry), *[near(x) for x in held])
 
 
 def share_kernel(*refs, rows):
@@ -255,7 +256,7 @@
     )(*[near(x) for x in data], near(after))
 
 
-def block_kernel(after, *refs):
+def block_kernel(*refs):
     out = refs[-1]
     total = refs[0][...]
     for x in refs[1:-1]:
@@ -263,14 +264,14 @@
     out[...] = total
 
 
-def block_sum(held, after):
+def block_sum(held):
     return pl.pallas_call(
         block_kernel,
         out_shape=pltpu.VMEM(held[0].shape, F32),
-        in_specs=[PLACED] + [WHOLE] * len(held),
+        in_specs=[WHOLE] * len(held),
         out_specs=WHOLE,
         compiler_params=ROOM,
-    )(near(after), *[near(x) for x in held])
+    )(*[near(x) for x in held])
 
 
 def final_kernel(k, v, g, lq, lk, lv, *refs, pieces, given):
@@ -330,8 +331,8 @@
         data = (queries, key_rows, value_rows, grad_out)
 
         split = ((1, 2), (0, *range(3, slots)))
-        away = away_states(data, slots, split)
-        keep = keep_states(data, slots, split)
+        away = away_states(data, split[0]) + near_states(data, split[1:], True)
+        keep = near_states(data, split, False)
         came = [swap(x, 1) for x in away]
         total, inner, outer = {}, {}, {}
         for part, a, b in zip(split, came, keep):
@@ -340,9 +341,9 @@
                 total[j], inner[j], outer[j] = sums[n], (into, n), (from_here, n)
 
         held = [total[0]] + [swap(total[j], 2 * j) for j in range(1, group)]
-        parts = local_parts(data, total[0])
-
-        block = block_sum(held, parts[0])
+
+        block = block_sum(held)
+        parts = local_parts(data, block)
         keys, rests = block[0], block[1]
         carry = jnp.zeros_like(block)
         bit = 2 * group
@@ -359,7 +360,7 @@
             )
             bit *= 2
 
-        around = [outside_of(carry, held, j) for j in range(group)]
+        around = [outside_of(carry, held, j, parts[0]) for j in range(group)]
         around = [swap(x, 2 * j) if j else x for j, x in enumerate(around)]
         soon, late = (0, group - 1), tuple(range(group - 2, 0, -1))
         mine, theirs = shares_of(inner, outer, around, soon)

time: 31.5 us -> 31.3 us (level)
    pallas_call x2 -> x3, Pallas kernels: 2.12 us -> 2.17 us  [state_call(): pl.pallas_call(kernel, out_shape=[pltpu.VMEM((len(part), 2, width, width)...]
  transfers between devices with their start and end apart: 11 -> 11, of which waited for: 6 -> 5; matrix products, arithmetic and copies ran while one was open for 0% -> 0% of each run, Pallas kernels for 16% -> 17%
where the time goes in v7:
time: 31.3 us; the launch traced here: 30.8 us
  starting transfers between devices  14.9 us (48%)
  Pallas kernels  7.71 us (25%)
  waiting for transfers between devices  7.35 us (23%)
  between operations  0.81 us (3%)
    ppermute x11, starting transfers between devices, swap(): return lax.ppermute(x, 'seq', [(i, i ^ mask) for i in range(count)])  14.9 us
    ppermute x11, waiting for transfers between devices, swap(): return lax.ppermute(x, 'seq', [(i, i ^ mask) for i in range(count)])  7.35 us
    pallas_call x3, Pallas kernels, final_sums(): pl.pallas_call(functools.partial(final_kernel, pieces=pieces, given=len(f...  3.14 us
    pallas_call x3, Pallas kernels, state_call(): pl.pallas_call(kernel, out_shape=[pltpu.VMEM((len(part), 2, width, width)...  2.17 us
    pallas_call x1, Pallas kernels, local_parts(): pl.pallas_call(local_kernel, out_shape=[pltpu.VMEM(data[0].shape, F32)] *...  2.02 us
  transfers between devices with their start and end apart: 11, of which 5 were waited for; matrix products, arithmetic and copies ran while one was open for 0% of the time, Pallas kernels for 17%

profile of v7, /device:TPU:1, one launch (start us, length us, event | category | flops | bytes accessed | tf_op | source)
XLA Modules:
  0.0 30.8 jit_solution(6455906443047424337)
XLA Ops:
  0.6 0.0 copy-start
  0.6 0.0 copy-start.1
  0.7 0.0 copy-start.2
  0.7 0.0 copy-start.3
  0.7 1.6 %shard_map.70 = f32[2,2,128,128]{3,2,1,0:T(8,128)S(1)} custom-call(bf16[8,256,128]{2,1,0:T(8,128)(2,1)} %qs.1, bf16[8,256,128]{2,1,0:T(8,128)(2,1)} %k.11, bf16[8,256,128]{2,1,0:T(8,128)(2,1)} %v.11, bf16[8,256,128]{2,1,0:T(8,128)(2,1)} %g.11), custom_call_target="tpu_custom_call" | custom-call | flops 33554432 | bytes 524288 | tf_op jit(solution)/shard_map/pallas_call | solution.py:133
  2.2 0.1 collective-permute-start.1
  2.4 0.0 copy-done
  2.4 0.0 copy-done.1
  2.4 0.0 copy-done.2
  2.4 0.0 copy-done.3
  2.4 0.3 shard_map.67
  2.7 0.5 %collective-permute-start = (f32[2,2,128,128]{3,2,1,0:T(8,128)S(1)}, f32[2,2,128,128]{3,2,1,0:T(8,128)S(1)}, u32[]{:S(2)}, u32[]{:S(2)}) collective-permute-start(f32[2,2,128,128]{3,2,1,0:T(8,128)S(1)} %shard_map.67), channel_id=1, source_target_pairs={{0,2},{2,0},{4,6},{6,4},{8,10},{10,8},{12,14},{14,12},{16,18},{18,... | collective-permute-start | bytes 786440 | tf_op jit(solution)/shard_map/ppermute | solution.py:324
  3.2 0.3 %shard_map.68 = (f32[2,2,128,128]{3,2,1,0:T(8,128)S(1)}, f32[2,2,128,128]{3,2,1,0:T(8,128)S(1)}) custom-call(bf16[8,256,128]{2,1,0:T(8,128)(2,1)S(1)} %copy-done.3, bf16[8,256,128]{2,1,0:T(8,128)(2,1)S(1)} %copy-done, bf16[8,256,128]{2,1,0:T(8,128)(2,1)S(1)} %copy-done.1, bf16[8,256,128]{2,1,0:T(8,128)(2,1)S(1)} %copy-done.2), custom_call_target="tpu_custom_call" | custom-call | flops 67108864 | bytes 1048576 | tf_op jit(solution)/shard_map/pallas_call | solution.py:133
  3.5 0.3 collective-permute-done.1.came
  3.9 2.4 %collective-permute-start.2 = (f32[2,128,128]{2,1,0:T(8,128)S(1)}, f32[2,128,128]{2,1,0:T(8,128)S(1)}, u32[]{:S(2)}, u32[]{:S(2)}) collective-permute-start(f32[2,128,128]{2,1,0:T(8,128)S(1)} %get-tuple-element.30), channel_id=1, source_target_pairs={{0,4},{2,6},{4,0},{6,2},{8,12},{10,14},{12,8},{14,10},{16,20},{18,... | collective-permute-start | bytes 393224 | tf_op jit(solution)/shard_map/ppermute | solution.py:324
  6.3 1.3 %collective-permute-start.3 = (f32[2,128,128]{2,1,0:T(8,128)S(1)}, f32[2,128,128]{2,1,0:T(8,128)S(1)}, u32[]{:S(2)}, u32[]{:S(2)}) collective-permute-start(f32[2,128,128]{2,1,0:T(8,128)S(1)} %get-tuple-element.31), channel_id=1, source_target_pairs={{0,8},{2,10},{4,12},{6,14},{8,0},{10,2},{12,4},{14,6},{16,24},{18,... | collective-permute-start | bytes 393224 | tf_op jit(solution)/shard_map/ppermute | solution.py:324
  7.6 0.0 collective-permute-done.came
  7.6 0.4 %collective-permute-start.4 = (f32[2,128,128]{2,1,0:T(8,128)S(1)}, f32[2,128,128]{2,1,0:T(8,128)S(1)}, u32[]{:S(2)}, u32[]{:S(2)}) collective-permute-start(f32[2,128,128]{2,1,0:T(8,128)S(1)} %get-tuple-element.32), channel_id=1, source_target_pairs={{0,12},{2,14},{4,8},{6,10},{8,4},{10,6},{12,0},{14,2},{16,28},{18,... | collective-permute-start | bytes 393224 | tf_op jit(solution)/shard_map/ppermute | solution.py:324
  8.0 1.8 %collective-permute-done.2.refs_1_ = f32[2,128,128]{2,1,0:T(8,128)S(1)} collective-permute-done((f32[2,128,128]{2,1,0:T(8,128)S(1)}, f32[2,128,128]{2,1,0:T(8,128)S(1)}, u32[]{:S(2)}, u32[]{:S(2)}) %collective-permute-start.2) | collective-permute-done | bytes 131104 | tf_op jit(solution)/shard_map/ppermute | solution.py:324
  9.9 0.8 %collective-permute-done.3.refs_2_ = f32[2,128,128]{2,1,0:T(8,128)S(1)} collective-permute-done((f32[2,128,128]{2,1,0:T(8,128)S(1)}, f32[2,128,128]{2,1,0:T(8,128)S(1)}, u32[]{:S(2)}, u32[]{:S(2)}) %collective-permute-start.3) | collective-permute-done | bytes 131104 | tf_op jit(solution)/shard_map/ppermute | solution.py:324
  10.7 2.6 %collective-permute-done.4.refs_3_ = f32[2,128,128]{2,1,0:T(8,128)S(1)} collective-permute-done((f32[2,128,128]{2,1,0:T(8,128)S(1)}, f32[2,128,128]{2,1,0:T(8,128)S(1)}, u32[]{:S(2)}, u32[]{:S(2)}) %collective-permute-start.4) | collective-permute-done | bytes 131104 | tf_op jit(solution)/shard_map/ppermute | solution.py:324
  13.3 2.7 %collective-permute-start.5 = (f32[128,128]{1,0:T(8,128)S(1)}, f32[128,128]{1,0:T(8,128)S(1)}, u32[]{:S(2)}, u32[]{:S(2)}) collective-permute-start(f32[128,128]{1,0:T(8,128)S(1)} %fusion), channel_id=1, source_target_pairs={{0,16},{2,18},{4,20},{6,22},{8,24},{10,26},{12,28},{14,30},{16,0},... | collective-permute-start | bytes 196616 | tf_op jit(solution)/shard_map/ppermute | solution.py:324
  16.0 2.0 %shard_map.73 = (f32[8,256,128]{2,1,0:T(8,128)S(1)}, f32[8,256,128]{2,1,0:T(8,128)S(1)}, f32[8,256,128]{2,1,0:T(8,128)S(1)}) custom-call(bf16[8,256,128]{2,1,0:T(8,128)(2,1)S(1)} %copy-done.3, bf16[8,256,128]{2,1,0:T(8,128)(2,1)S(1)} %copy-done, bf16[8,256,128]{2,1,0:T(8,128)(2,1)S(1)} %copy-done.1, bf16[8,256,128]{2,1,0:T(8,128)(2,1)S(1)} %copy-done.2, ...), custom_call_target="tpu_custom_call" | custom-call | flops 805306368 | bytes 5242880 | tf_op jit(solution)/shard_map/pallas_call | solution.py:245
  18.1 0.0 collective-permute-done.5
  18.1 0.1 shard_map.77
  18.2 2.1 %collective-permute-start.8 = (f32[2,128,128]{2,1,0:T(8,128)S(1)}, f32[2,128,128]{2,1,0:T(8,128)S(1)}, u32[]{:S(2)}, u32[]{:S(2)}) collective-permute-start(f32[2,128,128]{2,1,0:T(8,128)S(1)} %shard_map.77), channel_id=1, source_target_pairs={{0,12},{2,14},{4,8},{6,10},{8,4},{10,6},{12,0},{14,2},{16,28},{18,... | collective-permute-start | bytes 393224 | tf_op jit(solution)/shard_map/ppermute | solution.py:324
  20.3 0.2 collective-permute-start.6
  20.6 0.5 %collective-permute-start.7 = (f32[2,128,128]{2,1,0:T(8,128)S(1)}, f32[2,128,128]{2,1,0:T(8,128)S(1)}, u32[]{:S(2)}, u32[]{:S(2)}) collective-permute-start(f32[2,128,128]{2,1,0:T(8,128)S(1)} %shard_map.75), channel_id=1, source_target_pairs={{0,4},{2,6},{4,0},{6,2},{8,12},{10,14},{12,8},{14,10},{16,20},{18,... | collective-permute-start | bytes 393224 | tf_op jit(solution)/shard_map/ppermute | solution.py:324
  21.1 1.8 %collective-permute-done.8.refs_5_ = f32[2,128,128]{2,1,0:T(8,128)S(1)} collective-permute-done((f32[2,128,128]{2,1,0:T(8,128)S(1)}, f32[2,128,128]{2,1,0:T(8,128)S(1)}, u32[]{:S(2)}, u32[]{:S(2)}) %collective-permute-start.8) | collective-permute-done | bytes 131104 | tf_op jit(solution)/shard_map/ppermute | solution.py:324
  23.0 3.7 %collective-permute-start.10 = (f32[2,2,128,128]{3,2,1,0:T(8,128)S(1)}, f32[2,2,128,128]{3,2,1,0:T(8,128)S(1)}, u32[]{:S(2)}, u32[]{:S(2)}) collective-permute-start(f32[2,2,128,128]{3,2,1,0:T(8,128)S(1)} %get-tuple-element.43), channel_id=1, source_target_pairs={{0,2},{2,0},{4,6},{6,4},{8,10},{10,8},{12,14},{14,12},{16,18},{18,... | collective-permute-start | bytes 786440 | tf_op jit(solution)/shard_map/ppermute | solution.py:324
  26.7 1.0 %shard_map.79 = (bf16[8,256,128]{2,1,0:T(8,128)(2,1)}, bf16[8,256,128]{2,1,0:T(8,128)(2,1)}, bf16[8,256,128]{2,1,0:T(8,128)(2,1)}, f32[8,128]{1,0:T(8,128)S(1)}) custom-call(bf16[8,256,128]{2,1,0:T(8,128)(2,1)S(1)} %copy-done, bf16[8,256,128]{2,1,0:T(8,128)(2,1)S(1)} %copy-done.1, bf16[8,256,128]{2,1,0:T(8,128)(2,1)S(1)} %copy-done.2, ...), custom_call_target="tpu_custom_call" | custom-call | flops 50331648 | bytes 393216 | tf_op jit(solution)/shard_map/pallas_call | solution.py:304
  27.7 0.0 collective-permute-done.6.refs_2_
  27.7 0.0 collective-permute-done.7.refs_5_
  27.7 0.1 shard_map.80
  27.7 0.9 %collective-permute-start.9 = (f32[2,2,128,128]{3,2,1,0:T(8,128)S(1)}, f32[2,2,128,128]{3,2,1,0:T(8,128)S(1)}, u32[]{:S(2)}, u32[]{:S(2)}) collective-permute-start(f32[2,2,128,128]{3,2,1,0:T(8,128)S(1)} %get-tuple-element.42), channel_id=1, source_target_pairs={{0,2},{2,0},{4,6},{6,4},{8,10},{10,8},{12,14},{14,12},{16,18},{18,... | collective-permute-start | bytes 786440 | tf_op jit(solution)/shard_map/ppermute | solution.py:324
  28.7 0.0 collective-permute-done.10.refs_0_
  28.7 1.2 %shard_map.81 = (bf16[8,256,128]{2,1,0:T(8,128)(2,1)}, bf16[8,256,128]{2,1,0:T(8,128)(2,1)}, bf16[8,256,128]{2,1,0:T(8,128)(2,1)}) custom-call(bf16[8,256,128]{2,1,0:T(8,128)(2,1)S(1)} %copy-done, bf16[8,256,128]{2,1,0:T(8,128)(2,1)S(1)} %copy-done.1, ...), custom_call_target="tpu_custom_call", output_to_operand_aliasing={{0}: (8, {}), {1}: (9, {}), {2}: (10, {})} | custom-call | flops 100663296 | bytes 786432 | tf_op jit(solution)/shard_map/pallas_call | solution.py:304
  29.8 0.0 collective-permute-done.9.refs_0_
  29.9 1.0 %shard_map.82 = (bf16[8,256,128]{2,1,0:T(8,128)(2,1)}, bf16[8,256,128]{2,1,0:T(8,128)(2,1)}, bf16[8,256,128]{2,1,0:T(8,128)(2,1)}) custom-call(bf16[8,256,128]{2,1,0:T(8,128)(2,1)S(1)} %copy-done, bf16[8,256,128]{2,1,0:T(8,128)(2,1)S(1)} %copy-done.1, bf16[8,256,128]{2,1,0:T(8,128)(2,1)S(1)} %copy-done.2, ...), custom_call_target="tpu_custom_call", output_to_operand_aliasing={{0}: (7, {}), {1}: (8, {}), {2}: (9, {})} | custom-call | flops 50331648 | bytes 393216 | tf_op jit(solution)/shard_map/pallas_call | solution.py:304
  (10 shorter events, 0.3 us)
Async XLA Ops:
  0.6 1.7 %copy-start = (bf16[8,256,128]{2,1,0:T(8,128)(2,1)S(1)}, bf16[8,256,128]{2,1,0:T(8,128)(2,1)}, u32[]{:S(2)}) copy-start(bf16[8,256,128]{2,1,0:T(8,128)(2,1)} %k.11) | copy-start | bytes 1572868
  0.6 1.7 %copy-start.1 = (bf16[8,256,128]{2,1,0:T(8,128)(2,1)S(1)}, bf16[8,256,128]{2,1,0:T(8,128)(2,1)}, u32[]{:S(2)}) copy-start(bf16[8,256,128]{2,1,0:T(8,128)(2,1)} %v.11) | copy-start | bytes 1572868
  0.7 1.7 %copy-start.2 = (bf16[8,256,128]{2,1,0:T(8,128)(2,1)S(1)}, bf16[8,256,128]{2,1,0:T(8,128)(2,1)}, u32[]{:S(2)}) copy-start(bf16[8,256,128]{2,1,0:T(8,128)(2,1)} %g.11) | copy-start | bytes 1572868
  0.7 1.7 %copy-start.3 = (bf16[8,256,128]{2,1,0:T(8,128)(2,1)S(1)}, bf16[8,256,128]{2,1,0:T(8,128)(2,1)}, u32[]{:S(2)}) copy-start(bf16[8,256,128]{2,1,0:T(8,128)(2,1)} %qs.1) | copy-start | bytes 1572868
  2.2 1.6 %collective-permute-start.1 = (f32[2,2,128,128]{3,2,1,0:T(8,128)S(1)}, f32[2,2,128,128]{3,2,1,0:T(8,128)S(1)}, u32[]{:S(2)}, u32[]{:S(2)}) collective-permute-start(f32[2,2,128,128]{3,2,1,0:T(8,128)S(1)} %shard_map.70), channel_id=1, source_target_pairs={{0,2},{2,0},{4,6},{6,4},{8,10},{10,8},{12,14},{14,12},{16,18},{18,... | collective-permute-start | bytes 786440 | tf_op jit(solution)/shard_map/ppermute | solution.py:324
  2.7 4.9 %collective-permute-start = (f32[2,2,128,128]{3,2,1,0:T(8,128)S(1)}, f32[2,2,128,128]{3,2,1,0:T(8,128)S(1)}, u32[]{:S(2)}, u32[]{:S(2)}) collective-permute-start(f32[2,2,128,128]{3,2,1,0:T(8,128)S(1)} %shard_map.67), channel_id=1, source_target_pairs={{0,2},{2,0},{4,6},{6,4},{8,10},{10,8},{12,14},{14,12},{16,18},{18,... | collective-permute-start | bytes 786440 | tf_op jit(solution)/shard_map/ppermute | solution.py:324
  3.9 6.0 %collective-permute-start.2 = (f32[2,128,128]{2,1,0:T(8,128)S(1)}, f32[2,128,128]{2,1,0:T(8,128)S(1)}, u32[]{:S(2)}, u32[]{:S(2)}) collective-permute-start(f32[2,128,128]{2,1,0:T(8,128)S(1)} %get-tuple-element.30), channel_id=1, source_target_pairs={{0,4},{2,6},{4,0},{6,2},{8,12},{10,14},{12,8},{14,10},{16,20},{18,... | collective-permute-start | bytes 393224 | tf_op jit(solution)/shard_map/ppermute | solution.py:324
  6.3 4.4 %collective-permute-start.3 = (f32[2,128,128]{2,1,0:T(8,128)S(1)}, f32[2,128,128]{2,1,0:T(8,128)S(1)}, u32[]{:S(2)}, u32[]{:S(2)}) collective-permute-start(f32[2,128,128]{2,1,0:T(8,128)S(1)} %get-tuple-element.31), channel_id=1, source_target_pairs={{0,8},{2,10},{4,12},{6,14},{8,0},{10,2},{12,4},{14,6},{16,24},{18,... | collective-permute-start | bytes 393224 | tf_op jit(solution)/shard_map/ppermute | solution.py:324
  7.6 5.6 %collective-permute-start.4 = (f32[2,128,128]{2,1,0:T(8,128)S(1)}, f32[2,128,128]{2,1,0:T(8,128)S(1)}, u32[]{:S(2)}, u32[]{:S(2)}) collective-permute-start(f32[2,128,128]{2,1,0:T(8,128)S(1)} %get-tuple-element.32), channel_id=1, source_target_pairs={{0,12},{2,14},{4,8},{6,10},{8,4},{10,6},{12,0},{14,2},{16,28},{18,... | collective-permute-start | bytes 393224 | tf_op jit(solution)/shard_map/ppermute | solution.py:324
  13.3 4.7 %collective-permute-start.5 = (f32[128,128]{1,0:T(8,128)S(1)}, f32[128,128]{1,0:T(8,128)S(1)}, u32[]{:S(2)}, u32[]{:S(2)}) collective-permute-start(f32[128,128]{1,0:T(8,128)S(1)} %fusion), channel_id=1, source_target_pairs={{0,16},{2,18},{4,20},{6,22},{8,24},{10,26},{12,28},{14,30},{16,0},... | collective-permute-start | bytes 196616 | tf_op jit(solution)/shard_map/ppermute | solution.py:324
  18.2 4.8 %collective-permute-start.8 = (f32[2,128,128]{2,1,0:T(8,128)S(1)}, f32[2,128,128]{2,1,0:T(8,128)S(1)}, u32[]{:S(2)}, u32[]{:S(2)}) collective-permute-start(f32[2,128,128]{2,1,0:T(8,128)S(1)} %shard_map.77), channel_id=1, source_target_pairs={{0,12},{2,14},{4,8},{6,10},{8,4},{10,6},{12,0},{14,2},{16,28},{18,... | collective-permute-start | bytes 393224 | tf_op jit(solution)/shard_map/ppermute | solution.py:324
  20.3 7.3 %collective-permute-start.6 = (f32[2,128,128]{2,1,0:T(8,128)S(1)}, f32[2,128,128]{2,1,0:T(8,128)S(1)}, u32[]{:S(2)}, u32[]{:S(2)}) collective-permute-start(f32[2,128,128]{2,1,0:T(8,128)S(1)} %shard_map.74), channel_id=1, source_target_pairs={{0,8},{2,10},{4,12},{6,14},{8,0},{10,2},{12,4},{14,6},{16,24},{18,... | collective-permute-start | bytes 393224 | tf_op jit(solution)/shard_map/ppermute | solution.py:324
  20.6 7.0 %collective-permute-start.7 = (f32[2,128,128]{2,1,0:T(8,128)S(1)}, f32[2,128,128]{2,1,0:T(8,128)S(1)}, u32[]{:S(2)}, u32[]{:S(2)}) collective-permute-start(f32[2,128,128]{2,1,0:T(8,128)S(1)} %shard_map.75), channel_id=1, source_target_pairs={{0,4},{2,6},{4,0},{6,2},{8,12},{10,14},{12,8},{14,10},{16,20},{18,... | collective-permute-start | bytes 393224 | tf_op jit(solution)/shard_map/ppermute | solution.py:324
  23.0 5.7 %collective-permute-start.10 = (f32[2,2,128,128]{3,2,1,0:T(8,128)S(1)}, f32[2,2,128,128]{3,2,1,0:T(8,128)S(1)}, u32[]{:S(2)}, u32[]{:S(2)}) collective-permute-start(f32[2,2,128,128]{3,2,1,0:T(8,128)S(1)} %get-tuple-element.43), channel_id=1, source_target_pairs={{0,2},{2,0},{4,6},{6,4},{8,10},{10,8},{12,14},{14,12},{16,18},{18,... | collective-permute-start | bytes 786440 | tf_op jit(solution)/shard_map/ppermute | solution.py:324
  27.7 2.1 %collective-permute-start.9 = (f32[2,2,128,128]{3,2,1,0:T(8,128)S(1)}, f32[2,2,128,128]{3,2,1,0:T(8,128)S(1)}, u32[]{:S(2)}, u32[]{:S(2)}) collective-permute-start(f32[2,2,128,128]{3,2,1,0:T(8,128)S(1)} %get-tuple-element.42), channel_id=1, source_target_pairs={{0,2},{2,0},{4,6},{6,4},{8,10},{10,8},{12,14},{14,12},{16,18},{18,... | collective-permute-start | bytes 786440 | tf_op jit(solution)/shard_map/ppermute | solution.py:324

commit v8 on v7

--- a/solution.py
+++ b/solution.py
@@ -94,19 +94,27 @@
     return lax.dot_general(a, b, (((da,), (db,)), ((), ())), preferred_element_type=F32)
 
 
-def place_of(slots):
+def turned(slot, group):
+    return (group - slot) & (group - 1)
+
+
+def place_of(group):
     index = lax.axis_index("seq")
-    return index & 1, (index >> 1) & (slots - 1)
+    return index & 1, (index >> 1) & (group - 1)
+
+
+def partner(core, rank, slot, group):
+    return rank ^ (slot + core * (turned(slot, group) - slot))
 
 
 def away_kernel(q, k, v, g, out, qs, ks, vs, gs, sems, *, part):
     slots = q.shape[0] // 2
     core, rank = place_of(slots)
-    first = (1 - core) * slots
+    core = 1 - core
     copies = []
     for n, (there, here) in enumerate(((k, ks), (v, vs), (q, qs), (g, gs))):
         for m, slot in enumerate(part):
-            head = first + (rank ^ slot)
+            head = core * slots + partner(core, rank, slot, slots)
             copies.append(pltpu.make_async_copy(there.at[head], here.at[m], sems.at[n, m]))
             copies[-1].start()
     for copy in copies:
@@ -119,10 +127,10 @@
 def near_kernel(q, k, v, g, *outs, parts, other):
     slots = q.shape[0] // 2
     core, rank = place_of(slots)
-    first = (1 - core if other else core) * slots
+    core = 1 - core if other else core
     for out, part in zip(outs, parts):
         for m, slot in enumerate(part):
-            head = first + (rank ^ slot)
+            head = core * slots + partner(core, rank, slot, slots)
             out[m, 0] = dot(k[head], v[head], 0, 0)
             out[m, 1] = dot(q[head], g[head], 0, 0)
 
@@ -181,11 +189,12 @@
 
 def outside_kernel(after, carry, *refs, slot, group):
     out = refs[-1]
-    _, rank = place_of(group)
+    core, rank = place_of(group)
     earlier, later = carry[0], carry[1]
+    there = partner(core, rank, slot, group)
     for i in range(group):
         if i != slot:
-            before = (rank ^ i) < (rank ^ slot)
+            before = partner(core, rank, i, group) < there
             earlier = earlier + jnp.where(before, refs[i][0], 0.0)
             later = later + jnp.where(before, 0.0, refs[i][1])
     out[0] = earlier
@@ -283,10 +292,10 @@
     core, rank = place_of(half)
     copies = []
     for state, (other, slots) in zip(refs, pieces):
-        first = (1 - core if other else core) * half
+        side = 1 - core if other else core
         for i, slot in enumerate(slots):
             earlier, later = state[i, 0].astype(BF16), state[i, 1].astype(BF16)
-            head, n = first + (rank ^ slot), len(copies) // 3
+            head, n = side * half + partner(side, rank, slot, half), len(copies) // 3
             bq[n] = (lq[head] + dot(g[head], earlier, 1, 1)).astype(BF16)
             bk[n] = (lk[head] + dot(v[head], later, 1, 1)).astype(BF16)
             bv[n] = (lv[head] + dot(k[head], later, 1, 0)).astype(BF16)
@@ -322,6 +331,12 @@
 def swap(x, mask):
     count = lax.axis_size("seq")
     return lax.ppermute(x, "seq", [(i, i ^ mask) for i in range(count)])
+
+
+def swap_slot(x, slot, group):
+    count = lax.axis_size("seq")
+    masks = (2 * slot, 2 * turned(slot, group))
+    return lax.ppermute(x, "seq", [(i, i ^ masks[i & 1]) for i in range(count)])
 
 
 def sliced_body(group):
@@ -340,7 +355,7 @@
             for n, j in enumerate(part):
                 total[j], inner[j], outer[j] = sums[n], (into, n), (from_here, n)
 
-        held = [total[0]] + [swap(total[j], 2 * j) for j in range(1, group)]
+        held = [total[0]] + [swap_slot(total[j], j, group) for j in range(1, group)]
 
         block = block_sum(held)
         parts = local_parts(data, block)
@@ -361,7 +376,7 @@
             bit *= 2
 
         around = [outside_of(carry, held, j, parts[0]) for j in range(group)]
-        around = [swap(x, 2 * j) if j else x for j, x in enumerate(around)]
+        around = [swap_slot(x, j, group) if j else x for j, x in enumerate(around)]
         soon, late = (0, group - 1), tuple(range(group - 2, 0, -1))
         mine, theirs = shares_of(inner, outer, around, soon)
         other = swap(theirs, 1)

time: 31.3 us -> 31 us (level)
  waiting for transfers between devices: 7.35 us -> 6.42 us
  starting transfers between devices: 14.9 us -> 15.6 us
    ppermute x11 -> x5, waiting for transfers between devices: 7.35 us -> 0.32 us  [swap(): return lax.ppermute(x, 'seq', [(i, i ^ mask) for i in range(count)])]
    ppermute x0 -> x6, starting transfers between devices: none -> 6.69 us  [swap_slot(): return lax.ppermute(x, 'seq', [(i, i ^ masks[i & 1]) for i in range(count)])]
    ppermute x0 -> x6, waiting for transfers between devices: none -> 6.11 us  [swap_slot(): return lax.ppermute(x, 'seq', [(i, i ^ masks[i & 1]) for i in range(count)])]
    ppermute x11 -> x5, starting transfers between devices: 14.9 us -> 8.89 us  [swap(): return lax.ppermute(x, 'seq', [(i, i ^ mask) for i in range(count)])]
  transfers between devices with their start and end apart: 11 -> 11, of which waited for: 5 -> 4; matrix products, arithmetic and copies ran while one was open for 0% -> 0% of each run, Pallas kernels for 17% -> 17%
where the time goes in v8:
time: 31 us; the launch traced here: 30.6 us
  starting transfers between devices  15.6 us (50%)
  Pallas kernels  7.71 us (25%)
  waiting for transfers between devices  6.42 us (21%)
  between operations  0.81 us (3%)
    ppermute x5, starting transfers between devices, swap(): return lax.ppermute(x, 'seq', [(i, i ^ mask) for i in range(count)])  8.89 us
    ppermute x6, starting transfers between devices, swap_slot(): return lax.ppermute(x, 'seq', [(i, i ^ masks[i & 1]) for i in range(count)])  6.69 us
    ppermute x6, waiting for transfers between devices, swap_slot(): return lax.ppermute(x, 'seq', [(i, i ^ masks[i & 1]) for i in range(count)])  6.11 us
    pallas_call x3, Pallas kernels, final_sums(): pl.pallas_call(functools.partial(final_kernel, pieces=pieces, given=len(f...  3.15 us
    pallas_call x3, Pallas kernels, state_call(): pl.pallas_call(kernel, out_shape=[pltpu.VMEM((len(part), 2, width, width)...  2.17 us
    pallas_call x1, Pallas kernels, local_parts(): pl.pallas_call(local_kernel, out_shape=[pltpu.VMEM(data[0].shape, F32)] *...  2.02 us
  transfers between devices with their start and end apart: 11, of which 4 were waited for; matrix products, arithmetic and copies ran while one was open for 0% of the time, Pallas kernels for 17%

profile of v8, /device:TPU:1, one launch (start us, length us, event | category | flops | bytes accessed | tf_op | source)
XLA Modules:
  0.0 30.6 jit_solution(9991611655443661790)
XLA Ops:
  0.6 0.0 copy-start
  0.6 0.0 copy-start.1
  0.7 0.0 copy-start.2
  0.7 0.0 copy-start.3
  0.7 1.6 %shard_map.70 = f32[2,2,128,128]{3,2,1,0:T(8,128)S(1)} custom-call(bf16[8,256,128]{2,1,0:T(8,128)(2,1)} %qs.1, bf16[8,256,128]{2,1,0:T(8,128)(2,1)} %k.11, bf16[8,256,128]{2,1,0:T(8,128)(2,1)} %v.11, bf16[8,256,128]{2,1,0:T(8,128)(2,1)} %g.11), custom_call_target="tpu_custom_call" | custom-call | flops 33554432 | bytes 524288 | tf_op jit(solution)/shard_map/pallas_call | solution.py:141
  2.2 0.1 collective-permute-start.1
  2.4 0.0 copy-done
  2.4 0.0 copy-done.1
  2.4 0.0 copy-done.2
  2.4 0.0 copy-done.3
  2.4 0.3 shard_map.67
  2.7 0.5 %collective-permute-start = (f32[2,2,128,128]{3,2,1,0:T(8,128)S(1)}, f32[2,2,128,128]{3,2,1,0:T(8,128)S(1)}, u32[]{:S(2)}, u32[]{:S(2)}) collective-permute-start(f32[2,2,128,128]{3,2,1,0:T(8,128)S(1)} %shard_map.67), channel_id=1, source_target_pairs={{0,2},{2,0},{4,6},{6,4},{8,10},{10,8},{12,14},{14,12},{16,18},{18,... | collective-permute-start | bytes 786440 | tf_op jit(solution)/shard_map/ppermute | solution.py:333
  3.2 0.3 %shard_map.68 = (f32[2,2,128,128]{3,2,1,0:T(8,128)S(1)}, f32[2,2,128,128]{3,2,1,0:T(8,128)S(1)}) custom-call(bf16[8,256,128]{2,1,0:T(8,128)(2,1)S(1)} %copy-done.3, bf16[8,256,128]{2,1,0:T(8,128)(2,1)S(1)} %copy-done, bf16[8,256,128]{2,1,0:T(8,128)(2,1)S(1)} %copy-done.1, bf16[8,256,128]{2,1,0:T(8,128)(2,1)S(1)} %copy-done.2), custom_call_target="tpu_custom_call" | custom-call | flops 67108864 | bytes 1048576 | tf_op jit(solution)/shard_map/pallas_call | solution.py:141
  3.5 0.3 collective-permute-done.1.came
  3.9 3.4 %collective-permute-start.2 = (f32[2,128,128]{2,1,0:T(8,128)S(1)}, f32[2,128,128]{2,1,0:T(8,128)S(1)}, u32[]{:S(2)}, u32[]{:S(2)}) collective-permute-start(f32[2,128,128]{2,1,0:T(8,128)S(1)} %get-tuple-element.30), channel_id=1, source_target_pairs={{0,4},{2,14},{4,0},{6,10},{8,12},{10,6},{12,8},{14,2},{16,20},{18,... | collective-permute-start | bytes 393224 | tf_op jit(solution)/shard_map/ppermute | solution.py:339
  7.3 0.2 collective-permute-start.3
  7.5 0.0 collective-permute-done.came
  7.5 0.3 collective-permute-start.4
  7.8 2.3 %collective-permute-done.2.refs_1_ = f32[2,128,128]{2,1,0:T(8,128)S(1)} collective-permute-done((f32[2,128,128]{2,1,0:T(8,128)S(1)}, f32[2,128,128]{2,1,0:T(8,128)S(1)}, u32[]{:S(2)}, u32[]{:S(2)}) %collective-permute-start.2) | collective-permute-done | bytes 131104 | tf_op jit(solution)/shard_map/ppermute | solution.py:339
  10.1 2.9 %collective-permute-done.3.refs_2_ = f32[2,128,128]{2,1,0:T(8,128)S(1)} collective-permute-done((f32[2,128,128]{2,1,0:T(8,128)S(1)}, f32[2,128,128]{2,1,0:T(8,128)S(1)}, u32[]{:S(2)}, u32[]{:S(2)}) %collective-permute-start.3) | collective-permute-done | bytes 131104 | tf_op jit(solution)/shard_map/ppermute | solution.py:339
  13.0 0.0 collective-permute-done.4.refs_3_
  13.0 2.4 %collective-permute-start.5 = (f32[128,128]{1,0:T(8,128)S(1)}, f32[128,128]{1,0:T(8,128)S(1)}, u32[]{:S(2)}, u32[]{:S(2)}) collective-permute-start(f32[128,128]{1,0:T(8,128)S(1)} %fusion), channel_id=1, source_target_pairs={{0,16},{2,18},{4,20},{6,22},{8,24},{10,26},{12,28},{14,30},{16,0},... | collective-permute-start | bytes 196616 | tf_op jit(solution)/shard_map/ppermute | solution.py:333
  15.4 2.0 %shard_map.73 = (f32[8,256,128]{2,1,0:T(8,128)S(1)}, f32[8,256,128]{2,1,0:T(8,128)S(1)}, f32[8,256,128]{2,1,0:T(8,128)S(1)}) custom-call(bf16[8,256,128]{2,1,0:T(8,128)(2,1)S(1)} %copy-done.3, bf16[8,256,128]{2,1,0:T(8,128)(2,1)S(1)} %copy-done, bf16[8,256,128]{2,1,0:T(8,128)(2,1)S(1)} %copy-done.1, bf16[8,256,128]{2,1,0:T(8,128)(2,1)S(1)} %copy-done.2, ...), custom_call_target="tpu_custom_call" | custom-call | flops 805306368 | bytes 5242880 | tf_op jit(solution)/shard_map/pallas_call | solution.py:254
  17.4 0.0 collective-permute-done.5
  17.5 0.1 shard_map.77
  17.5 1.0 %collective-permute-start.8 = (f32[2,128,128]{2,1,0:T(8,128)S(1)}, f32[2,128,128]{2,1,0:T(8,128)S(1)}, u32[]{:S(2)}, u32[]{:S(2)}) collective-permute-start(f32[2,128,128]{2,1,0:T(8,128)S(1)} %shard_map.77), channel_id=1, source_target_pairs={{0,12},{2,6},{4,8},{6,2},{8,4},{10,14},{12,0},{14,10},{16,28},{18,... | collective-permute-start | bytes 393224 | tf_op jit(solution)/shard_map/ppermute | solution.py:339
  18.5 1.4 %collective-permute-start.6 = (f32[2,128,128]{2,1,0:T(8,128)S(1)}, f32[2,128,128]{2,1,0:T(8,128)S(1)}, u32[]{:S(2)}, u32[]{:S(2)}) collective-permute-start(f32[2,128,128]{2,1,0:T(8,128)S(1)} %shard_map.74), channel_id=1, source_target_pairs={{0,8},{2,10},{4,12},{6,14},{8,0},{10,2},{12,4},{14,6},{16,24},{18,... | collective-permute-start | bytes 393224 | tf_op jit(solution)/shard_map/ppermute | solution.py:339
  19.9 0.5 %collective-permute-start.7 = (f32[2,128,128]{2,1,0:T(8,128)S(1)}, f32[2,128,128]{2,1,0:T(8,128)S(1)}, u32[]{:S(2)}, u32[]{:S(2)}) collective-permute-start(f32[2,128,128]{2,1,0:T(8,128)S(1)} %shard_map.75), channel_id=1, source_target_pairs={{0,4},{2,14},{4,0},{6,10},{8,12},{10,6},{12,8},{14,2},{16,20},{18,... | collective-permute-start | bytes 393224 | tf_op jit(solution)/shard_map/ppermute | solution.py:339
  20.5 0.9 %collective-permute-done.8.refs_5_ = f32[2,128,128]{2,1,0:T(8,128)S(1)} collective-permute-done((f32[2,128,128]{2,1,0:T(8,128)S(1)}, f32[2,128,128]{2,1,0:T(8,128)S(1)}, u32[]{:S(2)}, u32[]{:S(2)}) %collective-permute-start.8) | collective-permute-done | bytes 131104 | tf_op jit(solution)/shard_map/ppermute | solution.py:339
  21.5 5.5 %collective-permute-start.10 = (f32[2,2,128,128]{3,2,1,0:T(8,128)S(1)}, f32[2,2,128,128]{3,2,1,0:T(8,128)S(1)}, u32[]{:S(2)}, u32[]{:S(2)}) collective-permute-start(f32[2,2,128,128]{3,2,1,0:T(8,128)S(1)} %get-tuple-element.43), channel_id=1, source_target_pairs={{0,2},{2,0},{4,6},{6,4},{8,10},{10,8},{12,14},{14,12},{16,18},{18,... | collective-permute-start | bytes 786440 | tf_op jit(solution)/shard_map/ppermute | solution.py:333
  26.9 1.0 %shard_map.79 = (bf16[8,256,128]{2,1,0:T(8,128)(2,1)}, bf16[8,256,128]{2,1,0:T(8,128)(2,1)}, bf16[8,256,128]{2,1,0:T(8,128)(2,1)}, f32[8,128]{1,0:T(8,128)S(1)}) custom-call(bf16[8,256,128]{2,1,0:T(8,128)(2,1)S(1)} %copy-done, bf16[8,256,128]{2,1,0:T(8,128)(2,1)S(1)} %copy-done.1, bf16[8,256,128]{2,1,0:T(8,128)(2,1)S(1)} %copy-done.2, ...), custom_call_target="tpu_custom_call" | custom-call | flops 50331648 | bytes 393216 | tf_op jit(solution)/shard_map/pallas_call | solution.py:313
  27.9 0.0 collective-permute-done.6.refs_2_
  27.9 0.0 collective-permute-done.7.refs_5_
  28.0 0.1 shard_map.80
  28.0 0.4 %collective-permute-start.9 = (f32[2,2,128,128]{3,2,1,0:T(8,128)S(1)}, f32[2,2,128,128]{3,2,1,0:T(8,128)S(1)}, u32[]{:S(2)}, u32[]{:S(2)}) collective-permute-start(f32[2,2,128,128]{3,2,1,0:T(8,128)S(1)} %get-tuple-element.42), channel_id=1, source_target_pairs={{0,2},{2,0},{4,6},{6,4},{8,10},{10,8},{12,14},{14,12},{16,18},{18,... | collective-permute-start | bytes 786440 | tf_op jit(solution)/shard_map/ppermute | solution.py:333
  28.4 0.0 collective-permute-done.10.refs_0_
  28.4 1.2 %shard_map.81 = (bf16[8,256,128]{2,1,0:T(8,128)(2,1)}, bf16[8,256,128]{2,1,0:T(8,128)(2,1)}, bf16[8,256,128]{2,1,0:T(8,128)(2,1)}) custom-call(bf16[8,256,128]{2,1,0:T(8,128)(2,1)S(1)} %copy-done, bf16[8,256,128]{2,1,0:T(8,128)(2,1)S(1)} %copy-done.1, ...), custom_call_target="tpu_custom_call", output_to_operand_aliasing={{0}: (8, {}), {1}: (9, {}), {2}: (10, {})} | custom-call | flops 100663296 | bytes 786432 | tf_op jit(solution)/shard_map/pallas_call | solution.py:313
  29.6 0.0 collective-permute-done.9.refs_0_
  29.6 1.0 %shard_map.82 = (bf16[8,256,128]{2,1,0:T(8,128)(2,1)}, bf16[8,256,128]{2,1,0:T(8,128)(2,1)}, bf16[8,256,128]{2,1,0:T(8,128)(2,1)}) custom-call(bf16[8,256,128]{2,1,0:T(8,128)(2,1)S(1)} %copy-done, bf16[8,256,128]{2,1,0:T(8,128)(2,1)S(1)} %copy-done.1, bf16[8,256,128]{2,1,0:T(8,128)(2,1)S(1)} %copy-done.2, ...), custom_call_target="tpu_custom_call", output_to_operand_aliasing={{0}: (7, {}), {1}: (8, {}), {2}: (9, {})} | custom-call | flops 50331648 | bytes 393216 | tf_op jit(solution)/shard_map/pallas_call | solution.py:313
  (10 shorter events, 0.3 us)
Async XLA Ops:
  0.6 1.7 %copy-start = (bf16[8,256,128]{2,1,0:T(8,128)(2,1)S(1)}, bf16[8,256,128]{2,1,0:T(8,128)(2,1)}, u32[]{:S(2)}) copy-start(bf16[8,256,128]{2,1,0:T(8,128)(2,1)} %k.11) | copy-start | bytes 1572868
  0.6 1.7 %copy-start.1 = (bf16[8,256,128]{2,1,0:T(8,128)(2,1)S(1)}, bf16[8,256,128]{2,1,0:T(8,128)(2,1)}, u32[]{:S(2)}) copy-start(bf16[8,256,128]{2,1,0:T(8,128)(2,1)} %v.11) | copy-start | bytes 1572868
  0.7 1.7 %copy-start.2 = (bf16[8,256,128]{2,1,0:T(8,128)(2,1)S(1)}, bf16[8,256,128]{2,1,0:T(8,128)(2,1)}, u32[]{:S(2)}) copy-start(bf16[8,256,128]{2,1,0:T(8,128)(2,1)} %g.11) | copy-start | bytes 1572868
  0.7 1.7 %copy-start.3 = (bf16[8,256,128]{2,1,0:T(8,128)(2,1)S(1)}, bf16[8,256,128]{2,1,0:T(8,128)(2,1)}, u32[]{:S(2)}) copy-start(bf16[8,256,128]{2,1,0:T(8,128)(2,1)} %qs.1) | copy-start | bytes 1572868
  2.2 1.6 %collective-permute-start.1 = (f32[2,2,128,128]{3,2,1,0:T(8,128)S(1)}, f32[2,2,128,128]{3,2,1,0:T(8,128)S(1)}, u32[]{:S(2)}, u32[]{:S(2)}) collective-permute-start(f32[2,2,128,128]{3,2,1,0:T(8,128)S(1)} %shard_map.70), channel_id=1, source_target_pairs={{0,2},{2,0},{4,6},{6,4},{8,10},{10,8},{12,14},{14,12},{16,18},{18,... | collective-permute-start | bytes 786440 | tf_op jit(solution)/shard_map/ppermute | solution.py:333
  2.7 4.8 %collective-permute-start = (f32[2,2,128,128]{3,2,1,0:T(8,128)S(1)}, f32[2,2,128,128]{3,2,1,0:T(8,128)S(1)}, u32[]{:S(2)}, u32[]{:S(2)}) collective-permute-start(f32[2,2,128,128]{3,2,1,0:T(8,128)S(1)} %shard_map.67), channel_id=1, source_target_pairs={{0,2},{2,0},{4,6},{6,4},{8,10},{10,8},{12,14},{14,12},{16,18},{18,... | collective-permute-start | bytes 786440 | tf_op jit(solution)/shard_map/ppermute | solution.py:333
  3.9 6.2 %collective-permute-start.2 = (f32[2,128,128]{2,1,0:T(8,128)S(1)}, f32[2,128,128]{2,1,0:T(8,128)S(1)}, u32[]{:S(2)}, u32[]{:S(2)}) collective-permute-start(f32[2,128,128]{2,1,0:T(8,128)S(1)} %get-tuple-element.30), channel_id=1, source_target_pairs={{0,4},{2,14},{4,0},{6,10},{8,12},{10,6},{12,8},{14,2},{16,20},{18,... | collective-permute-start | bytes 393224 | tf_op jit(solution)/shard_map/ppermute | solution.py:339
  7.3 5.7 %collective-permute-start.3 = (f32[2,128,128]{2,1,0:T(8,128)S(1)}, f32[2,128,128]{2,1,0:T(8,128)S(1)}, u32[]{:S(2)}, u32[]{:S(2)}) collective-permute-start(f32[2,128,128]{2,1,0:T(8,128)S(1)} %get-tuple-element.31), channel_id=1, source_target_pairs={{0,8},{2,10},{4,12},{6,14},{8,0},{10,2},{12,4},{14,6},{16,24},{18,... | collective-permute-start | bytes 393224 | tf_op jit(solution)/shard_map/ppermute | solution.py:339
  7.5 5.4 %collective-permute-start.4 = (f32[2,128,128]{2,1,0:T(8,128)S(1)}, f32[2,128,128]{2,1,0:T(8,128)S(1)}, u32[]{:S(2)}, u32[]{:S(2)}) collective-permute-start(f32[2,128,128]{2,1,0:T(8,128)S(1)} %get-tuple-element.32), channel_id=1, source_target_pairs={{0,12},{2,6},{4,8},{6,2},{8,4},{10,14},{12,0},{14,10},{16,28},{18,... | collective-permute-start | bytes 393224 | tf_op jit(solution)/shard_map/ppermute | solution.py:339
  13.0 4.4 %collective-permute-start.5 = (f32[128,128]{1,0:T(8,128)S(1)}, f32[128,128]{1,0:T(8,128)S(1)}, u32[]{:S(2)}, u32[]{:S(2)}) collective-permute-start(f32[128,128]{1,0:T(8,128)S(1)} %fusion), channel_id=1, source_target_pairs={{0,16},{2,18},{4,20},{6,22},{8,24},{10,26},{12,28},{14,30},{16,0},... | collective-permute-start | bytes 196616 | tf_op jit(solution)/shard_map/ppermute | solution.py:333
  17.5 3.9 %collective-permute-start.8 = (f32[2,128,128]{2,1,0:T(8,128)S(1)}, f32[2,128,128]{2,1,0:T(8,128)S(1)}, u32[]{:S(2)}, u32[]{:S(2)}) collective-permute-start(f32[2,128,128]{2,1,0:T(8,128)S(1)} %shard_map.77), channel_id=1, source_target_pairs={{0,12},{2,6},{4,8},{6,2},{8,4},{10,14},{12,0},{14,10},{16,28},{18,... | collective-permute-start | bytes 393224 | tf_op jit(solution)/shard_map/ppermute | solution.py:339
  18.5 9.4 %collective-permute-start.6 = (f32[2,128,128]{2,1,0:T(8,128)S(1)}, f32[2,128,128]{2,1,0:T(8,128)S(1)}, u32[]{:S(2)}, u32[]{:S(2)}) collective-permute-start(f32[2,128,128]{2,1,0:T(8,128)S(1)} %shard_map.74), channel_id=1, source_target_pairs={{0,8},{2,10},{4,12},{6,14},{8,0},{10,2},{12,4},{14,6},{16,24},{18,... | collective-permute-start | bytes 393224 | tf_op jit(solution)/shard_map/ppermute | solution.py:339
  19.9 8.0 %collective-permute-start.7 = (f32[2,128,128]{2,1,0:T(8,128)S(1)}, f32[2,128,128]{2,1,0:T(8,128)S(1)}, u32[]{:S(2)}, u32[]{:S(2)}) collective-permute-start(f32[2,128,128]{2,1,0:T(8,128)S(1)} %shard_map.75), channel_id=1, source_target_pairs={{0,4},{2,14},{4,0},{6,10},{8,12},{10,6},{12,8},{14,2},{16,20},{18,... | collective-permute-start | bytes 393224 | tf_op jit(solution)/shard_map/ppermute | solution.py:339
  21.5 7.0 %collective-permute-start.10 = (f32[2,2,128,128]{3,2,1,0:T(8,128)S(1)}, f32[2,2,128,128]{3,2,1,0:T(8,128)S(1)}, u32[]{:S(2)}, u32[]{:S(2)}) collective-permute-start(f32[2,2,128,128]{3,2,1,0:T(8,128)S(1)} %get-tuple-element.43), channel_id=1, source_target_pairs={{0,2},{2,0},{4,6},{6,4},{8,10},{10,8},{12,14},{14,12},{16,18},{18,... | collective-permute-start | bytes 786440 | tf_op jit(solution)/shard_map/ppermute | solution.py:333
  28.0 1.6 %collective-permute-start.9 = (f32[2,2,128,128]{3,2,1,0:T(8,128)S(1)}, f32[2,2,128,128]{3,2,1,0:T(8,128)S(1)}, u32[]{:S(2)}, u32[]{:S(2)}) collective-permute-start(f32[2,2,128,128]{3,2,1,0:T(8,128)S(1)} %get-tuple-element.42), channel_id=1, source_target_pairs={{0,2},{2,0},{4,6},{6,4},{8,10},{10,8},{12,14},{14,12},{16,18},{18,... | collective-permute-start | bytes 786440 | tf_op jit(solution)/shard_map/ppermute | solution.py:333

commit v9 on v8

--- a/solution.py
+++ b/solution.py
@@ -117,10 +117,13 @@
             head = core * slots + partner(core, rank, slot, slots)
             copies.append(pltpu.make_async_copy(there.at[head], here.at[m], sems.at[n, m]))
             copies[-1].start()
-    for copy in copies:
+    for copy in copies[: 2 * len(part)]:
         copy.wait()
     for m in range(len(part)):
         out[m, 0] = dot(ks[m], vs[m], 0, 0)
+    for copy in copies[2 * len(part) :]:
+        copy.wait()
+    for m in range(len(part)):
         out[m, 1] = dot(qs[m], gs[m], 0, 0)
 
 

time: 31 us -> 31.1 us (level)
  no operation moved by 1% of the time
where the time goes in v9:
time: 31.1 us; the launch traced here: 30.7 us
  starting transfers between devices  15.6 us (50%)
  Pallas kernels  7.79 us (25%)
  waiting for transfers between devices  6.42 us (21%)
  between operations  0.81 us (3%)
    ppermute x5, starting transfers between devices, swap(): return lax.ppermute(x, 'seq', [(i, i ^ mask) for i in range(count)])  8.91 us
    ppermute x6, starting transfers between devices, swap_slot(): return lax.ppermute(x, 'seq', [(i, i ^ masks[i & 1]) for i in range(count)])  6.69 us
    ppermute x6, waiting for transfers between devices, swap_slot(): return lax.ppermute(x, 'seq', [(i, i ^ masks[i & 1]) for i in range(count)])  6.11 us
    pallas_call x3, Pallas kernels, final_sums(): pl.pallas_call(functools.partial(final_kernel, pieces=pieces, given=len(f...  3.15 us
    pallas_call x3, Pallas kernels, state_call(): pl.pallas_call(kernel, out_shape=[pltpu.VMEM((len(part), 2, width, width)...  2.25 us
    pallas_call x1, Pallas kernels, local_parts(): pl.pallas_call(local_kernel, out_shape=[pltpu.VMEM(data[0].shape, F32)] *...  2.02 us
  transfers between devices with their start and end apart: 11, of which 4 were waited for; matrix products, arithmetic and copies ran while one was open for 0% of the time, Pallas kernels for 17%

profile of v9, /device:TPU:1, one launch (start us, length us, event | category | flops | bytes accessed | tf_op | source)
XLA Modules:
  0.0 30.7 jit_solution(9918376678434197137)
XLA Ops:
  0.6 0.0 copy-start
  0.6 0.0 copy-start.1
  0.7 0.0 copy-start.2
  0.7 0.0 copy-start.3
  0.7 1.6 %shard_map.70 = f32[2,2,128,128]{3,2,1,0:T(8,128)S(1)} custom-call(bf16[8,256,128]{2,1,0:T(8,128)(2,1)} %qs.1, bf16[8,256,128]{2,1,0:T(8,128)(2,1)} %k.11, bf16[8,256,128]{2,1,0:T(8,128)(2,1)} %v.11, bf16[8,256,128]{2,1,0:T(8,128)(2,1)} %g.11), custom_call_target="tpu_custom_call" | custom-call | flops 33554432 | bytes 524288 | tf_op jit(solution)/shard_map/pallas_call | solution.py:144
  2.3 0.1 collective-permute-start.1
  2.4 0.0 copy-done
  2.4 0.0 copy-done.1
  2.4 0.0 copy-done.2
  2.4 0.0 copy-done.3
  2.4 0.3 shard_map.67
  2.7 0.5 %collective-permute-start = (f32[2,2,128,128]{3,2,1,0:T(8,128)S(1)}, f32[2,2,128,128]{3,2,1,0:T(8,128)S(1)}, u32[]{:S(2)}, u32[]{:S(2)}) collective-permute-start(f32[2,2,128,128]{3,2,1,0:T(8,128)S(1)} %shard_map.67), channel_id=1, source_target_pairs={{0,2},{2,0},{4,6},{6,4},{8,10},{10,8},{12,14},{14,12},{16,18},{18,... | collective-permute-start | bytes 786440 | tf_op jit(solution)/shard_map/ppermute | solution.py:336
  3.2 0.3 %shard_map.68 = (f32[2,2,128,128]{3,2,1,0:T(8,128)S(1)}, f32[2,2,128,128]{3,2,1,0:T(8,128)S(1)}) custom-call(bf16[8,256,128]{2,1,0:T(8,128)(2,1)S(1)} %copy-done.3, bf16[8,256,128]{2,1,0:T(8,128)(2,1)S(1)} %copy-done, bf16[8,256,128]{2,1,0:T(8,128)(2,1)S(1)} %copy-done.1, bf16[8,256,128]{2,1,0:T(8,128)(2,1)S(1)} %copy-done.2), custom_call_target="tpu_custom_call" | custom-call | flops 67108864 | bytes 1048576 | tf_op jit(solution)/shard_map/pallas_call | solution.py:144
  3.6 0.3 collective-permute-done.1.came
  3.9 3.4 %collective-permute-start.2 = (f32[2,128,128]{2,1,0:T(8,128)S(1)}, f32[2,128,128]{2,1,0:T(8,128)S(1)}, u32[]{:S(2)}, u32[]{:S(2)}) collective-permute-start(f32[2,128,128]{2,1,0:T(8,128)S(1)} %get-tuple-element.30), channel_id=1, source_target_pairs={{0,4},{2,14},{4,0},{6,10},{8,12},{10,6},{12,8},{14,2},{16,20},{18,... | collective-permute-start | bytes 393224 | tf_op jit(solution)/shard_map/ppermute | solution.py:342
  7.4 0.2 collective-permute-start.3
  7.5 0.0 collective-permute-done.came
  7.6 0.3 collective-permute-start.4
  7.8 2.3 %collective-permute-done.2.refs_1_ = f32[2,128,128]{2,1,0:T(8,128)S(1)} collective-permute-done((f32[2,128,128]{2,1,0:T(8,128)S(1)}, f32[2,128,128]{2,1,0:T(8,128)S(1)}, u32[]{:S(2)}, u32[]{:S(2)}) %collective-permute-start.2) | collective-permute-done | bytes 131104 | tf_op jit(solution)/shard_map/ppermute | solution.py:342
  10.1 2.9 %collective-permute-done.3.refs_2_ = f32[2,128,128]{2,1,0:T(8,128)S(1)} collective-permute-done((f32[2,128,128]{2,1,0:T(8,128)S(1)}, f32[2,128,128]{2,1,0:T(8,128)S(1)}, u32[]{:S(2)}, u32[]{:S(2)}) %collective-permute-start.3) | collective-permute-done | bytes 131104 | tf_op jit(solution)/shard_map/ppermute | solution.py:342
  13.0 0.0 collective-permute-done.4.refs_3_
  13.1 2.4 %collective-permute-start.5 = (f32[128,128]{1,0:T(8,128)S(1)}, f32[128,128]{1,0:T(8,128)S(1)}, u32[]{:S(2)}, u32[]{:S(2)}) collective-permute-start(f32[128,128]{1,0:T(8,128)S(1)} %fusion), channel_id=1, source_target_pairs={{0,16},{2,18},{4,20},{6,22},{8,24},{10,26},{12,28},{14,30},{16,0},... | collective-permute-start | bytes 196616 | tf_op jit(solution)/shard_map/ppermute | solution.py:336
  15.5 2.0 %shard_map.73 = (f32[8,256,128]{2,1,0:T(8,128)S(1)}, f32[8,256,128]{2,1,0:T(8,128)S(1)}, f32[8,256,128]{2,1,0:T(8,128)S(1)}) custom-call(bf16[8,256,128]{2,1,0:T(8,128)(2,1)S(1)} %copy-done.3, bf16[8,256,128]{2,1,0:T(8,128)(2,1)S(1)} %copy-done, bf16[8,256,128]{2,1,0:T(8,128)(2,1)S(1)} %copy-done.1, bf16[8,256,128]{2,1,0:T(8,128)(2,1)S(1)} %copy-done.2, ...), custom_call_target="tpu_custom_call" | custom-call | flops 805306368 | bytes 5242880 | tf_op jit(solution)/shard_map/pallas_call | solution.py:257
  17.5 0.0 collective-permute-done.5
  17.5 0.1 shard_map.77
  17.6 1.0 %collective-permute-start.8 = (f32[2,128,128]{2,1,0:T(8,128)S(1)}, f32[2,128,128]{2,1,0:T(8,128)S(1)}, u32[]{:S(2)}, u32[]{:S(2)}) collective-permute-start(f32[2,128,128]{2,1,0:T(8,128)S(1)} %shard_map.77), channel_id=1, source_target_pairs={{0,12},{2,6},{4,8},{6,2},{8,4},{10,14},{12,0},{14,10},{16,28},{18,... | collective-permute-start | bytes 393224 | tf_op jit(solution)/shard_map/ppermute | solution.py:342
  18.6 1.4 %collective-permute-start.6 = (f32[2,128,128]{2,1,0:T(8,128)S(1)}, f32[2,128,128]{2,1,0:T(8,128)S(1)}, u32[]{:S(2)}, u32[]{:S(2)}) collective-permute-start(f32[2,128,128]{2,1,0:T(8,128)S(1)} %shard_map.74), channel_id=1, source_target_pairs={{0,8},{2,10},{4,12},{6,14},{8,0},{10,2},{12,4},{14,6},{16,24},{18,... | collective-permute-start | bytes 393224 | tf_op jit(solution)/shard_map/ppermute | solution.py:342
  20.0 0.5 %collective-permute-start.7 = (f32[2,128,128]{2,1,0:T(8,128)S(1)}, f32[2,128,128]{2,1,0:T(8,128)S(1)}, u32[]{:S(2)}, u32[]{:S(2)}) collective-permute-start(f32[2,128,128]{2,1,0:T(8,128)S(1)} %shard_map.75), channel_id=1, source_target_pairs={{0,4},{2,14},{4,0},{6,10},{8,12},{10,6},{12,8},{14,2},{16,20},{18,... | collective-permute-start | bytes 393224 | tf_op jit(solution)/shard_map/ppermute | solution.py:342
  20.6 0.9 %collective-permute-done.8.refs_5_ = f32[2,128,128]{2,1,0:T(8,128)S(1)} collective-permute-done((f32[2,128,128]{2,1,0:T(8,128)S(1)}, f32[2,128,128]{2,1,0:T(8,128)S(1)}, u32[]{:S(2)}, u32[]{:S(2)}) %collective-permute-start.8) | collective-permute-done | bytes 131104 | tf_op jit(solution)/shard_map/ppermute | solution.py:342
  21.5 5.5 %collective-permute-start.10 = (f32[2,2,128,128]{3,2,1,0:T(8,128)S(1)}, f32[2,2,128,128]{3,2,1,0:T(8,128)S(1)}, u32[]{:S(2)}, u32[]{:S(2)}) collective-permute-start(f32[2,2,128,128]{3,2,1,0:T(8,128)S(1)} %get-tuple-element.43), channel_id=1, source_target_pairs={{0,2},{2,0},{4,6},{6,4},{8,10},{10,8},{12,14},{14,12},{16,18},{18,... | collective-permute-start | bytes 786440 | tf_op jit(solution)/shard_map/ppermute | solution.py:336
  27.0 1.0 %shard_map.79 = (bf16[8,256,128]{2,1,0:T(8,128)(2,1)}, bf16[8,256,128]{2,1,0:T(8,128)(2,1)}, bf16[8,256,128]{2,1,0:T(8,128)(2,1)}, f32[8,128]{1,0:T(8,128)S(1)}) custom-call(bf16[8,256,128]{2,1,0:T(8,128)(2,1)S(1)} %copy-done, bf16[8,256,128]{2,1,0:T(8,128)(2,1)S(1)} %copy-done.1, bf16[8,256,128]{2,1,0:T(8,128)(2,1)S(1)} %copy-done.2, ...), custom_call_target="tpu_custom_call" | custom-call | flops 50331648 | bytes 393216 | tf_op jit(solution)/shard_map/pallas_call | solution.py:316
  28.0 0.0 collective-permute-done.6.refs_2_
  28.0 0.0 collective-permute-done.7.refs_5_
  28.0 0.1 shard_map.80
  28.1 0.4 %collective-permute-start.9 = (f32[2,2,128,128]{3,2,1,0:T(8,128)S(1)}, f32[2,2,128,128]{3,2,1,0:T(8,128)S(1)}, u32[]{:S(2)}, u32[]{:S(2)}) collective-permute-start(f32[2,2,128,128]{3,2,1,0:T(8,128)S(1)} %get-tuple-element.42), channel_id=1, source_target_pairs={{0,2},{2,0},{4,6},{6,4},{8,10},{10,8},{12,14},{14,12},{16,18},{18,... | collective-permute-start | bytes 786440 | tf_op jit(solution)/shard_map/ppermute | solution.py:336
  28.5 0.0 collective-permute-done.10.refs_0_
  28.5 1.2 %shard_map.81 = (bf16[8,256,128]{2,1,0:T(8,128)(2,1)}, bf16[8,256,128]{2,1,0:T(8,128)(2,1)}, bf16[8,256,128]{2,1,0:T(8,128)(2,1)}) custom-call(bf16[8,256,128]{2,1,0:T(8,128)(2,1)S(1)} %copy-done, bf16[8,256,128]{2,1,0:T(8,128)(2,1)S(1)} %copy-done.1, ...), custom_call_target="tpu_custom_call", output_to_operand_aliasing={{0}: (8, {}), {1}: (9, {}), {2}: (10, {})} | custom-call | flops 100663296 | bytes 786432 | tf_op jit(solution)/shard_map/pallas_call | solution.py:316
  29.7 0.0 collective-permute-done.9.refs_0_
  29.7 1.0 %shard_map.82 = (bf16[8,256,128]{2,1,0:T(8,128)(2,1)}, bf16[8,256,128]{2,1,0:T(8,128)(2,1)}, bf16[8,256,128]{2,1,0:T(8,128)(2,1)}) custom-call(bf16[8,256,128]{2,1,0:T(8,128)(2,1)S(1)} %copy-done, bf16[8,256,128]{2,1,0:T(8,128)(2,1)S(1)} %copy-done.1, bf16[8,256,128]{2,1,0:T(8,128)(2,1)S(1)} %copy-done.2, ...), custom_call_target="tpu_custom_call", output_to_operand_aliasing={{0}: (7, {}), {1}: (8, {}), {2}: (9, {})} | custom-call | flops 50331648 | bytes 393216 | tf_op jit(solution)/shard_map/pallas_call | solution.py:316
  (10 shorter events, 0.3 us)
Async XLA Ops:
  0.6 1.8 %copy-start = (bf16[8,256,128]{2,1,0:T(8,128)(2,1)S(1)}, bf16[8,256,128]{2,1,0:T(8,128)(2,1)}, u32[]{:S(2)}) copy-start(bf16[8,256,128]{2,1,0:T(8,128)(2,1)} %k.11) | copy-start | bytes 1572868
  0.6 1.8 %copy-start.1 = (bf16[8,256,128]{2,1,0:T(8,128)(2,1)S(1)}, bf16[8,256,128]{2,1,0:T(8,128)(2,1)}, u32[]{:S(2)}) copy-start(bf16[8,256,128]{2,1,0:T(8,128)(2,1)} %v.11) | copy-start | bytes 1572868
  0.7 1.8 %copy-start.2 = (bf16[8,256,128]{2,1,0:T(8,128)(2,1)S(1)}, bf16[8,256,128]{2,1,0:T(8,128)(2,1)}, u32[]{:S(2)}) copy-start(bf16[8,256,128]{2,1,0:T(8,128)(2,1)} %g.11) | copy-start | bytes 1572868
  0.7 1.8 %copy-start.3 = (bf16[8,256,128]{2,1,0:T(8,128)(2,1)S(1)}, bf16[8,256,128]{2,1,0:T(8,128)(2,1)}, u32[]{:S(2)}) copy-start(bf16[8,256,128]{2,1,0:T(8,128)(2,1)} %qs.1) | copy-start | bytes 1572868
  2.3 1.6 %collective-permute-start.1 = (f32[2,2,128,128]{3,2,1,0:T(8,128)S(1)}, f32[2,2,128,128]{3,2,1,0:T(8,128)S(1)}, u32[]{:S(2)}, u32[]{:S(2)}) collective-permute-start(f32[2,2,128,128]{3,2,1,0:T(8,128)S(1)} %shard_map.70), channel_id=1, source_target_pairs={{0,2},{2,0},{4,6},{6,4},{8,10},{10,8},{12,14},{14,12},{16,18},{18,... | collective-permute-start | bytes 786440 | tf_op jit(solution)/shard_map/ppermute | solution.py:336
  2.7 4.8 %collective-permute-start = (f32[2,2,128,128]{3,2,1,0:T(8,128)S(1)}, f32[2,2,128,128]{3,2,1,0:T(8,128)S(1)}, u32[]{:S(2)}, u32[]{:S(2)}) collective-permute-start(f32[2,2,128,128]{3,2,1,0:T(8,128)S(1)} %shard_map.67), channel_id=1, source_target_pairs={{0,2},{2,0},{4,6},{6,4},{8,10},{10,8},{12,14},{14,12},{16,18},{18,... | collective-permute-start | bytes 786440 | tf_op jit(solution)/shard_map/ppermute | solution.py:336
  3.9 6.2 %collective-permute-start.2 = (f32[2,128,128]{2,1,0:T(8,128)S(1)}, f32[2,128,128]{2,1,0:T(8,128)S(1)}, u32[]{:S(2)}, u32[]{:S(2)}) collective-permute-start(f32[2,128,128]{2,1,0:T(8,128)S(1)} %get-tuple-element.30), channel_id=1, source_target_pairs={{0,4},{2,14},{4,0},{6,10},{8,12},{10,6},{12,8},{14,2},{16,20},{18,... | collective-permute-start | bytes 393224 | tf_op jit(solution)/shard_map/ppermute | solution.py:342
  7.4 5.7 %collective-permute-start.3 = (f32[2,128,128]{2,1,0:T(8,128)S(1)}, f32[2,128,128]{2,1,0:T(8,128)S(1)}, u32[]{:S(2)}, u32[]{:S(2)}) collective-permute-start(f32[2,128,128]{2,1,0:T(8,128)S(1)} %get-tuple-element.31), channel_id=1, source_target_pairs={{0,8},{2,10},{4,12},{6,14},{8,0},{10,2},{12,4},{14,6},{16,24},{18,... | collective-permute-start | bytes 393224 | tf_op jit(solution)/shard_map/ppermute | solution.py:342
  7.6 5.4 %collective-permute-start.4 = (f32[2,128,128]{2,1,0:T(8,128)S(1)}, f32[2,128,128]{2,1,0:T(8,128)S(1)}, u32[]{:S(2)}, u32[]{:S(2)}) collective-permute-start(f32[2,128,128]{2,1,0:T(8,128)S(1)} %get-tuple-element.32), channel_id=1, source_target_pairs={{0,12},{2,6},{4,8},{6,2},{8,4},{10,14},{12,0},{14,10},{16,28},{18,... | collective-permute-start | bytes 393224 | tf_op jit(solution)/shard_map/ppermute | solution.py:342
  13.1 4.4 %collective-permute-start.5 = (f32[128,128]{1,0:T(8,128)S(1)}, f32[128,128]{1,0:T(8,128)S(1)}, u32[]{:S(2)}, u32[]{:S(2)}) collective-permute-start(f32[128,128]{1,0:T(8,128)S(1)} %fusion), channel_id=1, source_target_pairs={{0,16},{2,18},{4,20},{6,22},{8,24},{10,26},{12,28},{14,30},{16,0},... | collective-permute-start | bytes 196616 | tf_op jit(solution)/shard_map/ppermute | solution.py:336
  17.6 3.9 %collective-permute-start.8 = (f32[2,128,128]{2,1,0:T(8,128)S(1)}, f32[2,128,128]{2,1,0:T(8,128)S(1)}, u32[]{:S(2)}, u32[]{:S(2)}) collective-permute-start(f32[2,128,128]{2,1,0:T(8,128)S(1)} %shard_map.77), channel_id=1, source_target_pairs={{0,12},{2,6},{4,8},{6,2},{8,4},{10,14},{12,0},{14,10},{16,28},{18,... | collective-permute-start | bytes 393224 | tf_op jit(solution)/shard_map/ppermute | solution.py:342
  18.6 9.4 %collective-permute-start.6 = (f32[2,128,128]{2,1,0:T(8,128)S(1)}, f32[2,128,128]{2,1,0:T(8,128)S(1)}, u32[]{:S(2)}, u32[]{:S(2)}) collective-permute-start(f32[2,128,128]{2,1,0:T(8,128)S(1)} %shard_map.74), channel_id=1, source_target_pairs={{0,8},{2,10},{4,12},{6,14},{8,0},{10,2},{12,4},{14,6},{16,24},{18,... | collective-permute-start | bytes 393224 | tf_op jit(solution)/shard_map/ppermute | solution.py:342
  20.0 8.0 %collective-permute-start.7 = (f32[2,128,128]{2,1,0:T(8,128)S(1)}, f32[2,128,128]{2,1,0:T(8,128)S(1)}, u32[]{:S(2)}, u32[]{:S(2)}) collective-permute-start(f32[2,128,128]{2,1,0:T(8,128)S(1)} %shard_map.75), channel_id=1, source_target_pairs={{0,4},{2,14},{4,0},{6,10},{8,12},{10,6},{12,8},{14,2},{16,20},{18,... | collective-permute-start | bytes 393224 | tf_op jit(solution)/shard_map/ppermute | solution.py:342
  21.5 7.0 %collective-permute-start.10 = (f32[2,2,128,128]{3,2,1,0:T(8,128)S(1)}, f32[2,2,128,128]{3,2,1,0:T(8,128)S(1)}, u32[]{:S(2)}, u32[]{:S(2)}) collective-permute-start(f32[2,2,128,128]{3,2,1,0:T(8,128)S(1)} %get-tuple-element.43), channel_id=1, source_target_pairs={{0,2},{2,0},{4,6},{6,4},{8,10},{10,8},{12,14},{14,12},{16,18},{18,... | collective-permute-start | bytes 786440 | tf_op jit(solution)/shard_map/ppermute | solution.py:336
  28.1 1.6 %collective-permute-start.9 = (f32[2,2,128,128]{3,2,1,0:T(8,128)S(1)}, f32[2,2,128,128]{3,2,1,0:T(8,128)S(1)}, u32[]{:S(2)}, u32[]{:S(2)}) collective-permute-start(f32[2,2,128,128]{3,2,1,0:T(8,128)S(1)} %get-tuple-element.42), channel_id=1, source_target_pairs={{0,2},{2,0},{4,6},{6,4},{8,10},{10,8},{12,14},{14,12},{16,18},{18,... | collective-permute-start | bytes 786440 | tf_op jit(solution)/shard_map/ppermute | solution.py:336

commit v10 on v8

--- a/solution.py
+++ b/solution.py
@@ -187,7 +187,7 @@
     )(near(came), near(keep))
 
 
-def outside_kernel(after, carry, *refs, slot, group):
+def outside_kernel(carry, *refs, slot, group):
     out = refs[-1]
     core, rank = place_of(group)
     earlier, later = carry[0], carry[1]
@@ -201,14 +201,14 @@
     out[1] = later
 
 
-def outside_of(carry, held, slot, after):
+def outside_of(carry, held, slot):
     return pl.pallas_call(
         functools.partial(outside_kernel, slot=slot, group=len(held)),
         out_shape=pltpu.VMEM(carry.shape, F32),
-        in_specs=[PLACED] + [WHOLE] * (1 + len(held)),
+        in_specs=[WHOLE] * (1 + len(held)),
         out_specs=WHOLE,
         compiler_params=ROOM,
-    )(near(after), near(carry), *[near(x) for x in held])
+    )(near(carry), *[near(x) for x in held])
 
 
 def share_kernel(*refs, rows):
@@ -265,7 +265,7 @@
     )(*[near(x) for x in data], near(after))
 
 
-def block_kernel(*refs):
+def block_kernel(after, *refs):
     out = refs[-1]
     total = refs[0][...]
     for x in refs[1:-1]:
@@ -273,14 +273,14 @@
     out[...] = total
 
 
-def block_sum(held):
+def block_sum(held, after):
     return pl.pallas_call(
         block_kernel,
         out_shape=pltpu.VMEM(held[0].shape, F32),
-        in_specs=[WHOLE] * len(held),
+        in_specs=[PLACED] + [WHOLE] * len(held),
         out_specs=WHOLE,
         compiler_params=ROOM,
-    )(*[near(x) for x in held])
+    )(near(after), *[near(x) for x in held])
 
 
 def final_kernel(k, v, g, lq, lk, lv, *refs, pieces, given):
@@ -356,9 +356,9 @@
                 total[j], inner[j], outer[j] = sums[n], (into, n), (from_here, n)
 
         held = [total[0]] + [swap_slot(total[j], j, group) for j in range(1, group)]
-
-        block = block_sum(held)
-        parts = local_parts(data, block)
+        parts = local_parts(data, total[0])
+
+        block = block_sum(held, parts[0])
         keys, rests = block[0], block[1]
         carry = jnp.zeros_like(block)
         bit = 2 * group
@@ -375,7 +375,7 @@
             )
             bit *= 2
 
-        around = [outside_of(carry, held, j, parts[0]) for j in range(group)]
+        around = [outside_of(carry, held, j) for j in range(group)]
         around = [swap_slot(x, j, group) if j else x for j, x in enumerate(around)]
         soon, late = (0, group - 1), tuple(range(group - 2, 0, -1))
         mine, theirs = shares_of(inner, outer, around, soon)

time: 31 us -> 31 us (level)
  waiting for transfers between devices: 6.42 us -> 6.1 us
    ppermute x6, waiting for transfers between devices: 6.11 us -> 4.08 us  [swap_slot(): return lax.ppermute(x, 'seq', [(i, i ^ masks[i & 1]) for i in range(count)])]
    ppermute x5, waiting for transfers between devices: 0.32 us -> 2.02 us  [swap(): return lax.ppermute(x, 'seq', [(i, i ^ mask) for i in range(count)])]
    ppermute x5, starting transfers between devices: 8.89 us -> 9.22 us  [swap(): return lax.ppermute(x, 'seq', [(i, i ^ mask) for i in range(count)])]
  transfers between devices with their start and end apart: 11 -> 11, of which waited for: 4 -> 5; matrix products, arithmetic and copies ran while one was open for 0% -> 0% of each run, Pallas kernels for 17% -> 17%
where the time goes in v10:
time: 31 us; the launch traced here: 30.6 us
  starting transfers between devices  15.9 us (51%)
  Pallas kernels  7.71 us (25%)
  waiting for transfers between devices  6.1 us (20%)
  between operations  0.8 us (3%)
    ppermute x5, starting transfers between devices, swap(): return lax.ppermute(x, 'seq', [(i, i ^ mask) for i in range(count)])  9.22 us
    ppermute x6, starting transfers between devices, swap_slot(): return lax.ppermute(x, 'seq', [(i, i ^ masks[i & 1]) for i in range(count)])  6.69 us
    ppermute x6, waiting for transfers between devices, swap_slot(): return lax.ppermute(x, 'seq', [(i, i ^ masks[i & 1]) for i in range(count)])  4.08 us
    pallas_call x3, Pallas kernels, final_sums(): pl.pallas_call(functools.partial(final_kernel, pieces=pieces, given=len(f...  3.15 us
    pallas_call x3, Pallas kernels, state_call(): pl.pallas_call(kernel, out_shape=[pltpu.VMEM((len(part), 2, width, width)...  2.17 us
    pallas_call x1, Pallas kernels, local_parts(): pl.pallas_call(local_kernel, out_shape=[pltpu.VMEM(data[0].shape, F32)] *...  2.02 us
    ppermute x5, waiting for transfers between devices, swap(): return lax.ppermute(x, 'seq', [(i, i ^ mask) for i in range(count)])  2.02 us
  transfers between devices with their start and end apart: 11, of which 5 were waited for; matrix products, arithmetic and copies ran while one was open for 0% of the time, Pallas kernels for 17%

profile of v10, /device:TPU:1, one launch (start us, length us, event | category | flops | bytes accessed | tf_op | source)
XLA Modules:
  0.0 30.6 jit_solution(15812546884243555905)
XLA Ops:
  0.6 0.0 copy-start
  0.6 0.0 copy-start.1
  0.7 0.0 copy-start.2
  0.7 0.0 copy-start.3
  0.7 1.6 %shard_map.71 = f32[2,2,128,128]{3,2,1,0:T(8,128)S(1)} custom-call(bf16[8,256,128]{2,1,0:T(8,128)(2,1)} %q.5, bf16[8,256,128]{2,1,0:T(8,128)(2,1)} %k.11, bf16[8,256,128]{2,1,0:T(8,128)(2,1)} %v.11, bf16[8,256,128]{2,1,0:T(8,128)(2,1)} %g.11), custom_call_target="tpu_custom_call" | custom-call | flops 33554432 | bytes 524288 | tf_op jit(solution)/shard_map/pallas_call | solution.py:141
  2.2 0.1 collective-permute-start.1
  2.4 0.0 copy-done
  2.4 0.0 copy-done.1
  2.4 0.0 copy-done.2
  2.4 0.0 copy-done.3
  2.4 0.3 shard_map.67
  2.7 0.5 %collective-permute-start = (f32[2,2,128,128]{3,2,1,0:T(8,128)S(1)}, f32[2,2,128,128]{3,2,1,0:T(8,128)S(1)}, u32[]{:S(2)}, u32[]{:S(2)}) collective-permute-start(f32[2,2,128,128]{3,2,1,0:T(8,128)S(1)} %shard_map.67), channel_id=1, source_target_pairs={{0,2},{2,0},{4,6},{6,4},{8,10},{10,8},{12,14},{14,12},{16,18},{18,... | collective-permute-start | bytes 786440 | tf_op jit(solution)/shard_map/ppermute | solution.py:333
  3.2 0.3 %shard_map.68 = (f32[2,2,128,128]{3,2,1,0:T(8,128)S(1)}, f32[2,2,128,128]{3,2,1,0:T(8,128)S(1)}) custom-call(bf16[8,256,128]{2,1,0:T(8,128)(2,1)S(1)} %copy-done.3, bf16[8,256,128]{2,1,0:T(8,128)(2,1)S(1)} %copy-done, bf16[8,256,128]{2,1,0:T(8,128)(2,1)S(1)} %copy-done.1, bf16[8,256,128]{2,1,0:T(8,128)(2,1)S(1)} %copy-done.2), custom_call_target="tpu_custom_call" | custom-call | flops 67108864 | bytes 1048576 | tf_op jit(solution)/shard_map/pallas_call | solution.py:141
  3.5 0.3 collective-permute-done.1.came
  3.9 3.4 %collective-permute-start.2 = (f32[2,128,128]{2,1,0:T(8,128)S(1)}, f32[2,128,128]{2,1,0:T(8,128)S(1)}, u32[]{:S(2)}, u32[]{:S(2)}) collective-permute-start(f32[2,128,128]{2,1,0:T(8,128)S(1)} %get-tuple-element.35), channel_id=1, source_target_pairs={{0,4},{2,14},{4,0},{6,10},{8,12},{10,6},{12,8},{14,2},{16,20},{18,... | collective-permute-start | bytes 393224 | tf_op jit(solution)/shard_map/ppermute | solution.py:339
  7.3 0.2 collective-permute-start.3
  7.5 0.0 collective-permute-done.came
  7.5 0.3 collective-permute-start.4
  7.8 2.0 %shard_map.70 = (f32[8,256,128]{2,1,0:T(8,128)S(1)}, f32[8,256,128]{2,1,0:T(8,128)S(1)}, f32[8,256,128]{2,1,0:T(8,128)S(1)}) custom-call(bf16[8,256,128]{2,1,0:T(8,128)(2,1)S(1)} %copy-done.3, bf16[8,256,128]{2,1,0:T(8,128)(2,1)S(1)} %copy-done, bf16[8,256,128]{2,1,0:T(8,128)(2,1)S(1)} %copy-done.1, bf16[8,256,128]{2,1,0:T(8,128)(2,1)S(1)} %copy-done.2, ...), custom_call_target="tpu_custom_call" | custom-call | flops 805306368 | bytes 5242880 | tf_op jit(solution)/shard_map/pallas_call | solution.py:254
  9.8 0.2 collective-permute-done.2.refs_1_
  10.1 2.9 %collective-permute-done.3.refs_2_ = f32[2,128,128]{2,1,0:T(8,128)S(1)} collective-permute-done((f32[2,128,128]{2,1,0:T(8,128)S(1)}, f32[2,128,128]{2,1,0:T(8,128)S(1)}, u32[]{:S(2)}, u32[]{:S(2)}) %collective-permute-start.3) | collective-permute-done | bytes 131104 | tf_op jit(solution)/shard_map/ppermute | solution.py:339
  13.0 0.0 collective-permute-done.4.refs_3_
  13.0 2.4 %collective-permute-start.5 = (f32[128,128]{1,0:T(8,128)S(1)}, f32[128,128]{1,0:T(8,128)S(1)}, u32[]{:S(2)}, u32[]{:S(2)}) collective-permute-start(f32[128,128]{1,0:T(8,128)S(1)} %fusion), channel_id=1, source_target_pairs={{0,16},{2,18},{4,20},{6,22},{8,24},{10,26},{12,28},{14,30},{16,0},... | collective-permute-start | bytes 196616 | tf_op jit(solution)/shard_map/ppermute | solution.py:333
  15.4 1.7 %collective-permute-done.5 = f32[128,128]{1,0:T(8,128)S(1)} collective-permute-done((f32[128,128]{1,0:T(8,128)S(1)}, f32[128,128]{1,0:T(8,128)S(1)}, u32[]{:S(2)}, u32[]{:S(2)}) %collective-permute-start.5) | collective-permute-done | bytes 65568 | tf_op jit(solution)/shard_map/ppermute | solution.py:333
  17.1 0.1 shard_map.77
  17.2 1.0 %collective-permute-start.8 = (f32[2,128,128]{2,1,0:T(8,128)S(1)}, f32[2,128,128]{2,1,0:T(8,128)S(1)}, u32[]{:S(2)}, u32[]{:S(2)}) collective-permute-start(f32[2,128,128]{2,1,0:T(8,128)S(1)} %shard_map.77), channel_id=1, source_target_pairs={{0,12},{2,6},{4,8},{6,2},{8,4},{10,14},{12,0},{14,10},{16,28},{18,... | collective-permute-start | bytes 393224 | tf_op jit(solution)/shard_map/ppermute | solution.py:339
  18.2 1.5 %collective-permute-start.6 = (f32[2,128,128]{2,1,0:T(8,128)S(1)}, f32[2,128,128]{2,1,0:T(8,128)S(1)}, u32[]{:S(2)}, u32[]{:S(2)}) collective-permute-start(f32[2,128,128]{2,1,0:T(8,128)S(1)} %shard_map.74), channel_id=1, source_target_pairs={{0,8},{2,10},{4,12},{6,14},{8,0},{10,2},{12,4},{14,6},{16,24},{18,... | collective-permute-start | bytes 393224 | tf_op jit(solution)/shard_map/ppermute | solution.py:339
  19.7 0.4 %collective-permute-start.7 = (f32[2,128,128]{2,1,0:T(8,128)S(1)}, f32[2,128,128]{2,1,0:T(8,128)S(1)}, u32[]{:S(2)}, u32[]{:S(2)}) collective-permute-start(f32[2,128,128]{2,1,0:T(8,128)S(1)} %shard_map.75), channel_id=1, source_target_pairs={{0,4},{2,14},{4,0},{6,10},{8,12},{10,6},{12,8},{14,2},{16,20},{18,... | collective-permute-start | bytes 393224 | tf_op jit(solution)/shard_map/ppermute | solution.py:339
  20.2 0.9 %collective-permute-done.8.refs_5_ = f32[2,128,128]{2,1,0:T(8,128)S(1)} collective-permute-done((f32[2,128,128]{2,1,0:T(8,128)S(1)}, f32[2,128,128]{2,1,0:T(8,128)S(1)}, u32[]{:S(2)}, u32[]{:S(2)}) %collective-permute-start.8) | collective-permute-done | bytes 131104 | tf_op jit(solution)/shard_map/ppermute | solution.py:339
  21.1 5.6 %collective-permute-start.10 = (f32[2,2,128,128]{3,2,1,0:T(8,128)S(1)}, f32[2,2,128,128]{3,2,1,0:T(8,128)S(1)}, u32[]{:S(2)}, u32[]{:S(2)}) collective-permute-start(f32[2,2,128,128]{3,2,1,0:T(8,128)S(1)} %get-tuple-element.43), channel_id=1, source_target_pairs={{0,2},{2,0},{4,6},{6,4},{8,10},{10,8},{12,14},{14,12},{16,18},{18,... | collective-permute-start | bytes 786440 | tf_op jit(solution)/shard_map/ppermute | solution.py:333
  26.7 1.0 %shard_map.79 = (bf16[8,256,128]{2,1,0:T(8,128)(2,1)}, bf16[8,256,128]{2,1,0:T(8,128)(2,1)}, bf16[8,256,128]{2,1,0:T(8,128)(2,1)}, f32[8,128]{1,0:T(8,128)S(1)}) custom-call(bf16[8,256,128]{2,1,0:T(8,128)(2,1)S(1)} %copy-done, bf16[8,256,128]{2,1,0:T(8,128)(2,1)S(1)} %copy-done.1, bf16[8,256,128]{2,1,0:T(8,128)(2,1)S(1)} %copy-done.2, ...), custom_call_target="tpu_custom_call" | custom-call | flops 50331648 | bytes 393216 | tf_op jit(solution)/shard_map/pallas_call | solution.py:313
  27.7 0.0 collective-permute-done.6.refs_2_
  27.7 0.0 collective-permute-done.7.refs_5_
  27.7 0.1 shard_map.80
  27.8 0.7 %collective-permute-start.9 = (f32[2,2,128,128]{3,2,1,0:T(8,128)S(1)}, f32[2,2,128,128]{3,2,1,0:T(8,128)S(1)}, u32[]{:S(2)}, u32[]{:S(2)}) collective-permute-start(f32[2,2,128,128]{3,2,1,0:T(8,128)S(1)} %get-tuple-element.42), channel_id=1, source_target_pairs={{0,2},{2,0},{4,6},{6,4},{8,10},{10,8},{12,14},{14,12},{16,18},{18,... | collective-permute-start | bytes 786440 | tf_op jit(solution)/shard_map/ppermute | solution.py:333
  28.4 0.0 collective-permute-done.10.refs_0_
  28.4 1.2 %shard_map.81 = (bf16[8,256,128]{2,1,0:T(8,128)(2,1)}, bf16[8,256,128]{2,1,0:T(8,128)(2,1)}, bf16[8,256,128]{2,1,0:T(8,128)(2,1)}) custom-call(bf16[8,256,128]{2,1,0:T(8,128)(2,1)S(1)} %copy-done, bf16[8,256,128]{2,1,0:T(8,128)(2,1)S(1)} %copy-done.1, ...), custom_call_target="tpu_custom_call", output_to_operand_aliasing={{0}: (8, {}), {1}: (9, {}), {2}: (10, {})} | custom-call | flops 100663296 | bytes 786432 | tf_op jit(solution)/shard_map/pallas_call | solution.py:313
  29.6 0.0 collective-permute-done.9.refs_0_
  29.6 1.0 %shard_map.82 = (bf16[8,256,128]{2,1,0:T(8,128)(2,1)}, bf16[8,256,128]{2,1,0:T(8,128)(2,1)}, bf16[8,256,128]{2,1,0:T(8,128)(2,1)}) custom-call(bf16[8,256,128]{2,1,0:T(8,128)(2,1)S(1)} %copy-done, bf16[8,256,128]{2,1,0:T(8,128)(2,1)S(1)} %copy-done.1, bf16[8,256,128]{2,1,0:T(8,128)(2,1)S(1)} %copy-done.2, ...), custom_call_target="tpu_custom_call", output_to_operand_aliasing={{0}: (7, {}), {1}: (8, {}), {2}: (9, {})} | custom-call | flops 50331648 | bytes 393216 | tf_op jit(solution)/shard_map/pallas_call | solution.py:313
  (10 shorter events, 0.3 us)
Async XLA Ops:
  0.6 1.7 %copy-start = (bf16[8,256,128]{2,1,0:T(8,128)(2,1)S(1)}, bf16[8,256,128]{2,1,0:T(8,128)(2,1)}, u32[]{:S(2)}) copy-start(bf16[8,256,128]{2,1,0:T(8,128)(2,1)} %k.11) | copy-start | bytes 1572868
  0.6 1.7 %copy-start.1 = (bf16[8,256,128]{2,1,0:T(8,128)(2,1)S(1)}, bf16[8,256,128]{2,1,0:T(8,128)(2,1)}, u32[]{:S(2)}) copy-start(bf16[8,256,128]{2,1,0:T(8,128)(2,1)} %v.11) | copy-start | bytes 1572868
  0.7 1.7 %copy-start.2 = (bf16[8,256,128]{2,1,0:T(8,128)(2,1)S(1)}, bf16[8,256,128]{2,1,0:T(8,128)(2,1)}, u32[]{:S(2)}) copy-start(bf16[8,256,128]{2,1,0:T(8,128)(2,1)} %g.11) | copy-start | bytes 1572868
  0.7 1.7 %copy-start.3 = (bf16[8,256,128]{2,1,0:T(8,128)(2,1)S(1)}, bf16[8,256,128]{2,1,0:T(8,128)(2,1)}, u32[]{:S(2)}) copy-start(bf16[8,256,128]{2,1,0:T(8,128)(2,1)} %q.5) | copy-start | bytes 1572868
  2.2 1.6 %collective-permute-start.1 = (f32[2,2,128,128]{3,2,1,0:T(8,128)S(1)}, f32[2,2,128,128]{3,2,1,0:T(8,128)S(1)}, u32[]{:S(2)}, u32[]{:S(2)}) collective-permute-start(f32[2,2,128,128]{3,2,1,0:T(8,128)S(1)} %shard_map.71), channel_id=1, source_target_pairs={{0,2},{2,0},{4,6},{6,4},{8,10},{10,8},{12,14},{14,12},{16,18},{18,... | collective-permute-start | bytes 786440 | tf_op jit(solution)/shard_map/ppermute | solution.py:333
  2.7 4.8 %collective-permute-start = (f32[2,2,128,128]{3,2,1,0:T(8,128)S(1)}, f32[2,2,128,128]{3,2,1,0:T(8,128)S(1)}, u32[]{:S(2)}, u32[]{:S(2)}) collective-permute-start(f32[2,2,128,128]{3,2,1,0:T(8,128)S(1)} %shard_map.67), channel_id=1, source_target_pairs={{0,2},{2,0},{4,6},{6,4},{8,10},{10,8},{12,14},{14,12},{16,18},{18,... | collective-permute-start | bytes 786440 | tf_op jit(solution)/shard_map/ppermute | solution.py:333
  3.9 6.2 %collective-permute-start.2 = (f32[2,128,128]{2,1,0:T(8,128)S(1)}, f32[2,128,128]{2,1,0:T(8,128)S(1)}, u32[]{:S(2)}, u32[]{:S(2)}) collective-permute-start(f32[2,128,128]{2,1,0:T(8,128)S(1)} %get-tuple-element.35), channel_id=1, source_target_pairs={{0,4},{2,14},{4,0},{6,10},{8,12},{10,6},{12,8},{14,2},{16,20},{18,... | collective-permute-start | bytes 393224 | tf_op jit(solution)/shard_map/ppermute | solution.py:339
  7.3 5.7 %collective-permute-start.3 = (f32[2,128,128]{2,1,0:T(8,128)S(1)}, f32[2,128,128]{2,1,0:T(8,128)S(1)}, u32[]{:S(2)}, u32[]{:S(2)}) collective-permute-start(f32[2,128,128]{2,1,0:T(8,128)S(1)} %get-tuple-element.36), channel_id=1, source_target_pairs={{0,8},{2,10},{4,12},{6,14},{8,0},{10,2},{12,4},{14,6},{16,24},{18,... | collective-permute-start | bytes 393224 | tf_op jit(solution)/shard_map/ppermute | solution.py:339
  7.5 5.4 %collective-permute-start.4 = (f32[2,128,128]{2,1,0:T(8,128)S(1)}, f32[2,128,128]{2,1,0:T(8,128)S(1)}, u32[]{:S(2)}, u32[]{:S(2)}) collective-permute-start(f32[2,128,128]{2,1,0:T(8,128)S(1)} %get-tuple-element.37), channel_id=1, source_target_pairs={{0,12},{2,6},{4,8},{6,2},{8,4},{10,14},{12,0},{14,10},{16,28},{18,... | collective-permute-start | bytes 393224 | tf_op jit(solution)/shard_map/ppermute | solution.py:339
  13.0 4.1 %collective-permute-start.5 = (f32[128,128]{1,0:T(8,128)S(1)}, f32[128,128]{1,0:T(8,128)S(1)}, u32[]{:S(2)}, u32[]{:S(2)}) collective-permute-start(f32[128,128]{1,0:T(8,128)S(1)} %fusion), channel_id=1, source_target_pairs={{0,16},{2,18},{4,20},{6,22},{8,24},{10,26},{12,28},{14,30},{16,0},... | collective-permute-start | bytes 196616 | tf_op jit(solution)/shard_map/ppermute | solution.py:333
  17.2 3.9 %collective-permute-start.8 = (f32[2,128,128]{2,1,0:T(8,128)S(1)}, f32[2,128,128]{2,1,0:T(8,128)S(1)}, u32[]{:S(2)}, u32[]{:S(2)}) collective-permute-start(f32[2,128,128]{2,1,0:T(8,128)S(1)} %shard_map.77), channel_id=1, source_target_pairs={{0,12},{2,6},{4,8},{6,2},{8,4},{10,14},{12,0},{14,10},{16,28},{18,... | collective-permute-start | bytes 393224 | tf_op jit(solution)/shard_map/ppermute | solution.py:339
  18.2 9.5 %collective-permute-start.6 = (f32[2,128,128]{2,1,0:T(8,128)S(1)}, f32[2,128,128]{2,1,0:T(8,128)S(1)}, u32[]{:S(2)}, u32[]{:S(2)}) collective-permute-start(f32[2,128,128]{2,1,0:T(8,128)S(1)} %shard_map.74), channel_id=1, source_target_pairs={{0,8},{2,10},{4,12},{6,14},{8,0},{10,2},{12,4},{14,6},{16,24},{18,... | collective-permute-start | bytes 393224 | tf_op jit(solution)/shard_map/ppermute | solution.py:339
  19.7 8.0 %collective-permute-start.7 = (f32[2,128,128]{2,1,0:T(8,128)S(1)}, f32[2,128,128]{2,1,0:T(8,128)S(1)}, u32[]{:S(2)}, u32[]{:S(2)}) collective-permute-start(f32[2,128,128]{2,1,0:T(8,128)S(1)} %shard_map.75), channel_id=1, source_target_pairs={{0,4},{2,14},{4,0},{6,10},{8,12},{10,6},{12,8},{14,2},{16,20},{18,... | collective-permute-start | bytes 393224 | tf_op jit(solution)/shard_map/ppermute | solution.py:339
  21.1 7.3 %collective-permute-start.10 = (f32[2,2,128,128]{3,2,1,0:T(8,128)S(1)}, f32[2,2,128,128]{3,2,1,0:T(8,128)S(1)}, u32[]{:S(2)}, u32[]{:S(2)}) collective-permute-start(f32[2,2,128,128]{3,2,1,0:T(8,128)S(1)} %get-tuple-element.43), channel_id=1, source_target_pairs={{0,2},{2,0},{4,6},{6,4},{8,10},{10,8},{12,14},{14,12},{16,18},{18,... | collective-permute-start | bytes 786440 | tf_op jit(solution)/shard_map/ppermute | solution.py:333
  27.8 1.8 %collective-permute-start.9 = (f32[2,2,128,128]{3,2,1,0:T(8,128)S(1)}, f32[2,2,128,128]{3,2,1,0:T(8,128)S(1)}, u32[]{:S(2)}, u32[]{:S(2)}) collective-permute-start(f32[2,2,128,128]{3,2,1,0:T(8,128)S(1)} %get-tuple-element.42), channel_id=1, source_target_pairs={{0,2},{2,0},{4,6},{6,4},{8,10},{10,8},{12,14},{14,12},{16,18},{18,... | collective-permute-start | bytes 786440 | tf_op jit(solution)/shard_map/ppermute | solution.py:333

commit v11 on v10

--- a/solution.py
+++ b/solution.py
@@ -117,10 +117,13 @@
             head = core * slots + partner(core, rank, slot, slots)
             copies.append(pltpu.make_async_copy(there.at[head], here.at[m], sems.at[n, m]))
             copies[-1].start()
-    for copy in copies:
+    for copy in copies[: 2 * len(part)]:
         copy.wait()
     for m in range(len(part)):
         out[m, 0] = dot(ks[m], vs[m], 0, 0)
+    for copy in copies[2 * len(part) :]:
+        copy.wait()
+    for m in range(len(part)):
         out[m, 1] = dot(qs[m], gs[m], 0, 0)
 
 

time: 31 us -> 31.1 us (level)
  no operation moved by 1% of the time
where the time goes in v11:
time: 31.1 us; the launch traced here: 30.7 us
  starting transfers between devices  15.9 us (51%)
  Pallas kernels  7.79 us (25%)
  waiting for transfers between devices  6.1 us (20%)
  between operations  0.8 us (3%)
    ppermute x5, starting transfers between devices, swap(): return lax.ppermute(x, 'seq', [(i, i ^ mask) for i in range(count)])  9.24 us
    ppermute x6, starting transfers between devices, swap_slot(): return lax.ppermute(x, 'seq', [(i, i ^ masks[i & 1]) for i in range(count)])  6.69 us
    ppermute x6, waiting for transfers between devices, swap_slot(): return lax.ppermute(x, 'seq', [(i, i ^ masks[i & 1]) for i in range(count)])  4.08 us
    pallas_call x3, Pallas kernels, final_sums(): pl.pallas_call(functools.partial(final_kernel, pieces=pieces, given=len(f...  3.15 us
    pallas_call x3, Pallas kernels, state_call(): pl.pallas_call(kernel, out_shape=[pltpu.VMEM((len(part), 2, width, width)...  2.25 us
    pallas_call x1, Pallas kernels, local_parts(): pl.pallas_call(local_kernel, out_shape=[pltpu.VMEM(data[0].shape, F32)] *...  2.02 us
    ppermute x5, waiting for transfers between devices, swap(): return lax.ppermute(x, 'seq', [(i, i ^ mask) for i in range(count)])  2.02 us
  transfers between devices with their start and end apart: 11, of which 5 were waited for; matrix products, arithmetic and copies ran while one was open for 0% of the time, Pallas kernels for 17%

profile of v11, /device:TPU:1, one launch (start us, length us, event | category | flops | bytes accessed | tf_op | source)
XLA Modules:
  0.0 30.7 jit_solution(12229003836558462004)
XLA Ops:
  0.6 0.0 copy-start
  0.6 0.0 copy-start.1
  0.7 0.0 copy-start.2
  0.7 0.0 copy-start.3
  0.7 1.6 %shard_map.71 = f32[2,2,128,128]{3,2,1,0:T(8,128)S(1)} custom-call(bf16[8,256,128]{2,1,0:T(8,128)(2,1)} %q.5, bf16[8,256,128]{2,1,0:T(8,128)(2,1)} %k.11, bf16[8,256,128]{2,1,0:T(8,128)(2,1)} %v.11, bf16[8,256,128]{2,1,0:T(8,128)(2,1)} %g.11), custom_call_target="tpu_custom_call" | custom-call | flops 33554432 | bytes 524288 | tf_op jit(solution)/shard_map/pallas_call | solution.py:144
  2.3 0.1 collective-permute-start.1
  2.4 0.0 copy-done
  2.4 0.0 copy-done.1
  2.4 0.0 copy-done.2
  2.4 0.0 copy-done.3
  2.4 0.3 shard_map.67
  2.7 0.5 %collective-permute-start = (f32[2,2,128,128]{3,2,1,0:T(8,128)S(1)}, f32[2,2,128,128]{3,2,1,0:T(8,128)S(1)}, u32[]{:S(2)}, u32[]{:S(2)}) collective-permute-start(f32[2,2,128,128]{3,2,1,0:T(8,128)S(1)} %shard_map.67), channel_id=1, source_target_pairs={{0,2},{2,0},{4,6},{6,4},{8,10},{10,8},{12,14},{14,12},{16,18},{18,... | collective-permute-start | bytes 786440 | tf_op jit(solution)/shard_map/ppermute | solution.py:336
  3.2 0.3 %shard_map.68 = (f32[2,2,128,128]{3,2,1,0:T(8,128)S(1)}, f32[2,2,128,128]{3,2,1,0:T(8,128)S(1)}) custom-call(bf16[8,256,128]{2,1,0:T(8,128)(2,1)S(1)} %copy-done.3, bf16[8,256,128]{2,1,0:T(8,128)(2,1)S(1)} %copy-done, bf16[8,256,128]{2,1,0:T(8,128)(2,1)S(1)} %copy-done.1, bf16[8,256,128]{2,1,0:T(8,128)(2,1)S(1)} %copy-done.2), custom_call_target="tpu_custom_call" | custom-call | flops 67108864 | bytes 1048576 | tf_op jit(solution)/shard_map/pallas_call | solution.py:144
  3.6 0.3 collective-permute-done.1.came
  3.9 3.4 %collective-permute-start.2 = (f32[2,128,128]{2,1,0:T(8,128)S(1)}, f32[2,128,128]{2,1,0:T(8,128)S(1)}, u32[]{:S(2)}, u32[]{:S(2)}) collective-permute-start(f32[2,128,128]{2,1,0:T(8,128)S(1)} %get-tuple-element.35), channel_id=1, source_target_pairs={{0,4},{2,14},{4,0},{6,10},{8,12},{10,6},{12,8},{14,2},{16,20},{18,... | collective-permute-start | bytes 393224 | tf_op jit(solution)/shard_map/ppermute | solution.py:342
  7.4 0.2 collective-permute-start.3
  7.5 0.0 collective-permute-done.came
  7.6 0.3 collective-permute-start.4
  7.8 2.0 %shard_map.70 = (f32[8,256,128]{2,1,0:T(8,128)S(1)}, f32[8,256,128]{2,1,0:T(8,128)S(1)}, f32[8,256,128]{2,1,0:T(8,128)S(1)}) custom-call(bf16[8,256,128]{2,1,0:T(8,128)(2,1)S(1)} %copy-done.3, bf16[8,256,128]{2,1,0:T(8,128)(2,1)S(1)} %copy-done, bf16[8,256,128]{2,1,0:T(8,128)(2,1)S(1)} %copy-done.1, bf16[8,256,128]{2,1,0:T(8,128)(2,1)S(1)} %copy-done.2, ...), custom_call_target="tpu_custom_call" | custom-call | flops 805306368 | bytes 5242880 | tf_op jit(solution)/shard_map/pallas_call | solution.py:257
  9.9 0.2 collective-permute-done.2.refs_1_
  10.1 2.9 %collective-permute-done.3.refs_2_ = f32[2,128,128]{2,1,0:T(8,128)S(1)} collective-permute-done((f32[2,128,128]{2,1,0:T(8,128)S(1)}, f32[2,128,128]{2,1,0:T(8,128)S(1)}, u32[]{:S(2)}, u32[]{:S(2)}) %collective-permute-start.3) | collective-permute-done | bytes 131104 | tf_op jit(solution)/shard_map/ppermute | solution.py:342
  13.0 0.0 collective-permute-done.4.refs_3_
  13.1 2.4 %collective-permute-start.5 = (f32[128,128]{1,0:T(8,128)S(1)}, f32[128,128]{1,0:T(8,128)S(1)}, u32[]{:S(2)}, u32[]{:S(2)}) collective-permute-start(f32[128,128]{1,0:T(8,128)S(1)} %fusion), channel_id=1, source_target_pairs={{0,16},{2,18},{4,20},{6,22},{8,24},{10,26},{12,28},{14,30},{16,0},... | collective-permute-start | bytes 196616 | tf_op jit(solution)/shard_map/ppermute | solution.py:336
  15.5 1.7 %collective-permute-done.5 = f32[128,128]{1,0:T(8,128)S(1)} collective-permute-done((f32[128,128]{1,0:T(8,128)S(1)}, f32[128,128]{1,0:T(8,128)S(1)}, u32[]{:S(2)}, u32[]{:S(2)}) %collective-permute-start.5) | collective-permute-done | bytes 65568 | tf_op jit(solution)/shard_map/ppermute | solution.py:336
  17.2 0.1 shard_map.77
  17.3 1.0 %collective-permute-start.8 = (f32[2,128,128]{2,1,0:T(8,128)S(1)}, f32[2,128,128]{2,1,0:T(8,128)S(1)}, u32[]{:S(2)}, u32[]{:S(2)}) collective-permute-start(f32[2,128,128]{2,1,0:T(8,128)S(1)} %shard_map.77), channel_id=1, source_target_pairs={{0,12},{2,6},{4,8},{6,2},{8,4},{10,14},{12,0},{14,10},{16,28},{18,... | collective-permute-start | bytes 393224 | tf_op jit(solution)/shard_map/ppermute | solution.py:342
  18.3 1.5 %collective-permute-start.6 = (f32[2,128,128]{2,1,0:T(8,128)S(1)}, f32[2,128,128]{2,1,0:T(8,128)S(1)}, u32[]{:S(2)}, u32[]{:S(2)}) collective-permute-start(f32[2,128,128]{2,1,0:T(8,128)S(1)} %shard_map.74), channel_id=1, source_target_pairs={{0,8},{2,10},{4,12},{6,14},{8,0},{10,2},{12,4},{14,6},{16,24},{18,... | collective-permute-start | bytes 393224 | tf_op jit(solution)/shard_map/ppermute | solution.py:342
  19.8 0.4 %collective-permute-start.7 = (f32[2,128,128]{2,1,0:T(8,128)S(1)}, f32[2,128,128]{2,1,0:T(8,128)S(1)}, u32[]{:S(2)}, u32[]{:S(2)}) collective-permute-start(f32[2,128,128]{2,1,0:T(8,128)S(1)} %shard_map.75), channel_id=1, source_target_pairs={{0,4},{2,14},{4,0},{6,10},{8,12},{10,6},{12,8},{14,2},{16,20},{18,... | collective-permute-start | bytes 393224 | tf_op jit(solution)/shard_map/ppermute | solution.py:342
  20.2 0.9 %collective-permute-done.8.refs_5_ = f32[2,128,128]{2,1,0:T(8,128)S(1)} collective-permute-done((f32[2,128,128]{2,1,0:T(8,128)S(1)}, f32[2,128,128]{2,1,0:T(8,128)S(1)}, u32[]{:S(2)}, u32[]{:S(2)}) %collective-permute-start.8) | collective-permute-done | bytes 131104 | tf_op jit(solution)/shard_map/ppermute | solution.py:342
  21.2 5.6 %collective-permute-start.10 = (f32[2,2,128,128]{3,2,1,0:T(8,128)S(1)}, f32[2,2,128,128]{3,2,1,0:T(8,128)S(1)}, u32[]{:S(2)}, u32[]{:S(2)}) collective-permute-start(f32[2,2,128,128]{3,2,1,0:T(8,128)S(1)} %get-tuple-element.43), channel_id=1, source_target_pairs={{0,2},{2,0},{4,6},{6,4},{8,10},{10,8},{12,14},{14,12},{16,18},{18,... | collective-permute-start | bytes 786440 | tf_op jit(solution)/shard_map/ppermute | solution.py:336
  26.8 1.0 %shard_map.79 = (bf16[8,256,128]{2,1,0:T(8,128)(2,1)}, bf16[8,256,128]{2,1,0:T(8,128)(2,1)}, bf16[8,256,128]{2,1,0:T(8,128)(2,1)}, f32[8,128]{1,0:T(8,128)S(1)}) custom-call(bf16[8,256,128]{2,1,0:T(8,128)(2,1)S(1)} %copy-done, bf16[8,256,128]{2,1,0:T(8,128)(2,1)S(1)} %copy-done.1, bf16[8,256,128]{2,1,0:T(8,128)(2,1)S(1)} %copy-done.2, ...), custom_call_target="tpu_custom_call" | custom-call | flops 50331648 | bytes 393216 | tf_op jit(solution)/shard_map/pallas_call | solution.py:316
  27.8 0.0 collective-permute-done.6.refs_2_
  27.8 0.0 collective-permute-done.7.refs_5_
  27.8 0.1 shard_map.80
  27.8 0.7 %collective-permute-start.9 = (f32[2,2,128,128]{3,2,1,0:T(8,128)S(1)}, f32[2,2,128,128]{3,2,1,0:T(8,128)S(1)}, u32[]{:S(2)}, u32[]{:S(2)}) collective-permute-start(f32[2,2,128,128]{3,2,1,0:T(8,128)S(1)} %get-tuple-element.42), channel_id=1, source_target_pairs={{0,2},{2,0},{4,6},{6,4},{8,10},{10,8},{12,14},{14,12},{16,18},{18,... | collective-permute-start | bytes 786440 | tf_op jit(solution)/shard_map/ppermute | solution.py:336
  28.5 0.0 collective-permute-done.10.refs_0_
  28.5 1.2 %shard_map.81 = (bf16[8,256,128]{2,1,0:T(8,128)(2,1)}, bf16[8,256,128]{2,1,0:T(8,128)(2,1)}, bf16[8,256,128]{2,1,0:T(8,128)(2,1)}) custom-call(bf16[8,256,128]{2,1,0:T(8,128)(2,1)S(1)} %copy-done, bf16[8,256,128]{2,1,0:T(8,128)(2,1)S(1)} %copy-done.1, ...), custom_call_target="tpu_custom_call", output_to_operand_aliasing={{0}: (8, {}), {1}: (9, {}), {2}: (10, {})} | custom-call | flops 100663296 | bytes 786432 | tf_op jit(solution)/shard_map/pallas_call | solution.py:316
  29.7 0.0 collective-permute-done.9.refs_0_
  29.7 1.0 %shard_map.82 = (bf16[8,256,128]{2,1,0:T(8,128)(2,1)}, bf16[8,256,128]{2,1,0:T(8,128)(2,1)}, bf16[8,256,128]{2,1,0:T(8,128)(2,1)}) custom-call(bf16[8,256,128]{2,1,0:T(8,128)(2,1)S(1)} %copy-done, bf16[8,256,128]{2,1,0:T(8,128)(2,1)S(1)} %copy-done.1, bf16[8,256,128]{2,1,0:T(8,128)(2,1)S(1)} %copy-done.2, ...), custom_call_target="tpu_custom_call", output_to_operand_aliasing={{0}: (7, {}), {1}: (8, {}), {2}: (9, {})} | custom-call | flops 50331648 | bytes 393216 | tf_op jit(solution)/shard_map/pallas_call | solution.py:316
  (10 shorter events, 0.3 us)
Async XLA Ops:
  0.6 1.8 %copy-start = (bf16[8,256,128]{2,1,0:T(8,128)(2,1)S(1)}, bf16[8,256,128]{2,1,0:T(8,128)(2,1)}, u32[]{:S(2)}) copy-start(bf16[8,256,128]{2,1,0:T(8,128)(2,1)} %k.11) | copy-start | bytes 1572868
  0.6 1.8 %copy-start.1 = (bf16[8,256,128]{2,1,0:T(8,128)(2,1)S(1)}, bf16[8,256,128]{2,1,0:T(8,128)(2,1)}, u32[]{:S(2)}) copy-start(bf16[8,256,128]{2,1,0:T(8,128)(2,1)} %v.11) | copy-start | bytes 1572868
  0.7 1.8 %copy-start.2 = (bf16[8,256,128]{2,1,0:T(8,128)(2,1)S(1)}, bf16[8,256,128]{2,1,0:T(8,128)(2,1)}, u32[]{:S(2)}) copy-start(bf16[8,256,128]{2,1,0:T(8,128)(2,1)} %g.11) | copy-start | bytes 1572868
  0.7 1.8 %copy-start.3 = (bf16[8,256,128]{2,1,0:T(8,128)(2,1)S(1)}, bf16[8,256,128]{2,1,0:T(8,128)(2,1)}, u32[]{:S(2)}) copy-start(bf16[8,256,128]{2,1,0:T(8,128)(2,1)} %q.5) | copy-start | bytes 1572868
  2.3 1.6 %collective-permute-start.1 = (f32[2,2,128,128]{3,2,1,0:T(8,128)S(1)}, f32[2,2,128,128]{3,2,1,0:T(8,128)S(1)}, u32[]{:S(2)}, u32[]{:S(2)}) collective-permute-start(f32[2,2,128,128]{3,2,1,0:T(8,128)S(1)} %shard_map.71), channel_id=1, source_target_pairs={{0,2},{2,0},{4,6},{6,4},{8,10},{10,8},{12,14},{14,12},{16,18},{18,... | collective-permute-start | bytes 786440 | tf_op jit(solution)/shard_map/ppermute | solution.py:336
  2.7 4.8 %collective-permute-start = (f32[2,2,128,128]{3,2,1,0:T(8,128)S(1)}, f32[2,2,128,128]{3,2,1,0:T(8,128)S(1)}, u32[]{:S(2)}, u32[]{:S(2)}) collective-permute-start(f32[2,2,128,128]{3,2,1,0:T(8,128)S(1)} %shard_map.67), channel_id=1, source_target_pairs={{0,2},{2,0},{4,6},{6,4},{8,10},{10,8},{12,14},{14,12},{16,18},{18,... | collective-permute-start | bytes 786440 | tf_op jit(solution)/shard_map/ppermute | solution.py:336
  3.9 6.2 %collective-permute-start.2 = (f32[2,128,128]{2,1,0:T(8,128)S(1)}, f32[2,128,128]{2,1,0:T(8,128)S(1)}, u32[]{:S(2)}, u32[]{:S(2)}) collective-permute-start(f32[2,128,128]{2,1,0:T(8,128)S(1)} %get-tuple-element.35), channel_id=1, source_target_pairs={{0,4},{2,14},{4,0},{6,10},{8,12},{10,6},{12,8},{14,2},{16,20},{18,... | collective-permute-start | bytes 393224 | tf_op jit(solution)/shard_map/ppermute | solution.py:342
  7.4 5.7 %collective-permute-start.3 = (f32[2,128,128]{2,1,0:T(8,128)S(1)}, f32[2,128,128]{2,1,0:T(8,128)S(1)}, u32[]{:S(2)}, u32[]{:S(2)}) collective-permute-start(f32[2,128,128]{2,1,0:T(8,128)S(1)} %get-tuple-element.36), channel_id=1, source_target_pairs={{0,8},{2,10},{4,12},{6,14},{8,0},{10,2},{12,4},{14,6},{16,24},{18,... | collective-permute-start | bytes 393224 | tf_op jit(solution)/shard_map/ppermute | solution.py:342
  7.6 5.4 %collective-permute-start.4 = (f32[2,128,128]{2,1,0:T(8,128)S(1)}, f32[2,128,128]{2,1,0:T(8,128)S(1)}, u32[]{:S(2)}, u32[]{:S(2)}) collective-permute-start(f32[2,128,128]{2,1,0:T(8,128)S(1)} %get-tuple-element.37), channel_id=1, source_target_pairs={{0,12},{2,6},{4,8},{6,2},{8,4},{10,14},{12,0},{14,10},{16,28},{18,... | collective-permute-start | bytes 393224 | tf_op jit(solution)/shard_map/ppermute | solution.py:342
  13.1 4.1 %collective-permute-start.5 = (f32[128,128]{1,0:T(8,128)S(1)}, f32[128,128]{1,0:T(8,128)S(1)}, u32[]{:S(2)}, u32[]{:S(2)}) collective-permute-start(f32[128,128]{1,0:T(8,128)S(1)} %fusion), channel_id=1, source_target_pairs={{0,16},{2,18},{4,20},{6,22},{8,24},{10,26},{12,28},{14,30},{16,0},... | collective-permute-start | bytes 196616 | tf_op jit(solution)/shard_map/ppermute | solution.py:336
  17.3 3.9 %collective-permute-start.8 = (f32[2,128,128]{2,1,0:T(8,128)S(1)}, f32[2,128,128]{2,1,0:T(8,128)S(1)}, u32[]{:S(2)}, u32[]{:S(2)}) collective-permute-start(f32[2,128,128]{2,1,0:T(8,128)S(1)} %shard_map.77), channel_id=1, source_target_pairs={{0,12},{2,6},{4,8},{6,2},{8,4},{10,14},{12,0},{14,10},{16,28},{18,... | collective-permute-start | bytes 393224 | tf_op jit(solution)/shard_map/ppermute | solution.py:342
  18.3 9.5 %collective-permute-start.6 = (f32[2,128,128]{2,1,0:T(8,128)S(1)}, f32[2,128,128]{2,1,0:T(8,128)S(1)}, u32[]{:S(2)}, u32[]{:S(2)}) collective-permute-start(f32[2,128,128]{2,1,0:T(8,128)S(1)} %shard_map.74), channel_id=1, source_target_pairs={{0,8},{2,10},{4,12},{6,14},{8,0},{10,2},{12,4},{14,6},{16,24},{18,... | collective-permute-start | bytes 393224 | tf_op jit(solution)/shard_map/ppermute | solution.py:342
  19.8 8.0 %collective-permute-start.7 = (f32[2,128,128]{2,1,0:T(8,128)S(1)}, f32[2,128,128]{2,1,0:T(8,128)S(1)}, u32[]{:S(2)}, u32[]{:S(2)}) collective-permute-start(f32[2,128,128]{2,1,0:T(8,128)S(1)} %shard_map.75), channel_id=1, source_target_pairs={{0,4},{2,14},{4,0},{6,10},{8,12},{10,6},{12,8},{14,2},{16,20},{18,... | collective-permute-start | bytes 393224 | tf_op jit(solution)/shard_map/ppermute | solution.py:342
  21.2 7.3 %collective-permute-start.10 = (f32[2,2,128,128]{3,2,1,0:T(8,128)S(1)}, f32[2,2,128,128]{3,2,1,0:T(8,128)S(1)}, u32[]{:S(2)}, u32[]{:S(2)}) collective-permute-start(f32[2,2,128,128]{3,2,1,0:T(8,128)S(1)} %get-tuple-element.43), channel_id=1, source_target_pairs={{0,2},{2,0},{4,6},{6,4},{8,10},{10,8},{12,14},{14,12},{16,18},{18,... | collective-permute-start | bytes 786440 | tf_op jit(solution)/shard_map/ppermute | solution.py:336
  27.8 1.8 %collective-permute-start.9 = (f32[2,2,128,128]{3,2,1,0:T(8,128)S(1)}, f32[2,2,128,128]{3,2,1,0:T(8,128)S(1)}, u32[]{:S(2)}, u32[]{:S(2)}) collective-permute-start(f32[2,2,128,128]{3,2,1,0:T(8,128)S(1)} %get-tuple-element.42), channel_id=1, source_target_pairs={{0,2},{2,0},{4,6},{6,4},{8,10},{10,8},{12,14},{14,12},{16,18},{18,... | collective-permute-start | bytes 786440 | tf_op jit(solution)/shard_map/ppermute | solution.py:336
